TPU v7x, 512 devices: a whole 4x8x8 slice. The times are simulated.
512 devices in a mesh: cfg: 2 (over y_hi), seq: 32 (over z, y_lo), blk: 8 (over x, core).
Axes of the slice: x: 4, y: 8 (y_hi: 2, y_lo: 4; y = y_hi * 4 + y_lo), z: 8, core: 2. Of those that a mesh axis runs over, the one named last changes fastest.
Arguments:
- tokens_in: bfloat16 [2, 4096, 1536], P('cfg', 'seq'), may hold values from -6 to 6
- modulation: float32 [2, 8, 1536], replicated, may hold values from -3 to 3
- qk_gain: float32 [2, 64], replicated, as said below
- qkv_weight: bfloat16 [3, 1536, 1536], P(None, 'blk'), may hold values from -0.15625 to 0.15625
- out_weight: bfloat16 [1536, 1536], P('blk'), may hold values from -0.15625 to 0.15625
- up_weight: bfloat16 [1536, 6144], P('seq', 'blk'), may hold values from -0.15625 to 0.15625
- down_weight: bfloat16 [6144, 1536], P('blk', 'seq'), may hold values from -0.078125 to 0.078125
- proj_weight: bfloat16 [1536, 64], replicated, may hold values from -0.15625 to 0.15625
- latent: float32 [4096, 64], P(('seq', 'blk'), 'cfg'), may hold values from -6 to 6
- text_count: int32 [1], replicated, may hold values from 64 to 2047
- positions: int32 [3, 4096], P(None, 'seq'), may hold values from 0 to 47
- step_index: int32 [1], replicated, may hold values from 20 to 999
- guidance: float32 [1], replicated, may hold values from 4 to 8
Outputs:
- hidden_out: bfloat16 [2, 4096, 1536], P('cfg', ('seq', 'blk'))
- latent_prev: float32 [4096, 64], P(('seq', 'blk'), 'cfg')
Inputs may be any that keep to these rules, and one draw needn't show every extreme that they name: `qk_gain`: positive gains.
All inputs are finite; a program needn't handle non-finite values.
Results may differ from a plain program's by a relative error of at most 0.015.
The roundings to bfloat16 on the way count: a program that leaves them out, or rounds other values in their place, can miss the bound.
Values may be sent and summed in bfloat16 or wider, within the bound.
No kernel may reach another device: no remote copies, remote signals or barrier semaphores. Data moves between devices by JAX's collectives and lax.ppermute only.
A program may use at most 64 MiB of HBM per device.

v0:
```python
import math

import jax
import jax.numpy as jnp
from jax import lax
from jax.sharding import PartitionSpec as P

HEAD = 64
STRIDE = 20


rope_bands = (16, 24, 24)


def swapped(block, axis, stride):
    count = lax.axis_size(axis)
    route = []
    for low in range(count):
        high = low | 1 << stride
        if high != low and high < count:
            route += [(low, high), (high, low)]
    return lax.ppermute(block, axis, route)


def layer_norm(values, epsilon):
    average = jnp.mean(values, -1, keepdims=True)
    centered = values - average
    spread = jnp.mean(centered * centered, -1, keepdims=True)
    return centered * lax.rsqrt(spread + epsilon)


def pick_mods(modulation, is_video, which):
    return jnp.where(
        is_video[:, None], modulation[1, which][None, :], modulation[0, which][None, :]
    )


def modulate(values, modulation, is_video, shift_row, scale_row):
    normed = layer_norm(values, 1e-05)
    return normed * (1.0 + pick_mods(modulation, is_video, scale_row)) + pick_mods(
        modulation, is_video, shift_row
    )


def rope_tables(positions, is_video):
    angle_parts = []
    for axis_pos, band_width in enumerate(rope_bands):
        exponent = jnp.arange(band_width // 2, dtype=jnp.float32) * (2.0 / band_width)
        inverse = jnp.exp(-exponent * math.log(10000.0))
        angle_parts.append(positions[axis_pos].astype(jnp.float32)[:, None] * inverse[None, :])
    angles = jnp.concatenate(angle_parts, 1) * is_video.astype(jnp.float32)[:, None]
    return (jnp.cos(angles), jnp.sin(angles))


def rotate(vectors, cosine, sine):
    pieces = []
    offset = 0
    half_offset = 0
    for band_width in rope_bands:
        half_width = band_width // 2
        first_half = vectors[..., offset : offset + half_width]
        second = vectors[..., offset + half_width : offset + band_width]
        cos_band = cosine[:, None, half_offset : half_offset + half_width]
        sin_band = sine[:, None, half_offset : half_offset + half_width]
        pieces.append(first_half * cos_band - second * sin_band)
        pieces.append(second * cos_band + first_half * sin_band)
        offset = offset + band_width
        half_offset = half_offset + half_width
    return jnp.concatenate(pieces, -1)


def head_prep(flat_heads, gain, cosine, sine):
    token_count = flat_heads.shape[0]
    shaped = flat_heads.reshape(token_count, -1, HEAD)
    normed = layer_norm(shaped, 1e-06) * gain[None, None, :]
    turned = rotate(normed, cosine, sine)
    return turned.reshape(token_count, -1).astype(jnp.bfloat16)


def ddim_update(latent, guided, step_index):
    steps_all = jnp.arange(1000, dtype=jnp.float32)
    root_beta = math.sqrt(0.00085) + steps_all / 999.0 * (math.sqrt(0.012) - math.sqrt(0.00085))
    alpha_bar = jnp.exp(jnp.cumsum(jnp.log1p(-root_beta * root_beta)))
    indices = jnp.arange(1000, dtype=jnp.int32)
    alpha_now = jnp.sum(jnp.where(indices == step_index[0], alpha_bar, 0.0))
    alpha_prev = jnp.sum(jnp.where(indices == step_index[0] - STRIDE, alpha_bar, 0.0))
    clean_est = jnp.sqrt(alpha_now) * latent - jnp.sqrt(1.0 - alpha_now) * guided
    noise_est = jnp.sqrt(1.0 - alpha_now) * latent + jnp.sqrt(alpha_now) * guided
    return jnp.sqrt(alpha_prev) * clean_est + jnp.sqrt(1.0 - alpha_prev) * noise_est


def body(
    tokens_in,
    modulation,
    qk_gain,
    qkv_weight,
    out_weight,
    up_weight,
    down_weight,
    proj_weight,
    latent,
    text_count,
    positions,
    step_index,
    guidance,
):
    row_count = tokens_in.shape[1]
    own_count = row_count // lax.axis_size("blk")
    blk_index = lax.axis_index("blk")
    token_ids = lax.axis_index("seq") * row_count + jnp.arange(row_count, dtype=jnp.int32)
    is_video = token_ids >= text_count[0]
    own_video = lax.dynamic_slice_in_dim(is_video, blk_index * own_count, own_count, 0)
    residual = tokens_in[0].astype(jnp.float32)
    cosine, sine = rope_tables(positions, is_video)
    normed = modulate(residual, modulation, is_video, 0, 1).astype(jnp.bfloat16)
    projected = jnp.einsum("td,ked->kte", normed, qkv_weight, preferred_element_type=jnp.float32)
    head_count = projected.shape[2] // HEAD
    queries = head_prep(projected[0], qk_gain[0], cosine, sine)
    keys_local = head_prep(projected[1], qk_gain[1], cosine, sine)
    values_local = projected[2].astype(jnp.bfloat16)
    query_heads = queries.reshape(row_count, head_count, HEAD)
    initial = (
        jnp.full((head_count, row_count), -1e30, jnp.float32),
        jnp.zeros((head_count, row_count), jnp.float32),
        jnp.zeros((head_count, row_count, HEAD), jnp.float32),
    )
    key_piece = lax.all_gather(keys_local, "seq", axis=0, tiled=True)
    value_piece = lax.all_gather(values_local, "seq", axis=0, tiled=True)
    piece_len = key_piece.shape[0]
    key_blocks = key_piece.reshape(piece_len // piece_len, piece_len, head_count, HEAD)
    value_blocks = value_piece.reshape(piece_len // piece_len, piece_len, head_count, HEAD)

    def absorb_block(state, key_value):
        key_block, value_block = key_value
        running_max, running_sum, weighted = state
        scores = (
            jnp.einsum("thd,shd->hts", query_heads, key_block, preferred_element_type=jnp.float32)
            * 0.125
        )
        new_max = jnp.maximum(running_max, jnp.max(scores, -1))
        rescale = jnp.exp(running_max - new_max)
        weights = jnp.exp(scores - new_max[..., None])
        running_sum = running_sum * rescale + jnp.sum(weights, -1)
        weighted = weighted * rescale[..., None] + jnp.einsum(
            "hts,shd->htd",
            weights.astype(jnp.bfloat16),
            value_block,
            preferred_element_type=jnp.float32,
        )
        return ((new_max, running_sum, weighted), None)

    state, unused = lax.scan(absorb_block, initial, (key_blocks, value_blocks))
    running_max, running_sum, weighted = state
    attn_out = (
        (weighted / running_sum[..., None])
        .transpose(1, 0, 2)
        .reshape(row_count, head_count * HEAD)
        .astype(jnp.bfloat16)
    )
    attn_proj = lax.psum(
        jnp.dot(attn_out, out_weight, preferred_element_type=jnp.float32).astype(jnp.bfloat16),
        "blk",
    ).astype(jnp.float32)
    after_attn = residual + pick_mods(modulation, is_video, 2) * attn_proj
    normed_mlp = modulate(after_attn, modulation, is_video, 3, 4).astype(jnp.bfloat16)
    own_after = lax.dynamic_slice_in_dim(after_attn, blk_index * own_count, own_count, 0)
    up_full, down_full = (
        lax.all_gather(up_weight, "seq", axis=0, tiled=True),
        lax.all_gather(down_weight, "seq", axis=1, tiled=True),
    )
    hidden_up = jnp.dot(normed_mlp, up_full, preferred_element_type=jnp.float32)
    activated = jax.nn.gelu(hidden_up, approximate=True).astype(jnp.bfloat16)
    mlp_part = jnp.dot(activated, down_full, preferred_element_type=jnp.float32)
    mlp_rows = lax.psum_scatter(
        mlp_part.astype(jnp.bfloat16), "blk", scatter_dimension=0, tiled=True
    ).astype(jnp.float32)
    after_mlp = own_after + pick_mods(modulation, own_video, 5) * mlp_rows
    hidden_out = after_mlp.astype(jnp.bfloat16)[None]
    final_norm = modulate(after_mlp, modulation, own_video, 6, 7).astype(jnp.bfloat16)
    predicted = jnp.dot(final_norm, proj_weight, preferred_element_type=jnp.float32)
    half_width = latent.shape[1]
    branch_index = lax.axis_index("cfg")
    kept = lax.dynamic_slice_in_dim(predicted, branch_index * half_width, half_width, 1)
    outgoing = lax.dynamic_slice_in_dim(predicted, (1 - branch_index) * half_width, half_width, 1)
    partner = swapped(outgoing, "cfg", 0)
    is_cond = branch_index == 0
    cond_pred = jnp.where(is_cond, kept, partner)
    uncond_pred = jnp.where(is_cond, partner, kept)
    guided = uncond_pred + guidance[0] * (cond_pred - uncond_pred)
    latent_prev = ddim_update(latent, guided, step_index)
    return (hidden_out, latent_prev)


def solution(mesh):
    in_specs = (
        P("cfg", "seq", None),
        P(),
        P(),
        P(None, "blk", None),
        P("blk", None),
        P("seq", "blk"),
        P("blk", "seq"),
        P(),
        P(("seq", "blk"), "cfg"),
        P(),
        P(None, "seq"),
        P(),
        P(),
    )
    out_specs = (P("cfg", ("seq", "blk"), None), P(("seq", "blk"), "cfg"))
    return jax.shard_map(body, mesh=mesh, in_specs=in_specs, out_specs=out_specs, check_vma=False)
```

profile of v0, /device:TPU:56, one launch (start us, length us, event | category | flops | bytes accessed | tf_op | source)
XLA Modules:
  0.0 742.5 jit_solution(7766577091344267166)
XLA Ops:
  8.0 0.8 convert_bitcast_fusion.4
  9.1 1.8 slice_reduce_fusion.3
  10.9 1.1 convert_reduce_fusion
  12.0 1.3 fusion.21
  13.3 1.7 convolution_bitcast_fusion
  15.4 5.1 concatenate.13
  20.6 0.6 slice.262
  21.4 0.3 concatenate.12
  21.7 134.5 %all-gather.6.cloned.1.call-done = bf16[4096,192]{0,1:T(8,128)(2,1)} async-done(((bf16[128,192]{0,1:T(8,128)(2,1)}), bf16[4096,192]{0,1:T(8,128)(2,1)}) %all-gather.6.cloned.1.call-update) | async-done | bytes 1572880 | tf_op jit(solution)/shard_map/all_gather | solution.py:127
  156.2 2.5 fusion.90
  158.7 1.0 fusion
  159.7 1.7 copy-done.1
  161.3 125.2 %all-gather.12.cloned.1.call-done = bf16[1,4096,192]{1,2,0:T(8,128)(2,1)} async-done(((bf16[1,128,192]{1,2,0:T(8,128)(2,1)}), bf16[1,4096,192]{1,2,0:T(8,128)(2,1)}) %all-gather.12.cloned.1.call-update) | async-done | bytes 1572880 | tf_op jit(solution)/shard_map/all_gather | solution.py:128
  286.5 4.6 fusion.14
  291.1 1.1 convolution_convert_fusion.1
  292.3 0.5 all-gather.10.cloned.1.call-update
  292.8 0.5 all-gather.8.cloned.1.call-update
  293.4 65.8 %all-reduce.3.cloned.1.call-done = bf16[128,1536]{1,0:T(8,128)(2,1)} async-done(((bf16[128,1536]{1,0:T(8,128)(2,1)}), bf16[128,1536]{1,0:T(8,128)(2,1)}) %all-reduce.3.cloned.1.call-update) | async-done | bytes 393232 | tf_op jit(solution)/shard_map/psum | solution.py:160
  359.2 1.3 fusion.84
  360.5 0.2 multiply_reduce_fusion
  360.8 154.6 %all-gather.10.cloned.1.call-done = bf16[768,1536]{0,1:T(8,128)(2,1)} async-done(((bf16[768,48]{0,1:T(8,128)(2,1)}), bf16[768,1536]{0,1:T(8,128)(2,1)}) %all-gather.10.cloned.1.call-update) | async-done | bytes 2359312 | tf_op jit(solution)/shard_map/all_gather | solution.py:169
  515.4 162.1 %all-gather.8.cloned.1.call-done = bf16[1536,768]{1,0:T(8,128)(2,1)} async-done(((bf16[48,768]{1,0:T(8,128)(2,1)}), bf16[1536,768]{1,0:T(8,128)(2,1)}) %all-gather.8.cloned.1.call-update) | async-done | bytes 2359312 | tf_op jit(solution)/shard_map/all_gather | solution.py:168
  677.5 4.5 convolution_convert_fusion
  682.2 0.3 reduce-window.9
  683.4 40.0 %reduce-scatter.2.cloned.1.call-done = bf16[16,1536]{1,0:T(8,128)(2,1)} async-done(((bf16[128,1536]{1,0:T(8,128)(2,1)}), bf16[16,1536]{1,0:T(8,128)(2,1)}) %reduce-scatter.2.cloned.1.call-update) | async-done | bytes 49168 | tf_op jit(solution)/shard_map/reduce_scatter | solution.py:174
  723.4 1.0 fusion.83
  724.4 0.7 multiply_reduce_fusion.1
  725.2 0.2 fusion.64
  725.5 5.2 collective-permute-start
  730.7 0.7 select_reduce_fusion
  734.7 0.3 collective-permute-done
  735.0 0.7 multiply_add_fusion.1
  (62 shorter events, 1.5 us)
Async XLA Ops:
  7.2 6.2 copy-start
  7.2 149.0 %all-gather.6.cloned.1.call-start = ((), (), s32[]{:S(2)}) async-start(), calls=%async_computation.1 | async-start | bytes 1622016 | tf_op jit(solution)/shard_map/all_gather | solution.py:127
  12.0 3.2 copy-start.5
  20.5 266.0 %all-gather.12.cloned.1.call-start = ((), (), s32[]{:S(2)}) async-start(), calls=%async_computation.6 | async-start | bytes 1622016 | tf_op jit(solution)/shard_map/all_gather | solution.py:128
  21.3 337.9 %all-reduce.3.cloned.1.call-start = ((), (), s32[]{:S(2)}) async-start(), calls=%async_computation.2 | async-start | bytes 786432 | tf_op jit(solution)/shard_map/psum | solution.py:160
  158.7 2.7 copy-start.1
  286.5 4.6 copy-start.3
  286.5 72.7 %copy-start.2 = (bf16[1,128,1536]{2,1,0:T(8,128)(2,1)S(1)}, bf16[1,128,1536]{2,1,0:T(8,128)(2,1)}, u32[]{:S(2)}) copy-start(bf16[1,128,1536]{2,1,0:T(8,128)(2,1)} %param.13) | copy-start | bytes 1179652
  292.2 223.2 %all-gather.10.cloned.1.call-start = ((), (), s32[]{:S(2)}) async-start(), calls=%async_computation.4 | async-start | bytes 2433024 | tf_op jit(solution)/shard_map/all_gather | solution.py:169
  292.8 384.7 %all-gather.8.cloned.1.call-start = ((), (), s32[]{:S(2)}) async-start(), calls=%async_computation.3 | async-start | bytes 2433024 | tf_op jit(solution)/shard_map/all_gather | solution.py:168
  293.4 430.0 %reduce-scatter.2.cloned.1.call-start = ((), (), s32[]{:S(2)}) async-start(), calls=%async_computation.5 | async-start | bytes 442368 | tf_op jit(solution)/shard_map/reduce_scatter | solution.py:174
  677.5 47.7 %copy-start.6 = (bf16[1536,64]{0,1:T(8,128)(2,1)S(1)}, bf16[1536,64]{0,1:T(8,128)(2,1)}, u32[]{:S(2)}) copy-start(bf16[1536,64]{0,1:T(8,128)(2,1)} %param.20) | copy-start | bytes 589828
  677.5 57.5 %copy-start.4 = (f32[16,32]{1,0:T(8,128)S(1)}, f32[16,32]{1,0:T(8,128)}, u32[]{:S(2)}) copy-start(f32[16,32]{1,0:T(8,128)} %param.21) | copy-start | bytes 6148
  725.5 9.5 %collective-permute-start = (f32[16,32]{1,0:T(8,128)S(1)}, f32[16,32]{1,0:T(8,128)S(1)}, u32[]{:S(2)}, u32[]{:S(2)}) collective-permute-start(f32[16,32]{1,0:T(8,128)S(1)} %constant_dynamic-slice_fusion), channel_id=1, source_target_pairs={{0,256},{256,0},{1,257},{257,1},{2,258},{258,2},{3,259},{259,3},{4... | collective-permute-start | bytes 6152 | tf_op jit(solution)/shard_map/ppermute | solution.py:22
Sparse Core Ops, SparseCore 0:
  20.7 135.4 all-gather.5
  158.7 127.7 all-gather.11
  292.3 66.8 all-reduce.2
  361.4 153.9 all-gather.9
  517.5 159.9 all-gather.7
  682.2 41.1 reduce-scatter.1
where the time goes:
time: 745 us; the launch traced here: 743 us
  waiting for transfers between devices  684 us (92%)
  between operations  19.1 us (3%)
  matrix products  14.7 us (2%)
  local copies, waits for them, and re-layouts  9.89 us (1%)
  other arithmetic  9.82 us (1%)
    all_gather x1, waiting for transfers between devices, body(): lax.all_gather(up_weight, 'seq', axis=0, tiled=True)  162 us
    all_gather x1, waiting for transfers between devices, body(): lax.all_gather(down_weight, 'seq', axis=1, tiled=True)  155 us
    all_gather x1, waiting for transfers between devices, body(): key_piece = lax.all_gather(keys_local, 'seq', axis=0, tiled=True)  134 us
    all_gather x1, waiting for transfers between devices, body(): value_piece = lax.all_gather(values_local, 'seq', axis=0, tiled=True)  125 us
    psum x1, waiting for transfers between devices, body(): lax.psum(jnp.dot(attn_out, out_weight, preferred_element_type=jnp.float32...  65.8 us
    reduce_scatter x1, waiting for transfers between devices, body(): lax.psum_scatter(mlp_part.astype(jnp.bfloat16), 'blk', scatter_dimension=...  40 us
  transfers between devices with their start and end apart: 7, of which 7 were waited for; matrix products, arithmetic and copies ran while one was open for 1% of the time, Pallas kernels for 0%

commit v1 on v0

v1 whole, which is shorter than its diff:
```python
import math

import jax
import jax.numpy as jnp
import numpy as np
from jax import lax
from jax.experimental import pallas as pl
from jax.experimental.pallas import tpu as pltpu
from jax.sharding import PartitionSpec as P

BF16 = jnp.bfloat16
F32 = jnp.float32
STRIDE = 20
TOK = 128
OWN = 16
D = 1536
UNITS = 768
SEQ = 32
BLK = 8
PIECE = 48

ALONG_Z = [[4 * z + y for z in range(8)] for y in range(4)]
ALONG_Y = [[4 * z + y for y in range(4)] for z in range(8)]

VMEM = pl.BlockSpec(memory_space=pltpu.VMEM)
SMEM = pl.BlockSpec(memory_space=pltpu.SMEM)
ANY = pl.BlockSpec(memory_space=pl.ANY)

ROWS_BY_ROWS = (((1,), (1,)), ((), ()))


def frequencies():
    table = np.zeros((8, 128), np.float32)
    offset = 0
    for band, width in enumerate((16, 24, 24)):
        half = width // 2
        inverse = np.exp(-np.arange(half, dtype=np.float32) * np.float32(2.0 / width) * np.float32(math.log(10000.0)))
        for head in (0, 64):
            start = head + offset
            table[0, start : start + half] = inverse
            table[0, start + half : start + width] = inverse
            table[1, start : start + width] = band
            table[2, start : start + half] = 1.0
        offset += width
    return table


def layer_norm(values, epsilon):
    centered = values - jnp.mean(values, -1, keepdims=True)
    spread = jnp.mean(centered * centered, -1, keepdims=True)
    return centered * lax.rsqrt(spread + epsilon)


def picker(mods, video):
    return lambda row: jnp.where(video, mods[1, row : row + 1, :], mods[0, row : row + 1, :])


def project_kernel(where, text, tokens, mods, gain, qkv, positions, table, out):
    ids = where[1] * TOK + lax.broadcasted_iota(jnp.int32, (TOK, 1), 0)
    video = ids >= text[0]
    pick = picker(mods, video)
    residual = tokens[0].astype(F32)
    normed = (layer_norm(residual, 1e-05) * (1.0 + pick(1)) + pick(0)).astype(BF16)

    def project(weight):
        return lax.dot_general(normed, weight, ROWS_BY_ROWS, preferred_element_type=F32)

    heads = project(qkv[0:2].reshape(384, D))
    values_low = project(qkv[2, 0:128, :])
    values_high = project(qkv[2, 64:192, :])

    lane = lax.broadcasted_iota(jnp.int32, (TOK, 128), 1)
    low = lane < 64
    band = table[1:2, :]
    where_at = positions[...].astype(F32)
    spread = [jnp.broadcast_to(where_at[a : a + 1, :], (128, 128)).T for a in range(3)]
    chosen = jnp.where(band == 0.0, spread[0], jnp.where(band == 1.0, spread[1], spread[2]))
    angles = chosen * table[0:1, :] * video.astype(F32)
    cosine = jnp.cos(angles)
    sine = jnp.sin(angles)
    first = table[2:3, :] > 0.5
    sine = jnp.where(first, -sine, sine)
    narrow = band == 0.0

    row_head = lax.broadcasted_iota(jnp.int32, (128, 128), 0) >> 6
    average = jnp.where(row_head == (lane >> 6), 1.0 / 64.0, 0.0)

    def head_mean(block):
        return jnp.dot(block, average, precision=lax.Precision.HIGHEST, preferred_element_type=F32)

    def prepare(block, gains):
        centered = block - head_mean(block)
        normal = centered * lax.rsqrt(head_mean(centered * centered) + 1e-06) * gains
        ahead = jnp.where(narrow, pltpu.roll(normal, 120, 1), pltpu.roll(normal, 116, 1))
        behind = jnp.where(narrow, pltpu.roll(normal, 8, 1), pltpu.roll(normal, 12, 1))
        return normal * cosine + jnp.where(first, ahead, behind) * sine

    query_gain = jnp.concatenate([gain[0:1, :], gain[0:1, :]], 1)
    key_gain = jnp.concatenate([gain[1:2, :], gain[1:2, :]], 1)
    mixed_gain = jnp.concatenate([gain[0:1, :], gain[1:2, :]], 1)
    queries_low = prepare(heads[:, 0:128], query_gain)
    query_and_key = prepare(heads[:, 128:256], mixed_gain)
    keys_high = prepare(heads[:, 256:384], key_gain)

    def turned(block):
        return pltpu.roll(block, 64, 1)

    pairs = [
        jnp.where(low, turned(query_and_key), turned(values_low)),
        jnp.where(low, keys_high, values_low),
        jnp.where(low, turned(keys_high), values_high),
    ]
    queries = [
        (queries_low, turned(queries_low)),
        (turned(queries_low), queries_low),
        (query_and_key, turned(query_and_key)),
    ]
    low16 = low[0:16, :]
    for head in range(3):
        pair = pairs[head].astype(BF16)
        left, right = queries[head]
        for part in range(4):
            start = 32 * part
            packed = jnp.where(low16, left[start : start + 16, :], right[start + 16 : start + 32, :])
            packed = (packed * 0.125).astype(BF16)
            for half in range(2):
                goes = 8 * head + 4 * half + part
                out[goes, 0:64, :] = pair[64 * half : 64 * half + 64, :]
                out[goes, 64:80, :] = packed
    out[24:32] = jnp.zeros((8, 80, 128), BF16)


def attend_kernel(got, out):
    pairs = got[:, 0:64, :].reshape(2048, 128)
    queries = got[:, 64:80, :].reshape(512, 128).astype(F32)
    lane = lax.broadcasted_iota(jnp.int32, (256, 128), 1)
    low = lane < 64
    for side in range(2):
        turned = queries if side == 0 else pltpu.roll(queries, 64, 1)
        for chunk in range(2):
            block = jnp.where(low, turned[256 * chunk : 256 * chunk + 256, :], 0.0).astype(BF16)
            scores = lax.dot_general(block, pairs, ROWS_BY_ROWS, preferred_element_type=F32)
            highest = jnp.max(scores, -1, keepdims=True)
            weights = jnp.exp(scores - highest)
            total = jnp.sum(weights, -1, keepdims=True)
            mixed = jnp.dot(weights.astype(BF16), pairs, preferred_element_type=F32) / total
            level = highest + jnp.log(total)
            coarse = level.astype(BF16).astype(F32)
            medium = (level - coarse).astype(BF16).astype(F32)
            fine = level - coarse - medium
            parts = jnp.where(lane == 0, coarse, jnp.where(lane == 1, medium, fine))
            result = jnp.where(low, parts, mixed).astype(BF16)
            out[16 * chunk : 16 * chunk + 16, 16 * side : 16 * side + 16, :] = result.reshape(16, 16, 128)


def out_project_kernel(got, weight, out):
    total = None
    for head in range(3):
        sides = []
        for half in range(2):
            first = 8 * head + 4 * half
            block = got[first : first + 4].reshape(TOK, 128).astype(F32)
            level = block[:, 0:1] + block[:, 1:2] + block[:, 2:3]
            sides.append((block, level))
        (one, level_one), (two, level_two) = sides
        highest = jnp.maximum(level_one, level_two)
        share_one = jnp.exp(level_one - highest)
        share_two = jnp.exp(level_two - highest)
        mixed = (one * share_one + two * share_two) / (share_one + share_two)
        attended = mixed[:, 64:128].astype(BF16)
        term = jnp.dot(attended, weight[64 * head : 64 * head + 64, :], preferred_element_type=F32)
        total = term if total is None else total + term
    out[...] = total.astype(BF16).reshape(BLK, OWN, D)


def own_video(where, text):
    ids = where[1] * TOK + where[2] * OWN + lax.broadcasted_iota(jnp.int32, (OWN, 1), 0)
    return ids >= text[0]


def sum_blocks(got):
    total = got[0].astype(F32)
    for block in range(1, BLK):
        total = total + got[block].astype(F32)
    return total


def after_attention_kernel(where, text, got, tokens, mods, after, out):
    pick = picker(mods, own_video(where, text))
    residual = tokens[0, pl.ds(pl.multiple_of(where[2] * OWN, OWN), OWN), :].astype(F32)
    summed = residual + pick(2) * sum_blocks(got)
    after[...] = summed
    normed = (layer_norm(summed, 1e-05) * (1.0 + pick(4)) + pick(3)).astype(BF16)
    for block in range(BLK):
        out[block] = normed


def feed_forward_kernel(rows, weights, out, up, down, up_arrived, down_arrived):
    up_copy = pltpu.make_async_copy(weights.at[:, 0:PIECE, :], up, up_arrived)
    down_copy = pltpu.make_async_copy(weights.at[:, PIECE : 2 * PIECE, :], down, down_arrived)
    up_copy.start()
    down_copy.start()
    block = rows[...].reshape(TOK, D)
    up_copy.wait()
    hidden = jnp.dot(block, up[...].reshape(D, UNITS), preferred_element_type=F32)
    activated = jax.nn.gelu(hidden, approximate=True).astype(BF16)
    down_copy.wait()
    result = lax.dot_general(activated, down[...].reshape(D, UNITS), ROWS_BY_ROWS, preferred_element_type=F32)
    out[...] = result.astype(BF16).reshape(BLK, OWN, D)


def predict_kernel(where, text, got, after, mods, weight, hidden_out, predicted):
    pick = picker(mods, own_video(where, text))
    after_mlp = after[...] + pick(5) * sum_blocks(got)
    hidden_out[0] = after_mlp.astype(BF16)
    normed = (layer_norm(after_mlp, 1e-05) * (1.0 + pick(7)) + pick(6)).astype(BF16)
    predicted[...] = jnp.dot(normed, weight[...], preferred_element_type=F32)


def step_kernel(where, step, guidance, mine, other, latent, out):
    row = lax.broadcasted_iota(jnp.int32, (8, 128), 0)
    steps = row * 128 + lax.broadcasted_iota(jnp.int32, (8, 128), 1)
    low, high = math.sqrt(0.00085), math.sqrt(0.012)
    root_beta = low + steps.astype(F32) / 999.0 * (high - low)
    logs = jnp.log1p(-jnp.where(steps < 1000, root_beta * root_beta, 0.0))

    def alpha_bar(last):
        kept = jnp.where(steps <= last, logs, 0.0)
        return jnp.exp(jnp.sum(jnp.sum(kept, 1, keepdims=True), 0, keepdims=True))

    alpha_now = alpha_bar(step[0])
    alpha_prev = alpha_bar(step[0] - STRIDE)
    is_cond = where[0] == 0
    own, partner = mine[...], other[...]
    cond = jnp.where(is_cond, own, partner)
    uncond = jnp.where(is_cond, partner, own)
    both = uncond + guidance[0] * (cond - uncond)
    guided = jnp.where(is_cond, both[:, 0:32], both[:, 32:64])
    held = latent[...]
    root_now, root_rest = jnp.sqrt(alpha_now), jnp.sqrt(1.0 - alpha_now)
    clean = root_now * held - root_rest * guided
    noise = root_rest * held + root_now * guided
    out[...] = jnp.sqrt(alpha_prev) * clean + jnp.sqrt(1.0 - alpha_prev) * noise


def call(kernel, specs, shapes, mib=24, flops=10_000_000, scratch=()):
    return pl.pallas_call(
        kernel,
        out_shape=shapes,
        in_specs=specs,
        out_specs=jax.tree.map(lambda _: VMEM, shapes),
        scratch_shapes=scratch,
        compiler_params=pltpu.CompilerParams(vmem_limit_bytes=mib * 2**20),
        cost_estimate=pl.CostEstimate(flops=flops, bytes_accessed=4_000_000, transcendentals=0),
    )


def body(
    tokens_in,
    modulation,
    qk_gain,
    qkv_weight,
    out_weight,
    up_weight,
    down_weight,
    proj_weight,
    latent,
    text_count,
    positions,
    step_index,
    guidance,
):
    where = jnp.stack([lax.axis_index("cfg"), lax.axis_index("seq"), lax.axis_index("blk")]).astype(jnp.int32)

    piece = jnp.concatenate([up_weight, down_weight.T], 0)
    pieces = jnp.broadcast_to(piece[None], (4, 2 * PIECE, UNITS))
    pieces = lax.all_to_all(pieces, "seq", 0, 0, tiled=True, axis_index_groups=ALONG_Y)
    weights = lax.all_gather(
        pieces.reshape(8 * PIECE, UNITS), "seq", axis=0, tiled=True, axis_index_groups=ALONG_Z
    ).reshape(SEQ, 2 * PIECE, UNITS)

    sent = call(
        project_kernel,
        [SMEM, SMEM, VMEM, VMEM, VMEM, VMEM, VMEM, VMEM],
        jax.ShapeDtypeStruct((SEQ, 80, 128), BF16),
    )(where, text_count, tokens_in, modulation, qk_gain, qkv_weight, positions, jnp.asarray(frequencies()))
    got = lax.all_to_all(sent, "seq", 0, 0, tiled=True)
    attended = call(attend_kernel, [VMEM], jax.ShapeDtypeStruct((SEQ, 32, 128), BF16))(got)
    back = lax.all_to_all(attended, "seq", 0, 0, tiled=True)
    blocks = jax.ShapeDtypeStruct((BLK, OWN, D), BF16)
    partial = call(out_project_kernel, [VMEM, VMEM], blocks)(back, out_weight)
    partial = lax.all_to_all(partial, "blk", 0, 0, tiled=True)
    after, rows = call(
        after_attention_kernel,
        [SMEM, SMEM, VMEM, VMEM, VMEM],
        (jax.ShapeDtypeStruct((OWN, D), F32), blocks),
    )(where, text_count, partial, tokens_in, modulation)
    rows = lax.all_to_all(rows, "blk", 0, 0, tiled=True)
    half_weight = pltpu.VMEM((SEQ, PIECE, UNITS), BF16)
    mlp = call(
        feed_forward_kernel,
        [VMEM, ANY],
        blocks,
        scratch=[half_weight, half_weight, pltpu.SemaphoreType.DMA, pltpu.SemaphoreType.DMA],
    )(rows, weights)
    mlp = lax.all_to_all(mlp, "blk", 0, 0, tiled=True)
    hidden_out, predicted = call(
        predict_kernel,
        [SMEM, SMEM, VMEM, VMEM, VMEM, VMEM],
        (jax.ShapeDtypeStruct((1, OWN, D), BF16), jax.ShapeDtypeStruct((OWN, 64), F32)),
    )(where, text_count, mlp, after, modulation, proj_weight)
    partner = lax.ppermute(predicted, "cfg", [(0, 1), (1, 0)])
    latent_prev = call(
        step_kernel,
        [SMEM, SMEM, SMEM, VMEM, VMEM, VMEM],
        jax.ShapeDtypeStruct((OWN, 32), F32),
    )(where, step_index, guidance, predicted, partner, latent)
    return (hidden_out, latent_prev)


def solution(mesh):
    in_specs = (
        P("cfg", "seq", None),
        P(),
        P(),
        P(None, "blk", None),
        P("blk", None),
        P("seq", "blk"),
        P("blk", "seq"),
        P(),
        P(("seq", "blk"), "cfg"),
        P(),
        P(None, "seq"),
        P(),
        P(),
    )
    out_specs = (P("cfg", ("seq", "blk"), None), P(("seq", "blk"), "cfg"))
    return jax.shard_map(body, mesh=mesh, in_specs=in_specs, out_specs=out_specs, check_vma=False)
```

time: 745 us -> 155 us (0.21)
  waiting for transfers between devices: 684 us -> 14.3 us
  blocking collectives: 0 us -> 96.4 us
  matrix products: 14.7 us -> 0 us
  Pallas kernels: 0 us -> 12.5 us
  other arithmetic: 9.82 us -> 1.06 us
    all_gather x4 -> x1, waiting for transfers between devices: 576 us -> 0.01 us  [body(): lax.all_gather(pieces.reshape(8 * PIECE, UNITS), 'seq', axis=0, tiled=Tru...]
    all_to_all x0 -> x5, blocking collectives: none -> 96.4 us  [the longest x1 34.9 us: body(): got = lax.all_to_all(sent, 'seq', 0, 0, tiled=True)]
    psum x1 -> x0, waiting for transfers between devices: 65.8 us -> none  [body(): lax.psum(jnp.dot(attn_out, out_weight, preferred_element_type=jnp.float32...]
    reduce_scatter x1 -> x0, waiting for transfers between devices: 40 us -> none  [body(): lax.psum_scatter(mlp_part.astype(jnp.bfloat16), 'blk', scatter_dimension=...]
    dot_general x6 -> x0, matrix products: 14.7 us -> none  [the longest x1 4.6 us: absorb_block(): jnp.einsum('hts,shd->htd', weights.astype(jnp.bfloat16), value_block, pre...]
    pallas_call x0 -> x7, Pallas kernels: none -> 12.5 us  [the longest x1 3.46 us: body(): call(attend_kernel, [VMEM], jax.ShapeDtypeStruct((SEQ, 32, 128), BF16))(got)]
    all_to_all x0 -> x1, waiting for transfers between devices: none -> 8.62 us  [body(): mlp = lax.all_to_all(mlp, 'blk', 0, 0, tiled=True)]
    reduce_sum x12 -> x0, other arithmetic: 7.45 us -> none  [the longest x5 3.5 us: layer_norm(): average = jnp.mean(values, -1, keepdims=True)]
  transfers between devices with their start and end apart: 7 -> 3, of which waited for: 7 -> 2; matrix products, arithmetic and copies ran while one was open for 1% -> 0% of each run, Pallas kernels for 0% -> 5%
where the time goes in v1:
time: 155 us; the launch traced here: 154 us
  blocking collectives  96.4 us (62%)
  between operations  16.1 us (10%)
  waiting for transfers between devices  14.3 us (9%)
  Pallas kernels  12.5 us (8%)
  local copies, waits for them, and re-layouts  8.03 us (5%)
  starting transfers between devices  5.97 us (4%)
    all_to_all x1, blocking collectives, body(): got = lax.all_to_all(sent, 'seq', 0, 0, tiled=True)  34.9 us
    all_to_all x1, blocking collectives, body(): lax.all_to_all(pieces, 'seq', 0, 0, tiled=True, axis_index_groups=ALONG_Y)  20 us
    all_to_all x1, blocking collectives, body(): back = lax.all_to_all(attended, 'seq', 0, 0, tiled=True)  17.1 us
    all_to_all x1, blocking collectives, body(): partial = lax.all_to_all(partial, 'blk', 0, 0, tiled=True)  13 us
    all_to_all x1, blocking collectives, body(): rows = lax.all_to_all(rows, 'blk', 0, 0, tiled=True)  11.3 us
    all_to_all x1, waiting for transfers between devices, body(): mlp = lax.all_to_all(mlp, 'blk', 0, 0, tiled=True)  8.62 us
    unnamed x25, local copies, waits for them, and re-layouts  7.99 us
    ppermute x1, waiting for transfers between devices, body(): partner = lax.ppermute(predicted, 'cfg', [(0, 1), (1, 0)])  5.67 us
  transfers between devices with their start and end apart: 3, of which 2 were waited for; matrix products, arithmetic and copies ran while one was open for 0% of the time, Pallas kernels for 5%

profile of v1, /device:TPU:56, one launch (start us, length us, event | category | flops | bytes accessed | tf_op | source)
XLA Modules:
  0.0 154.4 jit_solution(5803785060005308228)
XLA Ops:
  7.2 0.0 copy-start.6
  7.2 0.0 all-gather.2.cloned.1.call-start
  7.2 1.0 pad_maximum_fusion
  8.3 0.0 copy-start.3
  8.3 0.0 copy-start.5
  8.3 20.0 %all_to_all.30 = bf16[4,96,768]{2,1,0:T(8,128)(2,1)} all-to-all(bf16[4,96,768]{2,1,0:T(8,128)(2,1)S(1)} %broadcast_in_dim.2), channel_id=1, replica_groups={{0,8,16,24},{32,40,48,56},{64,72,80,88},{96,104,112,120},{128,136,144,1..., dimensions={0} | all-to-all | bytes 1179648 | tf_op jit(solution)/shard_map/all_to_all | solution.py:277
  28.2 0.0 all-gather.2.cloned.1.call-update
  28.9 0.1 pad_add_fusion.where
  29.0 1.5 copy-done.1
  30.5 1.0 copy-done.2
  31.5 0.9 copy-done.4
  32.4 0.7 copy-done.7
  33.1 0.7 copy-done.8
  33.7 0.7 copy-done.9
  34.4 2.2 %shard_map.149 = bf16[32,80,128]{2,1,0:T(8,128)(2,1)S(1)} custom-call(s32[3]{0:T(128)S(1)} %pad_add_fusion.where, s32[1]{0:T(128)S(6)} %copy.17.text, bf16[1,128,1536]{2,1,0:T(8,128)(2,1)S(1)} %copy-done.2, f32[2,8,1536]{2,1,0:T(8,128)S(1)} %copy-done.4, f32[2,64]{1,0:T(2,128)S(1)} %copy-done.9, bf16[3,192,1536]{2,1,0:T(8,128)(2,1)S(1)} %copy-done.1, ...), custom_call_target="tpu_custom_call" | custom-call | flops 10000000 | bytes 4000000 | tf_op jit(solution)/shard_map/pallas_call | solution.py:282
  36.7 34.9 %all_to_all.31.got = bf16[32,80,128]{2,1,0:T(8,128)(2,1)S(1)} all-to-all(bf16[32,80,128]{2,1,0:T(8,128)(2,1)S(1)} %shard_map.149), channel_id=1, replica_groups=mesh['cfg'=2,'seq'=32,'blk'=8] {'seq'}, dimensions={0} | all-to-all | bytes 1310720 | tf_op jit(solution)/shard_map/all_to_all | solution.py:287
  71.6 3.5 %shard_map.150 = bf16[32,32,128]{2,1,0:T(8,128)(2,1)S(1)} custom-call(bf16[32,80,128]{2,1,0:T(8,128)(2,1)S(1)} %all_to_all.31.got), custom_call_target="tpu_custom_call" | custom-call | flops 10000000 | bytes 4000000 | tf_op jit(solution)/shard_map/pallas_call | solution.py:288
  75.1 17.1 %all_to_all.32.got = bf16[32,32,128]{2,1,0:T(8,128)(2,1)S(1)} all-to-all(bf16[32,32,128]{2,1,0:T(8,128)(2,1)S(1)} %shard_map.150), channel_id=1, replica_groups=mesh['cfg'=2,'seq'=32,'blk'=8] {'seq'}, dimensions={0} | all-to-all | bytes 524288 | tf_op jit(solution)/shard_map/all_to_all | solution.py:289
  92.2 0.9 shard_map.151
  93.1 13.0 %all_to_all.33.got = bf16[8,16,1536]{2,1,0:T(8,128)(2,1)S(1)} all-to-all(bf16[8,16,1536]{2,1,0:T(8,128)(2,1)S(1)} %shard_map.151), channel_id=1, replica_groups=mesh['cfg'=2,'seq'=32,'blk'=8] {'blk'}, dimensions={0} | all-to-all | bytes 786432 | tf_op jit(solution)/shard_map/all_to_all | solution.py:292
  106.1 0.0 copy-done.3
  106.1 0.8 shard_map.152
  107.0 11.3 %all_to_all.34.rows = bf16[8,16,1536]{2,1,0:T(8,128)(2,1)S(1)} all-to-all(bf16[8,16,1536]{2,1,0:T(8,128)(2,1)S(1)} %get-tuple-element.6), channel_id=1, replica_groups=mesh['cfg'=2,'seq'=32,'blk'=8] {'blk'}, dimensions={0} | all-to-all | bytes 786432 | tf_op jit(solution)/shard_map/all_to_all | solution.py:298
  118.3 2.3 %copy-done = bf16[3072,768]{1,0:T(8,128)(2,1)S(1)} copy-done((bf16[3072,768]{1,0:T(8,128)(2,1)S(1)}, bf16[3072,768]{1,0:T(8,128)(2,1)}, u32[]{:S(2)}) %copy-start) | copy-done | bytes 4718616
  120.6 2.6 %shard_map.153 = bf16[8,16,1536]{2,1,0:T(8,128)(2,1)} custom-call(bf16[8,16,1536]{2,1,0:T(8,128)(2,1)S(1)} %all_to_all.34.rows, bf16[32,96,768]{2,1,0:T(8,128)(2,1)S(1)} %bitcast.6), custom_call_target="tpu_custom_call" | custom-call | flops 10000000 | bytes 4000000 | tf_op jit(solution)/shard_map/pallas_call | solution.py:300
  123.3 3.5 %all-to-all-start.5 = ((bf16[8,16,1536]{2,1,0:T(8,128)(2,1)}), bf16[8,16,1536]{2,1,0:T(8,128)(2,1)S(1)}, u32[]{:S(2)}, u32[]{:S(2)}) async-start(bf16[8,16,1536]{2,1,0:T(8,128)(2,1)} %shard_map.153), calls=%async_computation.5 | async-start | bytes 786432 | tf_op jit(solution)/shard_map/all_to_all | solution.py:306
  126.7 0.2 copy.16.weight
  127.0 8.6 %all-to-all-done.5.got = bf16[8,16,1536]{2,1,0:T(8,128)(2,1)S(1)} async-done(((bf16[8,16,1536]{2,1,0:T(8,128)(2,1)}), bf16[8,16,1536]{2,1,0:T(8,128)(2,1)S(1)}, u32[]{:S(2)}, u32[]{:S(2)}) %all-to-all-start.5) | async-done | bytes 393248 | tf_op jit(solution)/shard_map/all_to_all | solution.py:306
  135.6 1.2 shard_map.154
  136.8 2.5 %collective-permute-start = (f32[16,64]{1,0:T(8,128)S(1)}, f32[16,64]{1,0:T(8,128)S(1)}, u32[]{:S(2)}, u32[]{:S(2)}) collective-permute-start(f32[16,64]{1,0:T(8,128)S(1)} %get-tuple-element.9.mine), channel_id=1, source_target_pairs={{0,256},{256,0},{1,257},{257,1},{2,258},{258,2},{3,259},{259,3},{4... | collective-permute-start | bytes 12296 | tf_op jit(solution)/shard_map/ppermute | solution.py:312
  140.6 5.7 %collective-permute-done.other = f32[16,64]{1,0:T(8,128)S(1)} collective-permute-done((f32[16,64]{1,0:T(8,128)S(1)}, f32[16,64]{1,0:T(8,128)S(1)}, u32[]{:S(2)}, u32[]{:S(2)}) %collective-permute-start) | collective-permute-done | bytes 4128 | tf_op jit(solution)/shard_map/ppermute | solution.py:312
  146.3 1.3 shard_map.155
  (15 shorter events, 0.1 us)
Async XLA Ops:
  7.2 85.0 %copy-start.6 = (bf16[192,1536]{1,0:T(8,128)(2,1)S(1)}, bf16[192,1536]{1,0:T(8,128)(2,1)}, u32[]{:S(2)}) copy-start(bf16[192,1536]{1,0:T(8,128)(2,1)} %weight.2) | copy-start | bytes 1769476
  7.2 111.1 %all-gather.2.cloned.1.call-start = ((), (), s32[]{:S(2)}) async-start(), calls=%async_computation.6 | async-start | bytes 5308416 | tf_op jit(solution)/shard_map/all_gather | solution.py:278
  8.3 97.9 %copy-start.3 = (bf16[1,128,1536]{2,1,0:T(8,128)(2,1)S(1)}, bf16[1,128,1536]{2,1,0:T(8,128)(2,1)}, u32[]{:S(2)}) copy-start(bf16[1,128,1536]{2,1,0:T(8,128)(2,1)} %tokens.3) | copy-start | bytes 1179652
  8.3 97.9 %copy-start.5 = (f32[2,8,1536]{2,1,0:T(8,128)S(1)}, f32[2,8,1536]{2,1,0:T(8,128)}, u32[]{:S(2)}) copy-start(f32[2,8,1536]{2,1,0:T(8,128)} %mods.5) | copy-start | bytes 294916
  29.0 1.5 copy-start.1
  30.5 1.0 copy-start.2
  31.5 0.9 copy-start.4
  32.4 0.7 copy-start.7
  33.1 0.7 copy-start.8
  33.7 0.7 copy-start.9
  92.2 34.5 %copy-start.11 = (bf16[1536,64]{0,1:T(8,128)(2,1)S(1)}, bf16[1536,64]{0,1:T(8,128)(2,1)}, u32[]{:S(2)}) copy-start(bf16[1536,64]{0,1:T(8,128)(2,1)} %param.21) | copy-start | bytes 589828
  106.1 40.1 %copy-start.10 = (f32[16,32]{1,0:T(8,128)S(1)}, f32[16,32]{1,0:T(8,128)}, u32[]{:S(2)}) copy-start(f32[16,32]{1,0:T(8,128)} %latent.1) | copy-start | bytes 6148
  118.3 2.3 %copy-start = (bf16[3072,768]{1,0:T(8,128)(2,1)S(1)}, bf16[3072,768]{1,0:T(8,128)(2,1)}, u32[]{:S(2)}) copy-start(bf16[3072,768]{1,0:T(8,128)(2,1)} %all-gather.2.cloned.1.call-done) | copy-start | bytes 14155780
  123.3 12.3 %all-to-all-start.5 = ((bf16[8,16,1536]{2,1,0:T(8,128)(2,1)}), bf16[8,16,1536]{2,1,0:T(8,128)(2,1)S(1)}, u32[]{:S(2)}, u32[]{:S(2)}) async-start(bf16[8,16,1536]{2,1,0:T(8,128)(2,1)} %shard_map.153), calls=%async_computation.5 | async-start | bytes 786432 | tf_op jit(solution)/shard_map/all_to_all | solution.py:306
  136.8 9.4 %collective-permute-start = (f32[16,64]{1,0:T(8,128)S(1)}, f32[16,64]{1,0:T(8,128)S(1)}, u32[]{:S(2)}, u32[]{:S(2)}) collective-permute-start(f32[16,64]{1,0:T(8,128)S(1)} %get-tuple-element.9.mine), channel_id=1, source_target_pairs={{0,256},{256,0},{1,257},{257,1},{2,258},{258,2},{3,259},{259,3},{4... | collective-permute-start | bytes 12296 | tf_op jit(solution)/shard_map/ppermute | solution.py:312
Sparse Core Ops, SparseCore 0:
  28.4 86.2 all-gather.1

commit v2 on v1

--- a/solution.py
+++ b/solution.py
@@ -19,7 +19,6 @@
 BLK = 8
 PIECE = 48
 
-ALONG_Z = [[4 * z + y for z in range(8)] for y in range(4)]
 ALONG_Y = [[4 * z + y for y in range(4)] for z in range(8)]
 
 VMEM = pl.BlockSpec(memory_space=pltpu.VMEM)
@@ -55,7 +54,15 @@
     return lambda row: jnp.where(video, mods[1, row : row + 1, :], mods[0, row : row + 1, :])
 
 
-def project_kernel(where, text, tokens, mods, gain, qkv, positions, table, out):
+def project_kernel(where, text, tokens_far, mods_far, gain, qkv_far, positions, table, out, tokens, mods, qkv, arrived):
+    copies = [
+        pltpu.make_async_copy(far, near, arrived.at[i])
+        for i, (far, near) in enumerate(((tokens_far, tokens), (mods_far, mods), (qkv_far, qkv)))
+    ]
+    for copy in copies:
+        copy.start()
+    copies[0].wait()
+    copies[1].wait()
     ids = where[1] * TOK + lax.broadcasted_iota(jnp.int32, (TOK, 1), 0)
     video = ids >= text[0]
     pick = picker(mods, video)
@@ -65,6 +72,7 @@
     def project(weight):
         return lax.dot_general(normed, weight, ROWS_BY_ROWS, preferred_element_type=F32)
 
+    copies[2].wait()
     heads = project(qkv[0:2].reshape(384, D))
     values_low = project(qkv[2, 0:128, :])
     values_high = project(qkv[2, 64:192, :])
@@ -195,16 +203,31 @@
         out[block] = normed
 
 
-def feed_forward_kernel(rows, weights, out, up, down, up_arrived, down_arrived):
-    up_copy = pltpu.make_async_copy(weights.at[:, 0:PIECE, :], up, up_arrived)
-    down_copy = pltpu.make_async_copy(weights.at[:, PIECE : 2 * PIECE, :], down, down_arrived)
-    up_copy.start()
-    down_copy.start()
+def feed_forward_kernel(where, rows, *refs):
+    weights, (out, up, down, arrived) = refs[:9], refs[9:]
+    places = [(where[1] // 4 + 8 - away) % 8 * 4 for away in (0, 1, 2, 3, -1, -2, -3, 4, 4)]
+    places[8] = places[8] + 2
+
+    def copies(side, near):
+        return [
+            pltpu.make_async_copy(
+                block.at[:, PIECE * side : PIECE * side + PIECE, :],
+                near.at[pl.ds(place, block.shape[0])],
+                arrived.at[side, i],
+            )
+            for i, (block, place) in enumerate(zip(weights, places))
+        ]
+
+    up_copies, down_copies = copies(0, up), copies(1, down)
+    for copy in up_copies + down_copies:
+        copy.start()
     block = rows[...].reshape(TOK, D)
-    up_copy.wait()
+    for copy in up_copies:
+        copy.wait()
     hidden = jnp.dot(block, up[...].reshape(D, UNITS), preferred_element_type=F32)
     activated = jax.nn.gelu(hidden, approximate=True).astype(BF16)
-    down_copy.wait()
+    for copy in down_copies:
+        copy.wait()
     result = lax.dot_general(activated, down[...].reshape(D, UNITS), ROWS_BY_ROWS, preferred_element_type=F32)
     out[...] = result.astype(BF16).reshape(BLK, OWN, D)
 
@@ -274,35 +297,53 @@
 
     piece = jnp.concatenate([up_weight, down_weight.T], 0)
     pieces = jnp.broadcast_to(piece[None], (4, 2 * PIECE, UNITS))
-    pieces = lax.all_to_all(pieces, "seq", 0, 0, tiled=True, axis_index_groups=ALONG_Y)
-    weights = lax.all_gather(
-        pieces.reshape(8 * PIECE, UNITS), "seq", axis=0, tiled=True, axis_index_groups=ALONG_Z
-    ).reshape(SEQ, 2 * PIECE, UNITS)
+    held = lax.all_to_all(pieces, "seq", 0, 0, tiled=True, axis_index_groups=ALONG_Y)
+
+    def shifted(block, step):
+        return lax.ppermute(block, "seq", [(s, (s + 4 * step) % SEQ) for s in range(SEQ)])
 
     sent = call(
         project_kernel,
-        [SMEM, SMEM, VMEM, VMEM, VMEM, VMEM, VMEM, VMEM],
+        [SMEM, SMEM, ANY, ANY, VMEM, ANY, VMEM, VMEM],
         jax.ShapeDtypeStruct((SEQ, 80, 128), BF16),
+        scratch=[
+            pltpu.VMEM((1, TOK, D), BF16),
+            pltpu.VMEM((2, 8, D), F32),
+            pltpu.VMEM((3, 192, D), BF16),
+            pltpu.SemaphoreType.DMA((3,)),
+        ],
     )(where, text_count, tokens_in, modulation, qk_gain, qkv_weight, positions, jnp.asarray(frequencies()))
+    sent, held = lax.optimization_barrier((sent, held))
+    below, above = [shifted(held, 1)], [shifted(held, -1)]
     got = lax.all_to_all(sent, "seq", 0, 0, tiled=True)
+    got, below, above = lax.optimization_barrier((got, below, above))
     attended = call(attend_kernel, [VMEM], jax.ShapeDtypeStruct((SEQ, 32, 128), BF16))(got)
+    below.append(shifted(below[0], 1))
+    above.append(shifted(above[0], -1))
     back = lax.all_to_all(attended, "seq", 0, 0, tiled=True)
+    back, below, above = lax.optimization_barrier((back, below, above))
     blocks = jax.ShapeDtypeStruct((BLK, OWN, D), BF16)
     partial = call(out_project_kernel, [VMEM, VMEM], blocks)(back, out_weight)
+    below.append(shifted(below[1], 1))
+    above.append(shifted(above[1], -1))
     partial = lax.all_to_all(partial, "blk", 0, 0, tiled=True)
+    partial, below, above = lax.optimization_barrier((partial, below, above))
     after, rows = call(
         after_attention_kernel,
         [SMEM, SMEM, VMEM, VMEM, VMEM],
         (jax.ShapeDtypeStruct((OWN, D), F32), blocks),
     )(where, text_count, partial, tokens_in, modulation)
+    far_low = shifted(below[2][0:2], 1)
+    far_high = shifted(above[2][2:4], -1)
     rows = lax.all_to_all(rows, "blk", 0, 0, tiled=True)
     half_weight = pltpu.VMEM((SEQ, PIECE, UNITS), BF16)
+    weights = [held, *below, *above, far_low, far_high]
     mlp = call(
         feed_forward_kernel,
-        [VMEM, ANY],
+        [SMEM, VMEM] + [ANY] * len(weights),
         blocks,
-        scratch=[half_weight, half_weight, pltpu.SemaphoreType.DMA, pltpu.SemaphoreType.DMA],
-    )(rows, weights)
+        scratch=[half_weight, half_weight, pltpu.SemaphoreType.DMA((2, len(weights)))],
+    )(where, rows, *weights)
     mlp = lax.all_to_all(mlp, "blk", 0, 0, tiled=True)
     hidden_out, predicted = call(
         predict_kernel,

time: 155 us -> 168 us (1.084)
  blocking collectives: 96.4 us -> 31.4 us
  starting transfers between devices: 5.97 us -> 59.3 us
  waiting for transfers between devices: 14.3 us -> 49.5 us
  between operations: 16.1 us -> 2.86 us
  Pallas kernels: 12.5 us -> 16.6 us
  local copies, waits for them, and re-layouts: 8.03 us -> 6.17 us
    all_to_all x3 -> x0, blocking collectives: 66.2 us -> none  [the longest x1 34.9 us: body(): got = lax.all_to_all(sent, 'seq', 0, 0, tiled=True)]
    ppermute x0 -> x8, starting transfers between devices: none -> 28.3 us  [shifted(): lax.ppermute(block, 'seq', [(s, (s + 4 * step) % SEQ) for s in range(SEQ)])]
    ppermute x0 -> x8, waiting for transfers between devices: none -> 28.2 us  [shifted(): lax.ppermute(block, 'seq', [(s, (s + 4 * step) % SEQ) for s in range(SEQ)])]
    all_to_all x0 -> x3, starting transfers between devices: none -> 23.7 us  [the longest x1 13.7 us: body(): got = lax.all_to_all(sent, 'seq', 0, 0, tiled=True)]
    all_to_all x0 -> x3, waiting for transfers between devices: none -> 8.19 us  [the longest x1 8.19 us: body(): lax.all_to_all(pieces, 'seq', 0, 0, tiled=True, axis_index_groups=ALONG_Y)]
    pallas_call x2, Pallas kernels: 4.87 us -> 8.08 us  [the longest x1 4.12 us: body(): call(feed_forward_kernel, [SMEM, VMEM] + [ANY] * len(weights), blocks, sc...]
    unnamed x25 -> x31, local copies, waits for them, and re-layouts: 7.99 us -> 5.27 us
  transfers between devices with their start and end apart: 3 -> 13, of which waited for: 2 -> 6; matrix products, arithmetic and copies ran while one was open for 0% -> 1% of each run, Pallas kernels for 5% -> 5%
where the time goes in v2:
time: 168 us; the launch traced here: 167 us
  starting transfers between devices  59.3 us (35%)
  waiting for transfers between devices  49.5 us (29%)
  blocking collectives  31.4 us (19%)
  Pallas kernels  16.6 us (10%)
  local copies, waits for them, and re-layouts  6.17 us (4%)
  between operations  2.86 us (2%)
    ppermute x8, starting transfers between devices, shifted(): lax.ppermute(block, 'seq', [(s, (s + 4 * step) % SEQ) for s in range(SEQ)])  28.3 us
    ppermute x8, waiting for transfers between devices, shifted(): lax.ppermute(block, 'seq', [(s, (s + 4 * step) % SEQ) for s in range(SEQ)])  28.2 us
    all_to_all x1, blocking collectives, body(): back = lax.all_to_all(attended, 'seq', 0, 0, tiled=True)  18.3 us
    all_to_all x1, starting transfers between devices, body(): got = lax.all_to_all(sent, 'seq', 0, 0, tiled=True)  13.7 us
    all_to_all x1, blocking collectives, body(): partial = lax.all_to_all(partial, 'blk', 0, 0, tiled=True)  13 us
    all_to_all x1, waiting for transfers between devices, body(): lax.all_to_all(pieces, 'seq', 0, 0, tiled=True, axis_index_groups=ALONG_Y)  8.19 us
    all_to_all x1, waiting for transfers between devices, body(): mlp = lax.all_to_all(mlp, 'blk', 0, 0, tiled=True)  7.79 us
    all_to_all x1, starting transfers between devices, body(): lax.all_to_all(pieces, 'seq', 0, 0, tiled=True, axis_index_groups=ALONG_Y)  6.37 us
  transfers between devices with their start and end apart: 13, of which 6 were waited for; matrix products, arithmetic and copies ran while one was open for 1% of the time, Pallas kernels for 5%

profile of v2, /device:TPU:56, one launch (start us, length us, event | category | flops | bytes accessed | tf_op | source)
XLA Modules:
  0.0 166.9 jit_solution(5784441613604147938)
XLA Ops:
  0.7 1.1 pad_maximum_fusion
  2.6 6.4 %all-to-all-start = ((bf16[4,96,768]{2,1,0:T(8,128)(2,1)}), bf16[4,96,768]{2,1,0:T(8,128)(2,1)S(1)}, u32[]{:S(2)}, u32[]{:S(2)}) async-start(bf16[4,96,768]{2,1,0:T(8,128)(2,1)} %broadcast_in_dim.2), calls=%async_computation | async-start | bytes 1179648 | tf_op jit(solution)/shard_map/all_to_all | solution.py:300
  10.6 4.0 %shard_map.149 = bf16[32,80,128]{2,1,0:T(8,128)(2,1)} custom-call(s32[3]{0:T(128)S(1)} %pad_add_fusion.where, s32[1]{0:T(128)S(6)} %copy.17.text, bf16[1,128,1536]{2,1,0:T(8,128)(2,1)S(1)} %copy-done.1, f32[2,8,1536]{2,1,0:T(8,128)S(1)} %copy-done.2, f32[2,64]{1,0:T(2,128)S(1)} %copy-done.13, bf16[3,192,1536]{2,1,0:T(8,128)(2,1)S(1)} %copy-done, ...), custom_call_target="tpu_custom_call" | custom-call | flops 10000000 | bytes 4000000 | tf_op jit(solution)/shard_map/pallas_call | solution.py:305
  14.6 8.2 %all-to-all-done.refs_0_ = bf16[4,96,768]{2,1,0:T(8,128)(2,1)S(1)} async-done(((bf16[4,96,768]{2,1,0:T(8,128)(2,1)}), bf16[4,96,768]{2,1,0:T(8,128)(2,1)S(1)}, u32[]{:S(2)}, u32[]{:S(2)}) %all-to-all-start) | async-done | bytes 589856 | tf_op jit(solution)/shard_map/all_to_all | solution.py:300
  22.8 13.7 %all-to-all-start.1 = ((bf16[32,80,128]{2,1,0:T(8,128)(2,1)}), bf16[32,80,128]{2,1,0:T(8,128)(2,1)S(1)}, u32[]{:S(2)}, u32[]{:S(2)}) async-start(bf16[32,80,128]{2,1,0:T(8,128)(2,1)} %shard_map.149), calls=%async_computation.1 | async-start | bytes 1310720 | tf_op jit(solution)/shard_map/all_to_all | solution.py:318
  36.5 3.5 %collective-permute-start = (bf16[4,96,768]{2,1,0:T(8,128)(2,1)S(1)}, bf16[4,96,768]{2,1,0:T(8,128)(2,1)S(1)}, u32[]{:S(2)}, u32[]{:S(2)}) collective-permute-start(bf16[4,96,768]{2,1,0:T(8,128)(2,1)S(1)} %all-to-all-done.refs_0_), channel_id=1, source_target_pairs={{0,32},{8,40},{16,48},{24,56},{32,64},{40,72},{48,80},{56,88},{64,... | collective-permute-start | bytes 1769480 | tf_op jit(solution)/shard_map/ppermute | solution.py:303
  40.1 3.7 %collective-permute-start.1 = (bf16[4,96,768]{2,1,0:T(8,128)(2,1)S(1)}, bf16[4,96,768]{2,1,0:T(8,128)(2,1)}, u32[]{:S(2)}, u32[]{:S(2)}) collective-permute-start(bf16[4,96,768]{2,1,0:T(8,128)(2,1)S(1)} %all-to-all-done.refs_0_), channel_id=1, source_target_pairs={{0,224},{8,232},{16,240},{24,248},{32,0},{40,8},{48,16},{56,24},{6... | collective-permute-start | bytes 1769480 | tf_op jit(solution)/shard_map/ppermute | solution.py:303
  43.8 21.6 %collective-permute-done.refs_1_ = bf16[4,96,768]{2,1,0:T(8,128)(2,1)S(1)} collective-permute-done((bf16[4,96,768]{2,1,0:T(8,128)(2,1)S(1)}, bf16[4,96,768]{2,1,0:T(8,128)(2,1)S(1)}, u32[]{:S(2)}, u32[]{:S(2)}) %collective-permute-start) | collective-permute-done | bytes 589856 | tf_op jit(solution)/shard_map/ppermute | solution.py:303
  65.3 2.4 %collective-permute-start.2 = (bf16[4,96,768]{2,1,0:T(8,128)(2,1)S(1)}, bf16[4,96,768]{2,1,0:T(8,128)(2,1)S(1)}, u32[]{:S(2)}, u32[]{:S(2)}) collective-permute-start(bf16[4,96,768]{2,1,0:T(8,128)(2,1)S(1)} %collective-permute-done.refs_1_), channel_id=1, source_target_pairs={{0,32},{8,40},{16,48},{24,56},{32,64},{40,72},{48,80},{56,88},{64,... | collective-permute-start | bytes 1769480 | tf_op jit(solution)/shard_map/ppermute | solution.py:303
  67.8 4.7 %collective-permute-start.3 = (bf16[4,96,768]{2,1,0:T(8,128)(2,1)}, bf16[4,96,768]{2,1,0:T(8,128)(2,1)S(1)}, u32[]{:S(2)}, u32[]{:S(2)}) collective-permute-start(bf16[4,96,768]{2,1,0:T(8,128)(2,1)} %collective-permute-done.1.refs_4_), channel_id=1, source_target_pairs={{0,224},{8,232},{16,240},{24,248},{32,0},{40,8},{48,16},{56,24},{6... | collective-permute-start | bytes 1769480 | tf_op jit(solution)/shard_map/ppermute | solution.py:303
  72.4 3.5 %shard_map.150 = bf16[32,32,128]{2,1,0:T(8,128)(2,1)S(1)} custom-call(bf16[32,80,128]{2,1,0:T(8,128)(2,1)S(1)} %all-to-all-done.1.got), custom_call_target="tpu_custom_call" | custom-call | flops 10000000 | bytes 4000000 | tf_op jit(solution)/shard_map/pallas_call | solution.py:320
  76.0 18.3 %all_to_all.30.got = bf16[32,32,128]{2,1,0:T(8,128)(2,1)S(1)} all-to-all(bf16[32,32,128]{2,1,0:T(8,128)(2,1)S(1)} %shard_map.150), channel_id=1, replica_groups=mesh['cfg'=2,'seq'=32,'blk'=8] {'seq'}, dimensions={0} | all-to-all | bytes 524288 | tf_op jit(solution)/shard_map/all_to_all | solution.py:323
  94.3 2.4 %collective-permute-start.4 = (bf16[4,96,768]{2,1,0:T(8,128)(2,1)S(1)}, bf16[4,96,768]{2,1,0:T(8,128)(2,1)S(1)}, u32[]{:S(2)}, u32[]{:S(2)}) collective-permute-start(bf16[4,96,768]{2,1,0:T(8,128)(2,1)S(1)} %collective-permute-done.2.refs_2_), channel_id=1, source_target_pairs={{0,32},{8,40},{16,48},{24,56},{32,64},{40,72},{48,80},{56,88},{64,... | collective-permute-start | bytes 1769480 | tf_op jit(solution)/shard_map/ppermute | solution.py:303
  96.7 4.6 %collective-permute-start.5 = (bf16[4,96,768]{2,1,0:T(8,128)(2,1)S(1)}, bf16[4,96,768]{2,1,0:T(8,128)(2,1)S(1)}, u32[]{:S(2)}, u32[]{:S(2)}) collective-permute-start(bf16[4,96,768]{2,1,0:T(8,128)(2,1)S(1)} %collective-permute-done.3.refs_5_), channel_id=1, source_target_pairs={{0,224},{8,232},{16,240},{24,248},{32,0},{40,8},{48,16},{56,24},{6... | collective-permute-start | bytes 1769480 | tf_op jit(solution)/shard_map/ppermute | solution.py:303
  101.4 1.1 copy-done.4
  103.3 13.0 %all_to_all.31.got = bf16[8,16,1536]{2,1,0:T(8,128)(2,1)S(1)} all-to-all(bf16[8,16,1536]{2,1,0:T(8,128)(2,1)S(1)} %shard_map.151), channel_id=1, replica_groups=mesh['cfg'=2,'seq'=32,'blk'=8] {'blk'}, dimensions={0} | all-to-all | bytes 786432 | tf_op jit(solution)/shard_map/all_to_all | solution.py:329
  116.4 1.6 shard_map.152
  118.0 3.6 %all-to-all-start.4 = ((bf16[8,16,1536]{2,1,0:T(8,128)(2,1)}), bf16[8,16,1536]{2,1,0:T(8,128)(2,1)S(1)}, u32[]{:S(2)}, u32[]{:S(2)}) async-start(bf16[8,16,1536]{2,1,0:T(8,128)(2,1)} %get-tuple-element.34), calls=%async_computation.4 | async-start | bytes 786432 | tf_op jit(solution)/shard_map/all_to_all | solution.py:338
  121.6 1.9 %collective-permute-start.6 = (bf16[2,96,768]{2,1,0:T(8,128)(2,1)S(1)}, bf16[2,96,768]{2,1,0:T(8,128)(2,1)S(1)}, u32[]{:S(2)}, u32[]{:S(2)}) collective-permute-start(bf16[2,96,768]{2,1,0:T(8,128)(2,1)S(1)} %slice.6), channel_id=1, source_target_pairs={{0,32},{8,40},{16,48},{24,56},{32,64},{40,72},{48,80},{56,88},{64,... | collective-permute-start | bytes 884744 | tf_op jit(solution)/shard_map/ppermute | solution.py:303
  123.6 5.1 %collective-permute-start.7 = (bf16[2,96,768]{2,1,0:T(8,128)(2,1)S(1)}, bf16[2,96,768]{2,1,0:T(8,128)(2,1)S(1)}, u32[]{:S(2)}, u32[]{:S(2)}) collective-permute-start(bf16[2,96,768]{2,1,0:T(8,128)(2,1)S(1)} %slice.7), channel_id=1, source_target_pairs={{0,224},{8,232},{16,240},{24,248},{32,0},{40,8},{48,16},{56,24},{6... | collective-permute-start | bytes 884744 | tf_op jit(solution)/shard_map/ppermute | solution.py:303
  128.7 5.3 %collective-permute-done.6.refs_7_ = bf16[2,96,768]{2,1,0:T(8,128)(2,1)S(1)} collective-permute-done((bf16[2,96,768]{2,1,0:T(8,128)(2,1)S(1)}, bf16[2,96,768]{2,1,0:T(8,128)(2,1)S(1)}, u32[]{:S(2)}, u32[]{:S(2)}) %collective-permute-start.6) | collective-permute-done | bytes 294944 | tf_op jit(solution)/shard_map/ppermute | solution.py:303
  134.1 1.2 collective-permute-done.7.refs_8_
  135.3 1.1 copy-done.6
  136.3 1.1 copy-done.10
  137.4 4.1 %shard_map.153 = bf16[8,16,1536]{2,1,0:T(8,128)(2,1)} custom-call(s32[3]{0:T(128)S(1)} %pad_add_fusion.where, bf16[8,16,1536]{2,1,0:T(8,128)(2,1)S(1)} %all-to-all-done.4.rows, bf16[4,96,768]{2,1,0:T(8,128)(2,1)S(1)} %all-to-all-done.refs_0_, bf16[4,96,768]{2,1,0:T(8,128)(2,1)S(1)} %copy-done.6, bf16[4,96,768]{2,1,0:T(8,128)(2,1)S(1)} %copy-done.8, ...), custom_call_target="tpu_custom_call" | custom-call | flops 10000000 | bytes 4000000 | tf_op jit(solution)/shard_map/pallas_call | solution.py:341
  141.5 4.4 %all-to-all-start.5 = ((bf16[8,16,1536]{2,1,0:T(8,128)(2,1)}), bf16[8,16,1536]{2,1,0:T(8,128)(2,1)S(1)}, u32[]{:S(2)}, u32[]{:S(2)}) async-start(bf16[8,16,1536]{2,1,0:T(8,128)(2,1)} %shard_map.153), calls=%async_computation.5 | async-start | bytes 786432 | tf_op jit(solution)/shard_map/all_to_all | solution.py:347
  146.0 1.1 copy.16.weight
  147.1 7.8 %all-to-all-done.5.got = bf16[8,16,1536]{2,1,0:T(8,128)(2,1)S(1)} async-done(((bf16[8,16,1536]{2,1,0:T(8,128)(2,1)}), bf16[8,16,1536]{2,1,0:T(8,128)(2,1)S(1)}, u32[]{:S(2)}, u32[]{:S(2)}) %all-to-all-start.5) | async-done | bytes 393248 | tf_op jit(solution)/shard_map/all_to_all | solution.py:347
  154.9 1.2 shard_map.154
  156.2 2.8 %collective-permute-start.8 = (f32[16,64]{1,0:T(8,128)S(1)}, f32[16,64]{1,0:T(8,128)S(1)}, u32[]{:S(2)}, u32[]{:S(2)}) collective-permute-start(f32[16,64]{1,0:T(8,128)S(1)} %get-tuple-element.43.mine), channel_id=1, source_target_pairs={{0,256},{256,0},{1,257},{257,1},{2,258},{258,2},{3,259},{259,3},{4... | collective-permute-start | bytes 12296 | tf_op jit(solution)/shard_map/ppermute | solution.py:353
  160.3 5.3 %collective-permute-done.8.other = f32[16,64]{1,0:T(8,128)S(1)} collective-permute-done((f32[16,64]{1,0:T(8,128)S(1)}, f32[16,64]{1,0:T(8,128)S(1)}, u32[]{:S(2)}, u32[]{:S(2)}) %collective-permute-start.8) | collective-permute-done | bytes 4128 | tf_op jit(solution)/shard_map/ppermute | solution.py:353
  165.6 1.3 shard_map.155
  (39 shorter events, 2.8 us)
Async XLA Ops:
  0.6 9.1 %copy-start.11 = (f32[8,128]{1,0:T(8,128)S(1)}, f32[8,128]{1,0:T(8,128)}, u32[]{:S(2)}) copy-start(f32[8,128]{1,0:T(8,128)} %constant.17.clone.table) | copy-start | bytes 12292
  0.6 9.1 %copy-start.1 = (bf16[1,128,1536]{2,1,0:T(8,128)(2,1)S(1)}, bf16[1,128,1536]{2,1,0:T(8,128)(2,1)}, u32[]{:S(2)}) copy-start(bf16[1,128,1536]{2,1,0:T(8,128)(2,1)} %tokens.1) | copy-start | bytes 1179652
  0.7 9.1 %copy-start.13 = (f32[2,64]{1,0:T(2,128)S(1)}, f32[2,64]{1,0:T(2,128)}, u32[]{:S(2)}) copy-start(f32[2,64]{1,0:T(2,128)} %gain.1) | copy-start | bytes 1540
  0.7 9.1 %copy-start = (bf16[3,192,1536]{2,1,0:T(8,128)(2,1)S(1)}, bf16[3,192,1536]{2,1,0:T(8,128)(2,1)}, u32[]{:S(2)}) copy-start(bf16[3,192,1536]{2,1,0:T(8,128)(2,1)} %qkv_far.1) | copy-start | bytes 5308420
  0.7 9.1 %copy-start.12 = (s32[3,128]{1,0:T(4,128)S(1)}, s32[3,128]{1,0:T(4,128)}, u32[]{:S(2)}) copy-start(s32[3,128]{1,0:T(4,128)} %positions.1) | copy-start | bytes 4612
  2.6 20.2 %all-to-all-start = ((bf16[4,96,768]{2,1,0:T(8,128)(2,1)}), bf16[4,96,768]{2,1,0:T(8,128)(2,1)S(1)}, u32[]{:S(2)}, u32[]{:S(2)}) async-start(bf16[4,96,768]{2,1,0:T(8,128)(2,1)} %broadcast_in_dim.2), calls=%async_computation | async-start | bytes 1179648 | tf_op jit(solution)/shard_map/all_to_all | solution.py:300
  9.7 0.9 copy-start.2
  22.8 42.5 %all-to-all-start.1 = ((bf16[32,80,128]{2,1,0:T(8,128)(2,1)}), bf16[32,80,128]{2,1,0:T(8,128)(2,1)S(1)}, u32[]{:S(2)}, u32[]{:S(2)}) async-start(bf16[32,80,128]{2,1,0:T(8,128)(2,1)} %shard_map.149), calls=%async_computation.1 | async-start | bytes 1310720 | tf_op jit(solution)/shard_map/all_to_all | solution.py:318
  36.5 79.9 %copy-start.3 = (f32[2,8,1536]{2,1,0:T(8,128)S(1)}, f32[2,8,1536]{2,1,0:T(8,128)}, u32[]{:S(2)}) copy-start(f32[2,8,1536]{2,1,0:T(8,128)} %mods.3) | copy-start | bytes 294916
  36.5 28.8 %collective-permute-start = (bf16[4,96,768]{2,1,0:T(8,128)(2,1)S(1)}, bf16[4,96,768]{2,1,0:T(8,128)(2,1)S(1)}, u32[]{:S(2)}, u32[]{:S(2)}) collective-permute-start(bf16[4,96,768]{2,1,0:T(8,128)(2,1)S(1)} %all-to-all-done.refs_0_), channel_id=1, source_target_pairs={{0,32},{8,40},{16,48},{24,56},{32,64},{40,72},{48,80},{56,88},{64,... | collective-permute-start | bytes 1769480 | tf_op jit(solution)/shard_map/ppermute | solution.py:303
  40.1 25.3 %collective-permute-start.1 = (bf16[4,96,768]{2,1,0:T(8,128)(2,1)S(1)}, bf16[4,96,768]{2,1,0:T(8,128)(2,1)}, u32[]{:S(2)}, u32[]{:S(2)}) collective-permute-start(bf16[4,96,768]{2,1,0:T(8,128)(2,1)S(1)} %all-to-all-done.refs_0_), channel_id=1, source_target_pairs={{0,224},{8,232},{16,240},{24,248},{32,0},{40,8},{48,16},{56,24},{6... | collective-permute-start | bytes 1769480 | tf_op jit(solution)/shard_map/ppermute | solution.py:303
  65.3 29.0 %copy-start.5 = (bf16[4,96,768]{2,1,0:T(8,128)(2,1)}, bf16[4,96,768]{2,1,0:T(8,128)(2,1)S(1)}, u32[]{:S(2)}) copy-start(bf16[4,96,768]{2,1,0:T(8,128)(2,1)S(1)} %collective-permute-done.refs_1_) | copy-start | bytes 1769476
  65.3 28.9 %collective-permute-start.2 = (bf16[4,96,768]{2,1,0:T(8,128)(2,1)S(1)}, bf16[4,96,768]{2,1,0:T(8,128)(2,1)S(1)}, u32[]{:S(2)}, u32[]{:S(2)}) collective-permute-start(bf16[4,96,768]{2,1,0:T(8,128)(2,1)S(1)} %collective-permute-done.refs_1_), channel_id=1, source_target_pairs={{0,32},{8,40},{16,48},{24,56},{32,64},{40,72},{48,80},{56,88},{64,... | collective-permute-start | bytes 1769480 | tf_op jit(solution)/shard_map/ppermute | solution.py:303
  67.8 26.6 %collective-permute-start.3 = (bf16[4,96,768]{2,1,0:T(8,128)(2,1)}, bf16[4,96,768]{2,1,0:T(8,128)(2,1)S(1)}, u32[]{:S(2)}, u32[]{:S(2)}) collective-permute-start(bf16[4,96,768]{2,1,0:T(8,128)(2,1)} %collective-permute-done.1.refs_4_), channel_id=1, source_target_pairs={{0,224},{8,232},{16,240},{24,248},{32,0},{40,8},{48,16},{56,24},{6... | collective-permute-start | bytes 1769480 | tf_op jit(solution)/shard_map/ppermute | solution.py:303
  94.3 22.1 %copy-start.7 = (bf16[4,96,768]{2,1,0:T(8,128)(2,1)}, bf16[4,96,768]{2,1,0:T(8,128)(2,1)S(1)}, u32[]{:S(2)}) copy-start(bf16[4,96,768]{2,1,0:T(8,128)(2,1)S(1)} %collective-permute-done.2.refs_2_) | copy-start | bytes 1769476
  94.3 23.7 %copy-start.9 = (bf16[4,96,768]{2,1,0:T(8,128)(2,1)}, bf16[4,96,768]{2,1,0:T(8,128)(2,1)S(1)}, u32[]{:S(2)}) copy-start(bf16[4,96,768]{2,1,0:T(8,128)(2,1)S(1)} %collective-permute-done.3.refs_5_) | copy-start | bytes 1769476
  94.3 22.1 %collective-permute-start.4 = (bf16[4,96,768]{2,1,0:T(8,128)(2,1)S(1)}, bf16[4,96,768]{2,1,0:T(8,128)(2,1)S(1)}, u32[]{:S(2)}, u32[]{:S(2)}) collective-permute-start(bf16[4,96,768]{2,1,0:T(8,128)(2,1)S(1)} %collective-permute-done.2.refs_2_), channel_id=1, source_target_pairs={{0,32},{8,40},{16,48},{24,56},{32,64},{40,72},{48,80},{56,88},{64,... | collective-permute-start | bytes 1769480 | tf_op jit(solution)/shard_map/ppermute | solution.py:303
  96.7 19.6 %collective-permute-start.5 = (bf16[4,96,768]{2,1,0:T(8,128)(2,1)S(1)}, bf16[4,96,768]{2,1,0:T(8,128)(2,1)S(1)}, u32[]{:S(2)}, u32[]{:S(2)}) collective-permute-start(bf16[4,96,768]{2,1,0:T(8,128)(2,1)S(1)} %collective-permute-done.3.refs_5_), channel_id=1, source_target_pairs={{0,224},{8,232},{16,240},{24,248},{32,0},{40,8},{48,16},{56,24},{6... | collective-permute-start | bytes 1769480 | tf_op jit(solution)/shard_map/ppermute | solution.py:303
  101.4 1.1 copy-start.4
  118.0 17.3 %copy-start.8 = (bf16[4,96,768]{2,1,0:T(8,128)(2,1)S(1)}, bf16[4,96,768]{2,1,0:T(8,128)(2,1)}, u32[]{:S(2)}) copy-start(bf16[4,96,768]{2,1,0:T(8,128)(2,1)} %copy-done.7) | copy-start | bytes 1769476
  118.0 17.3 %all-to-all-start.4 = ((bf16[8,16,1536]{2,1,0:T(8,128)(2,1)}), bf16[8,16,1536]{2,1,0:T(8,128)(2,1)S(1)}, u32[]{:S(2)}, u32[]{:S(2)}) async-start(bf16[8,16,1536]{2,1,0:T(8,128)(2,1)} %get-tuple-element.34), calls=%async_computation.4 | async-start | bytes 786432 | tf_op jit(solution)/shard_map/all_to_all | solution.py:338
  121.6 12.4 %collective-permute-start.6 = (bf16[2,96,768]{2,1,0:T(8,128)(2,1)S(1)}, bf16[2,96,768]{2,1,0:T(8,128)(2,1)S(1)}, u32[]{:S(2)}, u32[]{:S(2)}) collective-permute-start(bf16[2,96,768]{2,1,0:T(8,128)(2,1)S(1)} %slice.6), channel_id=1, source_target_pairs={{0,32},{8,40},{16,48},{24,56},{32,64},{40,72},{48,80},{56,88},{64,... | collective-permute-start | bytes 884744 | tf_op jit(solution)/shard_map/ppermute | solution.py:303
  123.6 11.7 %collective-permute-start.7 = (bf16[2,96,768]{2,1,0:T(8,128)(2,1)S(1)}, bf16[2,96,768]{2,1,0:T(8,128)(2,1)S(1)}, u32[]{:S(2)}, u32[]{:S(2)}) collective-permute-start(bf16[2,96,768]{2,1,0:T(8,128)(2,1)S(1)} %slice.7), channel_id=1, source_target_pairs={{0,224},{8,232},{16,240},{24,248},{32,0},{40,8},{48,16},{56,24},{6... | collective-permute-start | bytes 884744 | tf_op jit(solution)/shard_map/ppermute | solution.py:303
  135.3 1.1 copy-start.6
  136.3 1.1 copy-start.10
  141.5 24.1 %copy-start.14 = (f32[16,32]{1,0:T(8,128)S(1)}, f32[16,32]{1,0:T(8,128)}, u32[]{:S(2)}) copy-start(f32[16,32]{1,0:T(8,128)} %latent.1) | copy-start | bytes 6148
  141.5 13.4 %all-to-all-start.5 = ((bf16[8,16,1536]{2,1,0:T(8,128)(2,1)}), bf16[8,16,1536]{2,1,0:T(8,128)(2,1)S(1)}, u32[]{:S(2)}, u32[]{:S(2)}) async-start(bf16[8,16,1536]{2,1,0:T(8,128)(2,1)} %shard_map.153), calls=%async_computation.5 | async-start | bytes 786432 | tf_op jit(solution)/shard_map/all_to_all | solution.py:347
  156.2 9.4 %collective-permute-start.8 = (f32[16,64]{1,0:T(8,128)S(1)}, f32[16,64]{1,0:T(8,128)S(1)}, u32[]{:S(2)}, u32[]{:S(2)}) collective-permute-start(f32[16,64]{1,0:T(8,128)S(1)} %get-tuple-element.43.mine), channel_id=1, source_target_pairs={{0,256},{256,0},{1,257},{257,1},{2,258},{258,2},{3,259},{259,3},{4... | collective-permute-start | bytes 12296 | tf_op jit(solution)/shard_map/ppermute | solution.py:353

commit v3 on v1

--- a/solution.py
+++ b/solution.py
@@ -14,17 +14,20 @@
 TOK = 128
 OWN = 16
 D = 1536
-UNITS = 768
+UNITS = 384
 SEQ = 32
 BLK = 8
+GROUP = 16
 PIECE = 48
 
-ALONG_Z = [[4 * z + y for z in range(8)] for y in range(4)]
-ALONG_Y = [[4 * z + y for y in range(4)] for z in range(8)]
+SEQ_AXES = ("z", "pair", "side")
+LINE = ("pair", "side")
+SHARERS = ("side", "blk")
 
 VMEM = pl.BlockSpec(memory_space=pltpu.VMEM)
 SMEM = pl.BlockSpec(memory_space=pltpu.SMEM)
 ANY = pl.BlockSpec(memory_space=pl.ANY)
+HBM = pl.BlockSpec(memory_space=pltpu.HBM)
 
 ROWS_BY_ROWS = (((1,), (1,)), ((), ()))
 
@@ -55,7 +58,15 @@
     return lambda row: jnp.where(video, mods[1, row : row + 1, :], mods[0, row : row + 1, :])
 
 
-def project_kernel(where, text, tokens, mods, gain, qkv, positions, table, out):
+def project_kernel(where, text, tokens_far, mods_far, gain, qkv_far, positions, table, out, tokens, mods, qkv, arrived):
+    copies = [
+        pltpu.make_async_copy(far, near, arrived.at[i])
+        for i, (far, near) in enumerate(((tokens_far, tokens), (mods_far, mods), (qkv_far, qkv)))
+    ]
+    for copy in copies:
+        copy.start()
+    copies[0].wait()
+    copies[1].wait()
     ids = where[1] * TOK + lax.broadcasted_iota(jnp.int32, (TOK, 1), 0)
     video = ids >= text[0]
     pick = picker(mods, video)
@@ -65,6 +76,7 @@
     def project(weight):
         return lax.dot_general(normed, weight, ROWS_BY_ROWS, preferred_element_type=F32)
 
+    copies[2].wait()
     heads = project(qkv[0:2].reshape(384, D))
     values_low = project(qkv[2, 0:128, :])
     values_high = project(qkv[2, 64:192, :])
@@ -180,7 +192,7 @@
 
 def sum_blocks(got):
     total = got[0].astype(F32)
-    for block in range(1, BLK):
+    for block in range(1, got.shape[0]):
         total = total + got[block].astype(F32)
     return total
 
@@ -191,7 +203,7 @@
     summed = residual + pick(2) * sum_blocks(got)
     after[...] = summed
     normed = (layer_norm(summed, 1e-05) * (1.0 + pick(4)) + pick(3)).astype(BF16)
-    for block in range(BLK):
+    for block in range(GROUP):
         out[block] = normed
 
 
@@ -200,13 +212,26 @@
     down_copy = pltpu.make_async_copy(weights.at[:, PIECE : 2 * PIECE, :], down, down_arrived)
     up_copy.start()
     down_copy.start()
-    block = rows[...].reshape(TOK, D)
+    block = rows[...].reshape(GROUP * OWN, D)
     up_copy.wait()
     hidden = jnp.dot(block, up[...].reshape(D, UNITS), preferred_element_type=F32)
     activated = jax.nn.gelu(hidden, approximate=True).astype(BF16)
     down_copy.wait()
     result = lax.dot_general(activated, down[...].reshape(D, UNITS), ROWS_BY_ROWS, preferred_element_type=F32)
-    out[...] = result.astype(BF16).reshape(BLK, OWN, D)
+    out[...] = result.astype(BF16).reshape(GROUP, OWN, D)
+
+
+def pieces_kernel(up, down, out, arrived):
+    copies = []
+    for device in range(4):
+        half = pl.ds(UNITS * (device % 2), UNITS)
+        for side, weight in enumerate((up, down)):
+            rows = pl.ds(PIECE * side, PIECE)
+            copies.append(pltpu.make_async_copy(weight.at[:, half], out.at[device, rows, :], arrived.at[device, side]))
+    for copy in copies:
+        copy.start()
+    for copy in copies:
+        copy.wait()
 
 
 def predict_kernel(where, text, got, after, mods, weight, hidden_out, predicted):
@@ -270,40 +295,50 @@
     step_index,
     guidance,
 ):
-    where = jnp.stack([lax.axis_index("cfg"), lax.axis_index("seq"), lax.axis_index("blk")]).astype(jnp.int32)
-
-    piece = jnp.concatenate([up_weight, down_weight.T], 0)
-    pieces = jnp.broadcast_to(piece[None], (4, 2 * PIECE, UNITS))
-    pieces = lax.all_to_all(pieces, "seq", 0, 0, tiled=True, axis_index_groups=ALONG_Y)
-    weights = lax.all_gather(
-        pieces.reshape(8 * PIECE, UNITS), "seq", axis=0, tiled=True, axis_index_groups=ALONG_Z
-    ).reshape(SEQ, 2 * PIECE, UNITS)
+    where = jnp.stack([lax.axis_index("cfg"), lax.axis_index(SEQ_AXES), lax.axis_index("blk")]).astype(jnp.int32)
+
+    pieces = call(
+        pieces_kernel,
+        [HBM, HBM],
+        jax.ShapeDtypeStruct((4, 2 * PIECE, UNITS), BF16),
+        scratch=[pltpu.SemaphoreType.DMA((4, 2))],
+    )(up_weight, down_weight.T)
+    pieces = lax.all_to_all(pieces, LINE, 0, 0, tiled=True)
 
     sent = call(
         project_kernel,
-        [SMEM, SMEM, VMEM, VMEM, VMEM, VMEM, VMEM, VMEM],
+        [SMEM, SMEM, ANY, ANY, VMEM, ANY, VMEM, VMEM],
         jax.ShapeDtypeStruct((SEQ, 80, 128), BF16),
+        scratch=[
+            pltpu.VMEM((1, TOK, D), BF16),
+            pltpu.VMEM((2, 8, D), F32),
+            pltpu.VMEM((3, 192, D), BF16),
+            pltpu.SemaphoreType.DMA((3,)),
+        ],
     )(where, text_count, tokens_in, modulation, qk_gain, qkv_weight, positions, jnp.asarray(frequencies()))
-    got = lax.all_to_all(sent, "seq", 0, 0, tiled=True)
+    sent, pieces = lax.optimization_barrier((sent, pieces))
+    weights = lax.all_gather(pieces, "z", axis=0, tiled=True)
+    got = lax.all_to_all(sent, SEQ_AXES, 0, 0, tiled=True)
     attended = call(attend_kernel, [VMEM], jax.ShapeDtypeStruct((SEQ, 32, 128), BF16))(got)
-    back = lax.all_to_all(attended, "seq", 0, 0, tiled=True)
+    back = lax.all_to_all(attended, SEQ_AXES, 0, 0, tiled=True)
     blocks = jax.ShapeDtypeStruct((BLK, OWN, D), BF16)
+    shared = jax.ShapeDtypeStruct((GROUP, OWN, D), BF16)
     partial = call(out_project_kernel, [VMEM, VMEM], blocks)(back, out_weight)
     partial = lax.all_to_all(partial, "blk", 0, 0, tiled=True)
     after, rows = call(
         after_attention_kernel,
         [SMEM, SMEM, VMEM, VMEM, VMEM],
-        (jax.ShapeDtypeStruct((OWN, D), F32), blocks),
+        (jax.ShapeDtypeStruct((OWN, D), F32), shared),
     )(where, text_count, partial, tokens_in, modulation)
-    rows = lax.all_to_all(rows, "blk", 0, 0, tiled=True)
+    rows = lax.all_to_all(rows, SHARERS, 0, 0, tiled=True)
     half_weight = pltpu.VMEM((SEQ, PIECE, UNITS), BF16)
     mlp = call(
         feed_forward_kernel,
-        [VMEM, ANY],
-        blocks,
+        [VMEM, HBM],
+        shared,
         scratch=[half_weight, half_weight, pltpu.SemaphoreType.DMA, pltpu.SemaphoreType.DMA],
     )(rows, weights)
-    mlp = lax.all_to_all(mlp, "blk", 0, 0, tiled=True)
+    mlp = lax.all_to_all(mlp, SHARERS, 0, 0, tiled=True)
     hidden_out, predicted = call(
         predict_kernel,
         [SMEM, SMEM, VMEM, VMEM, VMEM, VMEM],
@@ -319,20 +354,23 @@
 
 
 def solution(mesh):
+    devices = mesh.devices.reshape(2, 8, 2, 2, 8)
+    fine = jax.sharding.Mesh(devices, ("cfg", *SEQ_AXES, "blk"))
+    rows = (*SEQ_AXES, "blk")
     in_specs = (
-        P("cfg", "seq", None),
+        P("cfg", SEQ_AXES, None),
         P(),
         P(),
         P(None, "blk", None),
         P("blk", None),
-        P("seq", "blk"),
-        P("blk", "seq"),
-        P(),
-        P(("seq", "blk"), "cfg"),
-        P(),
-        P(None, "seq"),
+        P(SEQ_AXES, "blk"),
+        P("blk", SEQ_AXES),
+        P(),
+        P(rows, "cfg"),
+        P(),
+        P(None, SEQ_AXES),
         P(),
         P(),
     )
-    out_specs = (P("cfg", ("seq", "blk"), None), P(("seq", "blk"), "cfg"))
-    return jax.shard_map(body, mesh=mesh, in_specs=in_specs, out_specs=out_specs, check_vma=False)
+    out_specs = (P("cfg", rows, None), P(rows, "cfg"))
+    return jax.shard_map(body, mesh=fine, in_specs=in_specs, out_specs=out_specs, check_vma=False)

time: 155 us -> 153 us (0.987)
  blocking collectives: 96.4 us -> 80.1 us
  starting transfers between devices: 5.97 us -> 14.3 us
  waiting for transfers between devices: 14.3 us -> 17.2 us
  local copies, waits for them, and re-layouts: 8.03 us -> 9.8 us
    all_to_all x4 -> x3, blocking collectives: 83.4 us -> 67 us  [the longest x1 34.8 us: body(): got = lax.all_to_all(sent, SEQ_AXES, 0, 0, tiled=True)]
    all_to_all x1 -> x2, starting transfers between devices: 3.46 us -> 11.2 us  [the longest x1 6.35 us: body(): pieces = lax.all_to_all(pieces, LINE, 0, 0, tiled=True)]
    all_to_all x1 -> x2, waiting for transfers between devices: 8.62 us -> 12.1 us  [the longest x1 12.1 us: body(): mlp = lax.all_to_all(mlp, SHARERS, 0, 0, tiled=True)]
    unnamed x25 -> x31, local copies, waits for them, and re-layouts: 7.99 us -> 9.8 us
    pallas_call x2 -> x3, Pallas kernels: 4.87 us -> 6.29 us  [the longest x1 3.1 us: body(): call(project_kernel, [SMEM, SMEM, ANY, ANY, VMEM, ANY, VMEM, VMEM], jax.S...]
  transfers between devices with their start and end apart: 3 -> 4, of which waited for: 2 -> 2; matrix products, arithmetic and copies ran while one was open for 0% -> 0% of each run, Pallas kernels for 5% -> 5%
where the time goes in v3:
time: 153 us; the launch traced here: 152 us
  blocking collectives  80.1 us (52%)
  waiting for transfers between devices  17.2 us (11%)
  between operations  16.1 us (11%)
  starting transfers between devices  14.3 us (9%)
  Pallas kernels  14 us (9%)
  local copies, waits for them, and re-layouts  9.8 us (6%)
    all_to_all x1, blocking collectives, body(): got = lax.all_to_all(sent, SEQ_AXES, 0, 0, tiled=True)  34.8 us
    all_to_all x1, blocking collectives, body(): back = lax.all_to_all(attended, SEQ_AXES, 0, 0, tiled=True)  16.2 us
    all_to_all x1, blocking collectives, body(): rows = lax.all_to_all(rows, SHARERS, 0, 0, tiled=True)  16.1 us
    all_to_all x1, blocking collectives, body(): partial = lax.all_to_all(partial, 'blk', 0, 0, tiled=True)  13 us
    all_to_all x1, waiting for transfers between devices, body(): mlp = lax.all_to_all(mlp, SHARERS, 0, 0, tiled=True)  12.1 us
    unnamed x31, local copies, waits for them, and re-layouts  9.8 us
    all_to_all x1, starting transfers between devices, body(): pieces = lax.all_to_all(pieces, LINE, 0, 0, tiled=True)  6.35 us
    ppermute x1, waiting for transfers between devices, body(): partner = lax.ppermute(predicted, 'cfg', [(0, 1), (1, 0)])  5.09 us
  transfers between devices with their start and end apart: 4, of which 2 were waited for; matrix products, arithmetic and copies ran while one was open for 0% of the time, Pallas kernels for 5%

profile of v3, /device:TPU:56, one launch (start us, length us, event | category | flops | bytes accessed | tf_op | source)
XLA Modules:
  0.0 151.5 jit_solution(551689829664039368)
XLA Ops:
  7.2 0.9 copy-done.7
  8.1 0.9 copy-done.8
  8.9 0.8 shard_map.150
  9.8 6.4 %all-to-all-start = ((bf16[4,96,384]{2,1,0:T(8,128)(2,1)}), bf16[4,96,384]{2,1,0:T(8,128)(2,1)S(1)}, u32[]{:S(2)}, u32[]{:S(2)}) async-start(bf16[4,96,384]{2,1,0:T(8,128)(2,1)} %shard_map.150), calls=%async_computation | async-start | bytes 589824 | tf_op jit(solution)/shard_map/all_to_all | solution.py:306
  16.8 0.1 pad_add_fusion.where
  16.9 1.5 copy-done.1
  18.4 1.0 copy-done.2
  19.3 0.9 copy-done.4
  20.2 0.7 copy-done.9
  20.9 0.7 copy-done.10
  21.6 0.7 copy-done.11
  22.3 3.1 %shard_map.149 = bf16[32,80,128]{2,1,0:T(8,128)(2,1)S(1)} custom-call(s32[3]{0:T(128)S(1)} %pad_add_fusion.where, s32[1]{0:T(128)S(6)} %copy.18.text, bf16[1,128,1536]{2,1,0:T(8,128)(2,1)S(1)} %copy-done.2, f32[2,8,1536]{2,1,0:T(8,128)S(1)} %copy-done.4, f32[2,64]{1,0:T(2,128)S(1)} %copy-done.11, bf16[3,192,1536]{2,1,0:T(8,128)(2,1)S(1)} %copy-done.1, ...), custom_call_target="tpu_custom_call" | custom-call | flops 10000000 | bytes 4000000 | tf_op jit(solution)/shard_map/pallas_call | solution.py:308
  25.4 0.7 copy-done.13
  26.1 0.0 all-gather.2.cloned.1.call-update
  26.2 0.0 copy-start.3
  26.2 0.0 copy-start.5
  26.2 34.8 %all_to_all.30.got = bf16[32,80,128]{2,1,0:T(8,128)(2,1)S(1)} all-to-all(bf16[32,80,128]{2,1,0:T(8,128)(2,1)S(1)} %shard_map.149), channel_id=1, replica_groups=mesh['cfg'=2,'z'=8,'pair'=2,'side'=2,'blk'=8] {'z','pair','side'}, dimensions={0} | all-to-all | bytes 1310720 | tf_op jit(solution)/shard_map/all_to_all | solution.py:321
  61.0 3.5 %shard_map.151 = bf16[32,32,128]{2,1,0:T(8,128)(2,1)S(1)} custom-call(bf16[32,80,128]{2,1,0:T(8,128)(2,1)S(1)} %all_to_all.30.got), custom_call_target="tpu_custom_call" | custom-call | flops 10000000 | bytes 4000000 | tf_op jit(solution)/shard_map/pallas_call | solution.py:322
  64.4 16.2 %all_to_all.31.got = bf16[32,32,128]{2,1,0:T(8,128)(2,1)S(1)} all-to-all(bf16[32,32,128]{2,1,0:T(8,128)(2,1)S(1)} %shard_map.151), channel_id=1, replica_groups=mesh['cfg'=2,'z'=8,'pair'=2,'side'=2,'blk'=8] {'z','pair','side'}, dimensions={0} | all-to-all | bytes 524288 | tf_op jit(solution)/shard_map/all_to_all | solution.py:323
  80.6 0.9 shard_map.152
  81.5 13.0 %all_to_all.32.got = bf16[8,16,1536]{2,1,0:T(8,128)(2,1)S(1)} all-to-all(bf16[8,16,1536]{2,1,0:T(8,128)(2,1)S(1)} %shard_map.152), channel_id=1, replica_groups=mesh['cfg'=2,'z'=8,'pair'=2,'side'=2,'blk'=8] {'blk'}, dimensions={0} | all-to-all | bytes 786432 | tf_op jit(solution)/shard_map/all_to_all | solution.py:327
  94.5 0.8 shard_map.153
  95.4 16.1 %all_to_all.33.rows = bf16[16,16,1536]{2,1,0:T(8,128)(2,1)S(1)} all-to-all(bf16[16,16,1536]{2,1,0:T(8,128)(2,1)S(1)} %get-tuple-element.9), channel_id=1, replica_groups=mesh['cfg'=2,'z'=8,'pair'=2,'side'=2,'blk'=8] {'side','blk'}, dimensions={0} | all-to-all | bytes 1572864 | tf_op jit(solution)/shard_map/all_to_all | solution.py:333
  111.5 1.7 %copy-done = bf16[32,96,384]{2,1,0:T(8,128)(2,1)S(1)} copy-done((bf16[32,96,384]{2,1,0:T(8,128)(2,1)S(1)}, bf16[32,96,384]{2,1,0:T(8,128)(2,1)}, u32[]{:S(2)}) %copy-start) | copy-done | bytes 2359320
  113.1 2.4 %shard_map.154 = bf16[16,16,1536]{2,1,0:T(8,128)(2,1)} custom-call(bf16[16,16,1536]{2,1,0:T(8,128)(2,1)S(1)} %all_to_all.33.rows, bf16[32,96,384]{2,1,0:T(8,128)(2,1)S(1)} %copy-done), custom_call_target="tpu_custom_call" | custom-call | flops 10000000 | bytes 4000000 | tf_op jit(solution)/shard_map/pallas_call | solution.py:335
  115.5 4.9 %all-to-all-start.5 = ((bf16[16,16,1536]{2,1,0:T(8,128)(2,1)}), bf16[16,16,1536]{2,1,0:T(8,128)(2,1)S(1)}, u32[]{:S(2)}, u32[]{:S(2)}) async-start(bf16[16,16,1536]{2,1,0:T(8,128)(2,1)} %shard_map.154), calls=%async_computation.5 | async-start | bytes 1572864 | tf_op jit(solution)/shard_map/all_to_all | solution.py:341
  120.4 0.2 copy.17.weight
  120.6 12.1 %all-to-all-done.5.got = bf16[16,16,1536]{2,1,0:T(8,128)(2,1)S(1)} async-done(((bf16[16,16,1536]{2,1,0:T(8,128)(2,1)}), bf16[16,16,1536]{2,1,0:T(8,128)(2,1)S(1)}, u32[]{:S(2)}, u32[]{:S(2)}) %all-to-all-start.5) | async-done | bytes 786464 | tf_op jit(solution)/shard_map/all_to_all | solution.py:341
  132.7 1.3 shard_map.155
  134.0 3.0 %collective-permute-start = (f32[16,64]{1,0:T(8,128)S(1)}, f32[16,64]{1,0:T(8,128)S(1)}, u32[]{:S(2)}, u32[]{:S(2)}) collective-permute-start(f32[16,64]{1,0:T(8,128)S(1)} %get-tuple-element.13.mine), channel_id=1, source_target_pairs={{0,256},{256,0},{1,257},{257,1},{2,258},{258,2},{3,259},{259,3},{4... | collective-permute-start | bytes 12296 | tf_op jit(solution)/shard_map/ppermute | solution.py:347
  138.3 5.1 %collective-permute-done.other = f32[16,64]{1,0:T(8,128)S(1)} collective-permute-done((f32[16,64]{1,0:T(8,128)S(1)}, f32[16,64]{1,0:T(8,128)S(1)}, u32[]{:S(2)}, u32[]{:S(2)}) %collective-permute-start) | collective-permute-done | bytes 4128 | tf_op jit(solution)/shard_map/ppermute | solution.py:347
  143.4 1.3 shard_map.156
  (21 shorter events, 0.0 us)
Async XLA Ops:
  7.2 0.9 copy-start.7
  8.0 0.9 copy-start.8
  9.8 15.6 %all-to-all-start = ((bf16[4,96,384]{2,1,0:T(8,128)(2,1)}), bf16[4,96,384]{2,1,0:T(8,128)(2,1)S(1)}, u32[]{:S(2)}, u32[]{:S(2)}) async-start(bf16[4,96,384]{2,1,0:T(8,128)(2,1)} %shard_map.150), calls=%async_computation | async-start | bytes 589824 | tf_op jit(solution)/shard_map/all_to_all | solution.py:306
  16.1 95.3 %all-gather.2.cloned.1.call-start = ((), (), s32[]{:S(2)}) async-start(), calls=%async_computation.6 | async-start | bytes 2654208 | tf_op jit(solution)/shard_map/all_gather | solution.py:320
  16.9 1.5 copy-start.1
  18.4 1.0 copy-start.2
  19.3 0.9 copy-start.4
  20.2 0.7 copy-start.9
  20.9 0.7 copy-start.10
  21.6 0.7 copy-start.11
  22.3 58.3 %copy-start.6 = (bf16[192,1536]{1,0:T(8,128)(2,1)S(1)}, bf16[192,1536]{1,0:T(8,128)(2,1)}, u32[]{:S(2)}) copy-start(bf16[192,1536]{1,0:T(8,128)(2,1)} %weight.2) | copy-start | bytes 1769476
  25.4 0.7 copy-start.13
  26.2 68.4 %copy-start.3 = (bf16[1,128,1536]{2,1,0:T(8,128)(2,1)S(1)}, bf16[1,128,1536]{2,1,0:T(8,128)(2,1)}, u32[]{:S(2)}) copy-start(bf16[1,128,1536]{2,1,0:T(8,128)(2,1)} %tokens.1) | copy-start | bytes 1179652
  26.2 68.4 %copy-start.5 = (f32[2,8,1536]{2,1,0:T(8,128)S(1)}, f32[2,8,1536]{2,1,0:T(8,128)}, u32[]{:S(2)}) copy-start(f32[2,8,1536]{2,1,0:T(8,128)} %mods.3) | copy-start | bytes 294916
  111.5 1.7 %copy-start = (bf16[32,96,384]{2,1,0:T(8,128)(2,1)S(1)}, bf16[32,96,384]{2,1,0:T(8,128)(2,1)}, u32[]{:S(2)}) copy-start(bf16[32,96,384]{2,1,0:T(8,128)(2,1)} %all-gather.2.cloned.1.call-done.weights) | copy-start | bytes 7077892
  113.1 7.2 %copy-start.14 = (bf16[1536,64]{0,1:T(8,128)(2,1)S(1)}, bf16[1536,64]{0,1:T(8,128)(2,1)}, u32[]{:S(2)}) copy-start(bf16[1536,64]{0,1:T(8,128)(2,1)} %param.21) | copy-start | bytes 589828
  115.5 27.9 %copy-start.12 = (f32[16,32]{1,0:T(8,128)S(1)}, f32[16,32]{1,0:T(8,128)}, u32[]{:S(2)}) copy-start(f32[16,32]{1,0:T(8,128)} %latent.1) | copy-start | bytes 6148
  115.5 17.2 %all-to-all-start.5 = ((bf16[16,16,1536]{2,1,0:T(8,128)(2,1)}), bf16[16,16,1536]{2,1,0:T(8,128)(2,1)S(1)}, u32[]{:S(2)}, u32[]{:S(2)}) async-start(bf16[16,16,1536]{2,1,0:T(8,128)(2,1)} %shard_map.154), calls=%async_computation.5 | async-start | bytes 1572864 | tf_op jit(solution)/shard_map/all_to_all | solution.py:341
  134.0 9.4 %collective-permute-start = (f32[16,64]{1,0:T(8,128)S(1)}, f32[16,64]{1,0:T(8,128)S(1)}, u32[]{:S(2)}, u32[]{:S(2)}) collective-permute-start(f32[16,64]{1,0:T(8,128)S(1)} %get-tuple-element.13.mine), channel_id=1, source_target_pairs={{0,256},{256,0},{1,257},{257,1},{2,258},{258,2},{3,259},{259,3},{4... | collective-permute-start | bytes 12296 | tf_op jit(solution)/shard_map/ppermute | solution.py:347
Sparse Core Ops, SparseCore 0:
  26.3 62.3 all-gather.1

commit v4 on v3

--- a/solution.py
+++ b/solution.py
@@ -17,12 +17,13 @@
 UNITS = 384
 SEQ = 32
 BLK = 8
-GROUP = 16
+GROUP = 8
 PIECE = 48
 
 SEQ_AXES = ("z", "pair", "side")
 LINE = ("pair", "side")
-SHARERS = ("side", "blk")
+BLK_AXES = ("x", "core")
+SHARERS = ("side", "x")
 
 VMEM = pl.BlockSpec(memory_space=pltpu.VMEM)
 SMEM = pl.BlockSpec(memory_space=pltpu.SMEM)
@@ -58,15 +59,14 @@
     return lambda row: jnp.where(video, mods[1, row : row + 1, :], mods[0, row : row + 1, :])
 
 
-def project_kernel(where, text, tokens_far, mods_far, gain, qkv_far, positions, table, out, tokens, mods, qkv, arrived):
-    copies = [
-        pltpu.make_async_copy(far, near, arrived.at[i])
-        for i, (far, near) in enumerate(((tokens_far, tokens), (mods_far, mods), (qkv_far, qkv)))
-    ]
+def project_kernel(where, text, tokens_far, mods_far, gain_far, positions_far, table_far, qkv_far, out, *scratch):
+    tokens, mods, gain, positions, table, qkv, arrived = scratch
+    far = (tokens_far, mods_far, gain_far, positions_far, table_far, qkv_far)
+    copies = [pltpu.make_async_copy(a, b, arrived.at[i]) for i, (a, b) in enumerate(zip(far, scratch))]
     for copy in copies:
         copy.start()
-    copies[0].wait()
-    copies[1].wait()
+    for copy in copies[:5]:
+        copy.wait()
     ids = where[1] * TOK + lax.broadcasted_iota(jnp.int32, (TOK, 1), 0)
     video = ids >= text[0]
     pick = picker(mods, video)
@@ -76,7 +76,7 @@
     def project(weight):
         return lax.dot_general(normed, weight, ROWS_BY_ROWS, preferred_element_type=F32)
 
-    copies[2].wait()
+    copies[5].wait()
     heads = project(qkv[0:2].reshape(384, D))
     values_low = project(qkv[2, 0:128, :])
     values_high = project(qkv[2, 64:192, :])
@@ -207,17 +207,23 @@
         out[block] = normed
 
 
-def feed_forward_kernel(rows, weights, out, up, down, up_arrived, down_arrived):
-    up_copy = pltpu.make_async_copy(weights.at[:, 0:PIECE, :], up, up_arrived)
-    down_copy = pltpu.make_async_copy(weights.at[:, PIECE : 2 * PIECE, :], down, down_arrived)
-    up_copy.start()
-    down_copy.start()
+def feed_forward_kernel(rows, own, other, out, up, down, arrived):
+    copies = []
+    for part, weights in enumerate((own, other)):
+        for side, near in enumerate((up, down)):
+            far = weights.at[:, PIECE * side : PIECE * side + PIECE, :]
+            copies.append(pltpu.make_async_copy(far, near.at[part], arrived.at[part, side]))
+    for copy in copies:
+        copy.start()
     block = rows[...].reshape(GROUP * OWN, D)
-    up_copy.wait()
-    hidden = jnp.dot(block, up[...].reshape(D, UNITS), preferred_element_type=F32)
-    activated = jax.nn.gelu(hidden, approximate=True).astype(BF16)
-    down_copy.wait()
-    result = lax.dot_general(activated, down[...].reshape(D, UNITS), ROWS_BY_ROWS, preferred_element_type=F32)
+    result = None
+    for part in range(2):
+        copies[2 * part].wait()
+        hidden = jnp.dot(block, up[part].reshape(D, UNITS), preferred_element_type=F32)
+        activated = jax.nn.gelu(hidden, approximate=True).astype(BF16)
+        copies[2 * part + 1].wait()
+        term = lax.dot_general(activated, down[part].reshape(D, UNITS), ROWS_BY_ROWS, preferred_element_type=F32)
+        result = term if result is None else result + term
     out[...] = result.astype(BF16).reshape(GROUP, OWN, D)
 
 
@@ -266,6 +272,9 @@
     clean = root_now * held - root_rest * guided
     noise = root_rest * held + root_now * guided
     out[...] = jnp.sqrt(alpha_prev) * clean + jnp.sqrt(1.0 - alpha_prev) * noise
+
+
+ALONE = 60
 
 
 def call(kernel, specs, shapes, mib=24, flops=10_000_000, scratch=()):
@@ -295,27 +304,32 @@
     step_index,
     guidance,
 ):
-    where = jnp.stack([lax.axis_index("cfg"), lax.axis_index(SEQ_AXES), lax.axis_index("blk")]).astype(jnp.int32)
+    where = jnp.stack([lax.axis_index("cfg"), lax.axis_index(SEQ_AXES), lax.axis_index(BLK_AXES)]).astype(jnp.int32)
 
     pieces = call(
         pieces_kernel,
         [HBM, HBM],
         jax.ShapeDtypeStruct((4, 2 * PIECE, UNITS), BF16),
+        mib=ALONE,
         scratch=[pltpu.SemaphoreType.DMA((4, 2))],
     )(up_weight, down_weight.T)
     pieces = lax.all_to_all(pieces, LINE, 0, 0, tiled=True)
 
     sent = call(
         project_kernel,
-        [SMEM, SMEM, ANY, ANY, VMEM, ANY, VMEM, VMEM],
+        [SMEM, SMEM] + [HBM] * 6,
         jax.ShapeDtypeStruct((SEQ, 80, 128), BF16),
+        mib=ALONE,
         scratch=[
             pltpu.VMEM((1, TOK, D), BF16),
             pltpu.VMEM((2, 8, D), F32),
+            pltpu.VMEM((2, 64), F32),
+            pltpu.VMEM((3, TOK), jnp.int32),
+            pltpu.VMEM((8, 128), F32),
             pltpu.VMEM((3, 192, D), BF16),
-            pltpu.SemaphoreType.DMA((3,)),
+            pltpu.SemaphoreType.DMA((6,)),
         ],
-    )(where, text_count, tokens_in, modulation, qk_gain, qkv_weight, positions, jnp.asarray(frequencies()))
+    )(where, text_count, tokens_in, modulation, qk_gain, positions, jnp.asarray(frequencies()), qkv_weight)
     sent, pieces = lax.optimization_barrier((sent, pieces))
     weights = lax.all_gather(pieces, "z", axis=0, tiled=True)
     got = lax.all_to_all(sent, SEQ_AXES, 0, 0, tiled=True)
@@ -324,20 +338,23 @@
     blocks = jax.ShapeDtypeStruct((BLK, OWN, D), BF16)
     shared = jax.ShapeDtypeStruct((GROUP, OWN, D), BF16)
     partial = call(out_project_kernel, [VMEM, VMEM], blocks)(back, out_weight)
-    partial = lax.all_to_all(partial, "blk", 0, 0, tiled=True)
+    partial = lax.all_to_all(partial, BLK_AXES, 0, 0, tiled=True)
     after, rows = call(
         after_attention_kernel,
         [SMEM, SMEM, VMEM, VMEM, VMEM],
         (jax.ShapeDtypeStruct((OWN, D), F32), shared),
     )(where, text_count, partial, tokens_in, modulation)
+    rows, weights = lax.optimization_barrier((rows, weights))
     rows = lax.all_to_all(rows, SHARERS, 0, 0, tiled=True)
-    half_weight = pltpu.VMEM((SEQ, PIECE, UNITS), BF16)
+    swapped = lax.ppermute(weights, "core", [(0, 1), (1, 0)])
+    both = pltpu.VMEM((2, SEQ, PIECE, UNITS), BF16)
     mlp = call(
         feed_forward_kernel,
-        [VMEM, HBM],
+        [VMEM, HBM, HBM],
         shared,
-        scratch=[half_weight, half_weight, pltpu.SemaphoreType.DMA, pltpu.SemaphoreType.DMA],
-    )(rows, weights)
+        mib=ALONE,
+        scratch=[both, both, pltpu.SemaphoreType.DMA((2, 2))],
+    )(rows, weights, swapped)
     mlp = lax.all_to_all(mlp, SHARERS, 0, 0, tiled=True)
     hidden_out, predicted = call(
         predict_kernel,
@@ -354,17 +371,17 @@
 
 
 def solution(mesh):
-    devices = mesh.devices.reshape(2, 8, 2, 2, 8)
-    fine = jax.sharding.Mesh(devices, ("cfg", *SEQ_AXES, "blk"))
-    rows = (*SEQ_AXES, "blk")
+    devices = mesh.devices.reshape(2, 8, 2, 2, 4, 2)
+    fine = jax.sharding.Mesh(devices, ("cfg", *SEQ_AXES, *BLK_AXES))
+    rows = (*SEQ_AXES, *BLK_AXES)
     in_specs = (
         P("cfg", SEQ_AXES, None),
         P(),
         P(),
-        P(None, "blk", None),
-        P("blk", None),
-        P(SEQ_AXES, "blk"),
-        P("blk", SEQ_AXES),
+        P(None, BLK_AXES, None),
+        P(BLK_AXES, None),
+        P(SEQ_AXES, BLK_AXES),
+        P(BLK_AXES, SEQ_AXES),
         P(),
         P(rows, "cfg"),
         P(),

time: 153 us -> 144 us (0.941)
  local copies, waits for them, and re-layouts: 9.8 us -> 2.37 us
  Pallas kernels: 14 us -> 19.3 us
  blocking collectives: 80.1 us -> 75.5 us
  waiting for transfers between devices: 17.2 us -> 12.9 us
  starting transfers between devices: 14.3 us -> 16.2 us
    unnamed x31 -> x17, local copies, waits for them, and re-layouts: 9.8 us -> 2.37 us
    all_to_all x1, waiting for transfers between devices: 12.1 us -> 6.56 us  [body(): mlp = lax.all_to_all(mlp, SHARERS, 0, 0, tiled=True)]
    pallas_call x2, Pallas kernels: 5.45 us -> 9.95 us  [the longest x1 5.07 us: body(): call(feed_forward_kernel, [VMEM, HBM, HBM], shared, mib=ALONE, scratch=[b...]
    all_to_all x1, blocking collectives: 16.1 us -> 12 us  [body(): rows = lax.all_to_all(rows, SHARERS, 0, 0, tiled=True)]
    ppermute x0 -> x1, starting transfers between devices: none -> 1.92 us  [body(): swapped = lax.ppermute(weights, 'core', [(0, 1), (1, 0)])]
  transfers between devices with their start and end apart: 4 -> 5, of which waited for: 2 -> 3; matrix products, arithmetic and copies ran while one was open for 0% -> 1% of each run, Pallas kernels for 5% -> 7%
where the time goes in v4:
time: 144 us; the launch traced here: 143 us
  blocking collectives  75.5 us (52%)
  Pallas kernels  19.3 us (13%)
  starting transfers between devices  16.2 us (11%)
  between operations  16.1 us (11%)
  waiting for transfers between devices  12.9 us (9%)
  local copies, waits for them, and re-layouts  2.37 us (2%)
    all_to_all x1, blocking collectives, body(): got = lax.all_to_all(sent, SEQ_AXES, 0, 0, tiled=True)  34.4 us
    all_to_all x1, blocking collectives, body(): back = lax.all_to_all(attended, SEQ_AXES, 0, 0, tiled=True)  16 us
    all_to_all x1, blocking collectives, body(): partial = lax.all_to_all(partial, BLK_AXES, 0, 0, tiled=True)  13 us
    all_to_all x1, blocking collectives, body(): rows = lax.all_to_all(rows, SHARERS, 0, 0, tiled=True)  12 us
    all_to_all x1, waiting for transfers between devices, body(): mlp = lax.all_to_all(mlp, SHARERS, 0, 0, tiled=True)  6.56 us
    all_to_all x1, starting transfers between devices, body(): pieces = lax.all_to_all(pieces, LINE, 0, 0, tiled=True)  6.35 us
    pallas_call x1, Pallas kernels, body(): call(feed_forward_kernel, [VMEM, HBM, HBM], shared, mib=ALONE, scratch=[b...  5.07 us
    ppermute x1, waiting for transfers between devices, body(): partner = lax.ppermute(predicted, 'cfg', [(0, 1), (1, 0)])  4.98 us
  transfers between devices with their start and end apart: 5, of which 3 were waited for; matrix products, arithmetic and copies ran while one was open for 1% of the time, Pallas kernels for 7%

profile of v4, /device:TPU:56, one launch (start us, length us, event | category | flops | bytes accessed | tf_op | source)
XLA Modules:
  0.0 142.9 jit_solution(79008288328090762)
XLA Ops:
  7.2 1.7 %shard_map.150 = bf16[4,96,384]{2,1,0:T(8,128)(2,1)} custom-call(bf16[48,768]{1,0:T(8,128)(2,1)} %up.1, bf16[48,768]{1,0:T(8,128)(2,1)} %bitcast.4), custom_call_target="tpu_custom_call" | custom-call | flops 10000000 | bytes 4000000 | tf_op jit(solution)/shard_map/pallas_call | solution.py:309
  8.8 6.4 %all-to-all-start = ((bf16[4,96,384]{2,1,0:T(8,128)(2,1)}), bf16[4,96,384]{2,1,0:T(8,128)(2,1)S(1)}, u32[]{:S(2)}, u32[]{:S(2)}) async-start(bf16[4,96,384]{2,1,0:T(8,128)(2,1)} %shard_map.150), calls=%async_computation | async-start | bytes 589824 | tf_op jit(solution)/shard_map/all_to_all | solution.py:316
  15.2 0.0 all-gather.2.cloned.1.call-start
  15.9 0.6 pad_add_fusion.where
  16.5 4.9 %shard_map.149 = bf16[32,80,128]{2,1,0:T(8,128)(2,1)} custom-call(s32[3]{0:T(128)} %pad_add_fusion.where, s32[1]{0:T(128)S(6)} %copy.18.text, bf16[1,128,1536]{2,1,0:T(8,128)(2,1)} %tokens.1, f32[2,8,1536]{2,1,0:T(8,128)} %mods.3, f32[2,64]{1,0:T(2,128)} %gain_far.1, s32[3,128]{1,0:T(4,128)} %positions_far.1, f32[8,128]{1,0:T(8,128)} %constant.30.clone.table_far, ...), custom_call_target="tpu_custom_call" | custom-call | flops 10000000 | bytes 4000000 | tf_op jit(solution)/shard_map/pallas_call | solution.py:318
  21.4 1.3 all-to-all-done
  22.7 0.7 copy-done.6
  23.4 0.0 all-gather.2.cloned.1.call-update
  23.4 0.0 copy-start
  23.4 0.0 copy-start.1
  23.5 0.0 copy-start.3
  23.5 34.4 %all_to_all.30.got = bf16[32,80,128]{2,1,0:T(8,128)(2,1)S(1)} all-to-all(bf16[32,80,128]{2,1,0:T(8,128)(2,1)} %shard_map.149), channel_id=1, replica_groups=mesh['cfg'=2,'z'=8,'pair'=2,'side'=2,'x'=4,'core'=2] {'z','pair','side'}, dimensions={0} | all-to-all | bytes 1310720 | tf_op jit(solution)/shard_map/all_to_all | solution.py:335
  57.9 3.5 %shard_map.151 = bf16[32,32,128]{2,1,0:T(8,128)(2,1)S(1)} custom-call(bf16[32,80,128]{2,1,0:T(8,128)(2,1)S(1)} %all_to_all.30.got), custom_call_target="tpu_custom_call" | custom-call | flops 10000000 | bytes 4000000 | tf_op jit(solution)/shard_map/pallas_call | solution.py:336
  61.4 16.0 %all_to_all.31.got = bf16[32,32,128]{2,1,0:T(8,128)(2,1)S(1)} all-to-all(bf16[32,32,128]{2,1,0:T(8,128)(2,1)S(1)} %shard_map.151), channel_id=1, replica_groups=mesh['cfg'=2,'z'=8,'pair'=2,'side'=2,'x'=4,'core'=2] {'z','pair','side'}, dimensions={0} | all-to-all | bytes 524288 | tf_op jit(solution)/shard_map/all_to_all | solution.py:337
  77.4 0.0 copy-done.2
  77.4 0.9 shard_map.152
  78.3 13.0 %all_to_all.32.got = bf16[8,16,1536]{2,1,0:T(8,128)(2,1)S(1)} all-to-all(bf16[8,16,1536]{2,1,0:T(8,128)(2,1)S(1)} %shard_map.152), channel_id=1, replica_groups=mesh['cfg'=2,'z'=8,'pair'=2,'side'=2,'x'=4,'core'=2] {'x','core'}, dimensions={0} | all-to-all | bytes 786432 | tf_op jit(solution)/shard_map/all_to_all | solution.py:341
  91.3 0.8 shard_map.153
  92.1 0.0 all-gather.2.cloned.1.call-done.own
  92.2 1.9 %collective-permute-start = (bf16[32,96,384]{2,1,0:T(8,128)(2,1)}, bf16[32,96,384]{2,1,0:T(8,128)(2,1)S(1)}, u32[]{:S(2)}, u32[]{:S(2)}) collective-permute-start(bf16[32,96,384]{2,1,0:T(8,128)(2,1)} %all-gather.2.cloned.1.call-done.own), channel_id=1, source_target_pairs={{0,1},{1,0},{2,3},{3,2},{4,5},{5,4},{6,7},{7,6},{8,9},{9,8},{10,11... | collective-permute-start | bytes 7077896 | tf_op jit(solution)/shard_map/ppermute | solution.py:349
  94.1 12.0 %all_to_all.33.rows = bf16[8,16,1536]{2,1,0:T(8,128)(2,1)} all-to-all(bf16[8,16,1536]{2,1,0:T(8,128)(2,1)S(1)} %get-tuple-element.13), channel_id=1, replica_groups=mesh['cfg'=2,'z'=8,'pair'=2,'side'=2,'x'=4,'core'=2] {'side','x'}, dimensions={0} | all-to-all | bytes 786432 | tf_op jit(solution)/shard_map/all_to_all | solution.py:348
  106.1 0.0 collective-permute-done.other
  106.1 1.4 copy-done.5
  107.5 5.1 %shard_map.154 = bf16[8,16,1536]{2,1,0:T(8,128)(2,1)} custom-call(bf16[8,16,1536]{2,1,0:T(8,128)(2,1)} %all_to_all.33.rows, bf16[32,96,384]{2,1,0:T(8,128)(2,1)} %all-gather.2.cloned.1.call-done.own, bf16[32,96,384]{2,1,0:T(8,128)(2,1)} %copy-done.5), custom_call_target="tpu_custom_call" | custom-call | flops 10000000 | bytes 4000000 | tf_op jit(solution)/shard_map/pallas_call | solution.py:351
  112.6 0.0 copy-start.4
  112.6 4.7 %all-to-all-start.5 = ((bf16[8,16,1536]{2,1,0:T(8,128)(2,1)}), bf16[8,16,1536]{2,1,0:T(8,128)(2,1)S(1)}, u32[]{:S(2)}, u32[]{:S(2)}) async-start(bf16[8,16,1536]{2,1,0:T(8,128)(2,1)} %shard_map.154), calls=%async_computation.5 | async-start | bytes 786432 | tf_op jit(solution)/shard_map/all_to_all | solution.py:358
  117.4 0.2 copy.17.weight
  117.6 6.6 %all-to-all-done.5.got = bf16[8,16,1536]{2,1,0:T(8,128)(2,1)S(1)} async-done(((bf16[8,16,1536]{2,1,0:T(8,128)(2,1)}), bf16[8,16,1536]{2,1,0:T(8,128)(2,1)S(1)}, u32[]{:S(2)}, u32[]{:S(2)}) %all-to-all-start.5) | async-done | bytes 393248 | tf_op jit(solution)/shard_map/all_to_all | solution.py:358
  124.1 1.2 shard_map.155
  125.4 3.2 %collective-permute-start.1 = (f32[16,64]{1,0:T(8,128)S(1)}, f32[16,64]{1,0:T(8,128)S(1)}, u32[]{:S(2)}, u32[]{:S(2)}) collective-permute-start(f32[16,64]{1,0:T(8,128)S(1)} %get-tuple-element.17.mine), channel_id=1, source_target_pairs={{0,256},{256,0},{1,257},{257,1},{2,258},{258,2},{3,259},{259,3},{4... | collective-permute-start | bytes 12296 | tf_op jit(solution)/shard_map/ppermute | solution.py:364
  129.8 5.0 %collective-permute-done.1.other = f32[16,64]{1,0:T(8,128)S(1)} collective-permute-done((f32[16,64]{1,0:T(8,128)S(1)}, f32[16,64]{1,0:T(8,128)S(1)}, u32[]{:S(2)}, u32[]{:S(2)}) %collective-permute-start.1) | collective-permute-done | bytes 4128 | tf_op jit(solution)/shard_map/ppermute | solution.py:364
  134.8 1.3 shard_map.156
  (9 shorter events, 0.0 us)
Async XLA Ops:
  8.8 13.8 %all-to-all-start = ((bf16[4,96,384]{2,1,0:T(8,128)(2,1)}), bf16[4,96,384]{2,1,0:T(8,128)(2,1)S(1)}, u32[]{:S(2)}, u32[]{:S(2)}) async-start(bf16[4,96,384]{2,1,0:T(8,128)(2,1)} %shard_map.150), calls=%async_computation | async-start | bytes 589824 | tf_op jit(solution)/shard_map/all_to_all | solution.py:316
  15.2 76.9 %all-gather.2.cloned.1.call-start = ((), (), s32[]{:S(2)}) async-start(), calls=%async_computation.6 | async-start | bytes 2654208 | tf_op jit(solution)/shard_map/all_gather | solution.py:334
  16.5 60.9 %copy-start.2 = (bf16[192,1536]{1,0:T(8,128)(2,1)S(1)}, bf16[192,1536]{1,0:T(8,128)(2,1)}, u32[]{:S(2)}) copy-start(bf16[192,1536]{1,0:T(8,128)(2,1)} %weight.2) | copy-start | bytes 1769476
  22.7 0.7 copy-start.6
  23.4 67.9 %copy-start = (bf16[1,128,1536]{2,1,0:T(8,128)(2,1)S(1)}, bf16[1,128,1536]{2,1,0:T(8,128)(2,1)}, u32[]{:S(2)}) copy-start(bf16[1,128,1536]{2,1,0:T(8,128)(2,1)} %tokens.1) | copy-start | bytes 1179652
  23.4 67.9 %copy-start.1 = (f32[2,8,1536]{2,1,0:T(8,128)S(1)}, f32[2,8,1536]{2,1,0:T(8,128)}, u32[]{:S(2)}) copy-start(f32[2,8,1536]{2,1,0:T(8,128)} %mods.3) | copy-start | bytes 294916
  23.5 67.9 %copy-start.3 = (s32[3]{0:T(128)S(1)}, s32[3]{0:T(128)}, u32[]{:S(2)}) copy-start(s32[3]{0:T(128)} %pad_add_fusion.where) | copy-start | bytes 40
  92.2 14.0 %collective-permute-start = (bf16[32,96,384]{2,1,0:T(8,128)(2,1)}, bf16[32,96,384]{2,1,0:T(8,128)(2,1)S(1)}, u32[]{:S(2)}, u32[]{:S(2)}) collective-permute-start(bf16[32,96,384]{2,1,0:T(8,128)(2,1)} %all-gather.2.cloned.1.call-done.own), channel_id=1, source_target_pairs={{0,1},{1,0},{2,3},{3,2},{4,5},{5,4},{6,7},{7,6},{8,9},{9,8},{10,11... | collective-permute-start | bytes 7077896 | tf_op jit(solution)/shard_map/ppermute | solution.py:349
  106.1 11.2 %copy-start.7 = (bf16[1536,64]{0,1:T(8,128)(2,1)S(1)}, bf16[1536,64]{0,1:T(8,128)(2,1)}, u32[]{:S(2)}) copy-start(bf16[1536,64]{0,1:T(8,128)(2,1)} %param.21) | copy-start | bytes 589828
  106.1 1.4 copy-start.5
  112.6 22.2 %copy-start.4 = (f32[16,32]{1,0:T(8,128)S(1)}, f32[16,32]{1,0:T(8,128)}, u32[]{:S(2)}) copy-start(f32[16,32]{1,0:T(8,128)} %latent.1) | copy-start | bytes 6148
  112.6 11.5 %all-to-all-start.5 = ((bf16[8,16,1536]{2,1,0:T(8,128)(2,1)}), bf16[8,16,1536]{2,1,0:T(8,128)(2,1)S(1)}, u32[]{:S(2)}, u32[]{:S(2)}) async-start(bf16[8,16,1536]{2,1,0:T(8,128)(2,1)} %shard_map.154), calls=%async_computation.5 | async-start | bytes 786432 | tf_op jit(solution)/shard_map/all_to_all | solution.py:358
  125.4 9.4 %collective-permute-start.1 = (f32[16,64]{1,0:T(8,128)S(1)}, f32[16,64]{1,0:T(8,128)S(1)}, u32[]{:S(2)}, u32[]{:S(2)}) collective-permute-start(f32[16,64]{1,0:T(8,128)S(1)} %get-tuple-element.17.mine), channel_id=1, source_target_pairs={{0,256},{256,0},{1,257},{257,1},{2,258},{258,2},{3,259},{259,3},{4... | collective-permute-start | bytes 12296 | tf_op jit(solution)/shard_map/ppermute | solution.py:364
Sparse Core Ops, SparseCore 0:
  23.5 62.0 all-gather.1

commit v5 on v4

--- a/solution.py
+++ b/solution.py
@@ -59,15 +59,17 @@
     return lambda row: jnp.where(video, mods[1, row : row + 1, :], mods[0, row : row + 1, :])
 
 
-def project_kernel(where, text, tokens_far, mods_far, gain_far, positions_far, table_far, qkv_far, out, *scratch):
+def project_kernel(place, text, step, tokens_far, mods_far, gain_far, positions_far, table_far, qkv_far, out, alphas, *scratch):
     tokens, mods, gain, positions, table, qkv, arrived = scratch
     far = (tokens_far, mods_far, gain_far, positions_far, table_far, qkv_far)
     copies = [pltpu.make_async_copy(a, b, arrived.at[i]) for i, (a, b) in enumerate(zip(far, scratch))]
     for copy in copies:
         copy.start()
+    row = lax.broadcasted_iota(jnp.int32, (8, 128), 0)
+    alphas[...] = jnp.where(row == 0, alpha_bar(step[0]), alpha_bar(step[0] - STRIDE))
     for copy in copies[:5]:
         copy.wait()
-    ids = where[1] * TOK + lax.broadcasted_iota(jnp.int32, (TOK, 1), 0)
+    ids = place[0] * TOK + lax.broadcasted_iota(jnp.int32, (TOK, 1), 0)
     video = ids >= text[0]
     pick = picker(mods, video)
     residual = tokens[0].astype(F32)
@@ -185,8 +187,8 @@
     out[...] = total.astype(BF16).reshape(BLK, OWN, D)
 
 
-def own_video(where, text):
-    ids = where[1] * TOK + where[2] * OWN + lax.broadcasted_iota(jnp.int32, (OWN, 1), 0)
+def own_video(place, part, text):
+    ids = place[0] * TOK + part[0] * OWN + lax.broadcasted_iota(jnp.int32, (OWN, 1), 0)
     return ids >= text[0]
 
 
@@ -197,9 +199,9 @@
     return total
 
 
-def after_attention_kernel(where, text, got, tokens, mods, after, out):
-    pick = picker(mods, own_video(where, text))
-    residual = tokens[0, pl.ds(pl.multiple_of(where[2] * OWN, OWN), OWN), :].astype(F32)
+def after_attention_kernel(place, part, text, got, tokens, mods, after, out):
+    pick = picker(mods, own_video(place, part, text))
+    residual = tokens[0, pl.ds(pl.multiple_of(part[0] * OWN, OWN), OWN), :].astype(F32)
     summed = residual + pick(2) * sum_blocks(got)
     after[...] = summed
     normed = (layer_norm(summed, 1e-05) * (1.0 + pick(4)) + pick(3)).astype(BF16)
@@ -207,21 +209,24 @@
         out[block] = normed
 
 
-def feed_forward_kernel(rows, own, other, out, up, down, arrived):
-    copies = []
-    for part, weights in enumerate((own, other)):
-        for side, near in enumerate((up, down)):
-            far = weights.at[:, PIECE * side : PIECE * side + PIECE, :]
-            copies.append(pltpu.make_async_copy(far, near.at[part], arrived.at[part, side]))
-    for copy in copies:
-        copy.start()
+def feed_forward_kernel(rows, weights, out, up, down, arrived):
+    def fetch(part, side):
+        far = weights.at[pl.ds(SEQ * part, SEQ), PIECE * side : PIECE * side + PIECE, :]
+        return pltpu.make_async_copy(far, (up, down)[side].at[part], arrived.at[part, side])
+
+    fetch(0, 0).start()
+    fetch(0, 1).start()
     block = rows[...].reshape(GROUP * OWN, D)
     result = None
     for part in range(2):
-        copies[2 * part].wait()
+        fetch(part, 0).wait()
+        if part == 0:
+            fetch(1, 0).start()
         hidden = jnp.dot(block, up[part].reshape(D, UNITS), preferred_element_type=F32)
         activated = jax.nn.gelu(hidden, approximate=True).astype(BF16)
-        copies[2 * part + 1].wait()
+        fetch(part, 1).wait()
+        if part == 0:
+            fetch(1, 1).start()
         term = lax.dot_general(activated, down[part].reshape(D, UNITS), ROWS_BY_ROWS, preferred_element_type=F32)
         result = term if result is None else result + term
     out[...] = result.astype(BF16).reshape(GROUP, OWN, D)
@@ -240,28 +245,26 @@
         copy.wait()
 
 
-def predict_kernel(where, text, got, after, mods, weight, hidden_out, predicted):
-    pick = picker(mods, own_video(where, text))
+def predict_kernel(place, part, text, got, after, mods, weight, hidden_out, predicted):
+    pick = picker(mods, own_video(place, part, text))
     after_mlp = after[...] + pick(5) * sum_blocks(got)
     hidden_out[0] = after_mlp.astype(BF16)
     normed = (layer_norm(after_mlp, 1e-05) * (1.0 + pick(7)) + pick(6)).astype(BF16)
     predicted[...] = jnp.dot(normed, weight[...], preferred_element_type=F32)
 
 
-def step_kernel(where, step, guidance, mine, other, latent, out):
+def alpha_bar(last):
     row = lax.broadcasted_iota(jnp.int32, (8, 128), 0)
     steps = row * 128 + lax.broadcasted_iota(jnp.int32, (8, 128), 1)
     low, high = math.sqrt(0.00085), math.sqrt(0.012)
     root_beta = low + steps.astype(F32) / 999.0 * (high - low)
-    logs = jnp.log1p(-jnp.where(steps < 1000, root_beta * root_beta, 0.0))
-
-    def alpha_bar(last):
-        kept = jnp.where(steps <= last, logs, 0.0)
-        return jnp.exp(jnp.sum(jnp.sum(kept, 1, keepdims=True), 0, keepdims=True))
-
-    alpha_now = alpha_bar(step[0])
-    alpha_prev = alpha_bar(step[0] - STRIDE)
-    is_cond = where[0] == 0
+    kept = jnp.where(steps <= last, jnp.log1p(-jnp.where(steps < 1000, root_beta * root_beta, 0.0)), 0.0)
+    return jnp.exp(jnp.sum(jnp.sum(kept, 1, keepdims=True), 0, keepdims=True))
+
+
+def step_kernel(branch, guidance, alphas, mine, other, latent, out):
+    alpha_now, alpha_prev = alphas[0:1, 0:1], alphas[1:2, 0:1]
+    is_cond = branch[0] == 0
     own, partner = mine[...], other[...]
     cond = jnp.where(is_cond, own, partner)
     uncond = jnp.where(is_cond, partner, own)
@@ -277,15 +280,15 @@
 ALONE = 60
 
 
-def call(kernel, specs, shapes, mib=24, flops=10_000_000, scratch=()):
+def call(kernel, specs, shapes, mib=24, result=VMEM, scratch=()):
     return pl.pallas_call(
         kernel,
         out_shape=shapes,
         in_specs=specs,
-        out_specs=jax.tree.map(lambda _: VMEM, shapes),
+        out_specs=jax.tree.map(lambda _: result, shapes),
         scratch_shapes=scratch,
         compiler_params=pltpu.CompilerParams(vmem_limit_bytes=mib * 2**20),
-        cost_estimate=pl.CostEstimate(flops=flops, bytes_accessed=4_000_000, transcendentals=0),
+        cost_estimate=pl.CostEstimate(flops=10_000_000, bytes_accessed=4_000_000, transcendentals=0),
     )
 
 
@@ -304,21 +307,22 @@
     step_index,
     guidance,
 ):
-    where = jnp.stack([lax.axis_index("cfg"), lax.axis_index(SEQ_AXES), lax.axis_index(BLK_AXES)]).astype(jnp.int32)
+    branch, place, part = (lax.axis_index(axes).reshape(1) for axes in ("cfg", SEQ_AXES, BLK_AXES))
 
     pieces = call(
         pieces_kernel,
         [HBM, HBM],
         jax.ShapeDtypeStruct((4, 2 * PIECE, UNITS), BF16),
         mib=ALONE,
+        result=HBM,
         scratch=[pltpu.SemaphoreType.DMA((4, 2))],
     )(up_weight, down_weight.T)
     pieces = lax.all_to_all(pieces, LINE, 0, 0, tiled=True)
 
-    sent = call(
+    sent, alphas = call(
         project_kernel,
-        [SMEM, SMEM] + [HBM] * 6,
-        jax.ShapeDtypeStruct((SEQ, 80, 128), BF16),
+        [SMEM, SMEM, SMEM] + [HBM] * 6,
+        (jax.ShapeDtypeStruct((SEQ, 80, 128), BF16), jax.ShapeDtypeStruct((8, 128), F32)),
         mib=ALONE,
         scratch=[
             pltpu.VMEM((1, TOK, D), BF16),
@@ -329,9 +333,10 @@
             pltpu.VMEM((3, 192, D), BF16),
             pltpu.SemaphoreType.DMA((6,)),
         ],
-    )(where, text_count, tokens_in, modulation, qk_gain, positions, jnp.asarray(frequencies()), qkv_weight)
+    )(place, text_count, step_index, tokens_in, modulation, qk_gain, positions, jnp.asarray(frequencies()), qkv_weight)
     sent, pieces = lax.optimization_barrier((sent, pieces))
     weights = lax.all_gather(pieces, "z", axis=0, tiled=True)
+    weights = lax.all_gather(weights, "core", axis=0, tiled=True)
     got = lax.all_to_all(sent, SEQ_AXES, 0, 0, tiled=True)
     attended = call(attend_kernel, [VMEM], jax.ShapeDtypeStruct((SEQ, 32, 128), BF16))(got)
     back = lax.all_to_all(attended, SEQ_AXES, 0, 0, tiled=True)
@@ -341,32 +346,30 @@
     partial = lax.all_to_all(partial, BLK_AXES, 0, 0, tiled=True)
     after, rows = call(
         after_attention_kernel,
-        [SMEM, SMEM, VMEM, VMEM, VMEM],
+        [SMEM, SMEM, SMEM, VMEM, VMEM, VMEM],
         (jax.ShapeDtypeStruct((OWN, D), F32), shared),
-    )(where, text_count, partial, tokens_in, modulation)
-    rows, weights = lax.optimization_barrier((rows, weights))
+    )(place, part, text_count, partial, tokens_in, modulation)
     rows = lax.all_to_all(rows, SHARERS, 0, 0, tiled=True)
-    swapped = lax.ppermute(weights, "core", [(0, 1), (1, 0)])
     both = pltpu.VMEM((2, SEQ, PIECE, UNITS), BF16)
     mlp = call(
         feed_forward_kernel,
-        [VMEM, HBM, HBM],
+        [VMEM, HBM],
         shared,
         mib=ALONE,
         scratch=[both, both, pltpu.SemaphoreType.DMA((2, 2))],
-    )(rows, weights, swapped)
+    )(rows, weights)
     mlp = lax.all_to_all(mlp, SHARERS, 0, 0, tiled=True)
     hidden_out, predicted = call(
         predict_kernel,
-        [SMEM, SMEM, VMEM, VMEM, VMEM, VMEM],
+        [SMEM, SMEM, SMEM, VMEM, VMEM, VMEM, VMEM],
         (jax.ShapeDtypeStruct((1, OWN, D), BF16), jax.ShapeDtypeStruct((OWN, 64), F32)),
-    )(where, text_count, mlp, after, modulation, proj_weight)
+    )(place, part, text_count, mlp, after, modulation, proj_weight)
     partner = lax.ppermute(predicted, "cfg", [(0, 1), (1, 0)])
     latent_prev = call(
         step_kernel,
-        [SMEM, SMEM, SMEM, VMEM, VMEM, VMEM],
+        [SMEM, SMEM, VMEM, VMEM, VMEM, VMEM],
         jax.ShapeDtypeStruct((OWN, 32), F32),
-    )(where, step_index, guidance, predicted, partner, latent)
+    )(branch, guidance, alphas, predicted, partner, latent)
     return (hidden_out, latent_prev)
 
 

time: 144 us -> 187 us (1.30)
  waiting for transfers between devices: 12.9 us -> 69.8 us
  blocking collectives: 75.5 us -> 50.6 us
  Pallas kernels: 19.3 us -> 26.6 us
  starting transfers between devices: 16.2 us -> 20.5 us
    all_gather x1, waiting for transfers between devices: 0.02 us -> 48.7 us  [body(): weights = lax.all_gather(pieces, 'z', axis=0, tiled=True)]
    all_to_all x1 -> x0, blocking collectives: 13 us -> none  [body(): partial = lax.all_to_all(partial, BLK_AXES, 0, 0, tiled=True)]
    all_to_all x1, blocking collectives: 34.4 us -> 23.6 us  [body(): got = lax.all_to_all(sent, SEQ_AXES, 0, 0, tiled=True)]
    all_to_all x0 -> x1, waiting for transfers between devices: none -> 8.94 us  [body(): partial = lax.all_to_all(partial, BLK_AXES, 0, 0, tiled=True)]
    pallas_call x1, Pallas kernels: 1.67 us -> 10.1 us  [body(): call(pieces_kernel, [HBM, HBM], jax.ShapeDtypeStruct((4, 2 * PIECE, UNITS...]
    all_to_all x0 -> x1, starting transfers between devices: none -> 4.23 us  [body(): partial = lax.all_to_all(partial, BLK_AXES, 0, 0, tiled=True)]
    ppermute x1, starting transfers between devices: 3.16 us -> 5.09 us  [body(): partner = lax.ppermute(predicted, 'cfg', [(0, 1), (1, 0)])]
    ppermute x1 -> x0, starting transfers between devices: 1.92 us -> none  [body(): swapped = lax.ppermute(weights, 'core', [(0, 1), (1, 0)])]
  transfers between devices with their start and end apart: 5 -> 6, of which waited for: 3 -> 5; matrix products, arithmetic and copies ran while one was open for 1% -> 0% of each run, Pallas kernels for 7% -> 5%
where the time goes in v5:
time: 187 us; the launch traced here: 185 us
  waiting for transfers between devices  69.8 us (37%)
  blocking collectives  50.6 us (27%)
  Pallas kernels  26.6 us (14%)
  starting transfers between devices  20.5 us (11%)
  between operations  16.1 us (9%)
    all_gather x1, waiting for transfers between devices, body(): weights = lax.all_gather(pieces, 'z', axis=0, tiled=True)  48.7 us
    all_to_all x1, blocking collectives, body(): got = lax.all_to_all(sent, SEQ_AXES, 0, 0, tiled=True)  23.6 us
    all_to_all x1, blocking collectives, body(): back = lax.all_to_all(attended, SEQ_AXES, 0, 0, tiled=True)  16.1 us
    all_to_all x1, blocking collectives, body(): rows = lax.all_to_all(rows, SHARERS, 0, 0, tiled=True)  10.9 us
    pallas_call x1, Pallas kernels, body(): call(pieces_kernel, [HBM, HBM], jax.ShapeDtypeStruct((4, 2 * PIECE, UNITS...  10.1 us
    all_to_all x1, waiting for transfers between devices, body(): partial = lax.all_to_all(partial, BLK_AXES, 0, 0, tiled=True)  8.94 us
    all_to_all x1, starting transfers between devices, body(): pieces = lax.all_to_all(pieces, LINE, 0, 0, tiled=True)  6.35 us
    all_to_all x1, waiting for transfers between devices, body(): mlp = lax.all_to_all(mlp, SHARERS, 0, 0, tiled=True)  6.32 us
  transfers between devices with their start and end apart: 6, of which 5 were waited for; matrix products, arithmetic and copies ran while one was open for 0% of the time, Pallas kernels for 5%

profile of v5, /device:TPU:56, one launch (start us, length us, event | category | flops | bytes accessed | tf_op | source)
XLA Modules:
  0.0 184.5 jit_solution(14217367781160686882)
XLA Ops:
  7.2 10.1 %shard_map.150 = bf16[4,96,384]{2,1,0:T(8,128)(2,1)} custom-call(bf16[48,768]{1,0:T(8,128)(2,1)} %up.1, bf16[48,768]{1,0:T(8,128)(2,1)} %bitcast.4), custom_call_target="tpu_custom_call" | custom-call | flops 10000000 | bytes 4000000 | tf_op jit(solution)/shard_map/pallas_call | solution.py:312
  17.3 6.4 %all-to-all-start = ((bf16[4,96,384]{2,1,0:T(8,128)(2,1)}), bf16[4,96,384]{2,1,0:T(8,128)(2,1)S(1)}, u32[]{:S(2)}, u32[]{:S(2)}) async-start(bf16[4,96,384]{2,1,0:T(8,128)(2,1)} %shard_map.150), calls=%async_computation | async-start | bytes 589824 | tf_op jit(solution)/shard_map/all_to_all | solution.py:320
  23.6 0.0 all-gather.3.cloned.1.call-start
  24.9 4.1 %shard_map.149 = (bf16[32,80,128]{2,1,0:T(8,128)(2,1)}, f32[8,128]{1,0:T(8,128)}) custom-call(s32[1]{0:T(128)} %bitcast.place, s32[1]{0:T(128)S(6)} %copy.18.text, s32[1]{0:T(128)S(6)} %copy.19.step, bf16[1,128,1536]{2,1,0:T(8,128)(2,1)} %tokens.1, f32[2,8,1536]{2,1,0:T(8,128)} %mods.3, f32[2,64]{1,0:T(2,128)} %gain_far.1, s32[3,128]{1,0:T(4,128)} %positions_far.1, ...), custom_call_target="tpu_custom_call" | custom-call | flops 10000000 | bytes 4000000 | tf_op jit(solution)/shard_map/pallas_call | solution.py:322
  29.0 0.0 copy-start.6
  29.0 2.1 %all-to-all-done = bf16[4,96,384]{2,1,0:T(8,128)(2,1)S(1)} async-done(((bf16[4,96,384]{2,1,0:T(8,128)(2,1)}), bf16[4,96,384]{2,1,0:T(8,128)(2,1)S(1)}, u32[]{:S(2)}, u32[]{:S(2)}) %all-to-all-start) | async-done | bytes 294944 | tf_op jit(solution)/shard_map/all_to_all | solution.py:320
  31.1 0.7 copy-done.5
  31.8 0.0 all-gather.3.cloned.1.call-update
  31.9 0.0 all-gather.5.cloned.1.call-start
  31.9 48.7 %all-gather.3.cloned.1.call-done = bf16[32,96,384]{2,1,0:T(8,128)(2,1)} async-done(((bf16[4,96,384]{2,1,0:T(8,128)(2,1)}), bf16[32,96,384]{2,1,0:T(8,128)(2,1)}) %all-gather.3.cloned.1.call-update) | async-done | bytes 2359312 | tf_op jit(solution)/shard_map/all_gather | solution.py:338
  80.7 0.0 all-gather.5.cloned.1.call-update
  80.7 0.0 copy-done.6
  80.7 0.0 copy-start
  80.7 0.0 copy-start.1
  80.7 23.6 %all_to_all.30.got = bf16[32,80,128]{2,1,0:T(8,128)(2,1)S(1)} all-to-all(bf16[32,80,128]{2,1,0:T(8,128)(2,1)S(1)} %copy-done.6), channel_id=1, replica_groups=mesh['cfg'=2,'z'=8,'pair'=2,'side'=2,'x'=4,'core'=2] {'z','pair','side'}, dimensions={0} | all-to-all | bytes 1310720 | tf_op jit(solution)/shard_map/all_to_all | solution.py:340
  104.3 3.5 %shard_map.151 = bf16[32,32,128]{2,1,0:T(8,128)(2,1)S(1)} custom-call(bf16[32,80,128]{2,1,0:T(8,128)(2,1)S(1)} %all_to_all.30.got), custom_call_target="tpu_custom_call" | custom-call | flops 10000000 | bytes 4000000 | tf_op jit(solution)/shard_map/pallas_call | solution.py:341
  107.7 16.1 %all_to_all.31.got = bf16[32,32,128]{2,1,0:T(8,128)(2,1)S(1)} all-to-all(bf16[32,32,128]{2,1,0:T(8,128)(2,1)S(1)} %shard_map.151), channel_id=1, replica_groups=mesh['cfg'=2,'z'=8,'pair'=2,'side'=2,'x'=4,'core'=2] {'z','pair','side'}, dimensions={0} | all-to-all | bytes 524288 | tf_op jit(solution)/shard_map/all_to_all | solution.py:342
  123.8 1.6 shard_map.152
  125.4 4.2 %all-to-all-start.3 = ((bf16[8,16,1536]{2,1,0:T(8,128)(2,1)}), bf16[8,16,1536]{2,1,0:T(8,128)(2,1)S(1)}, u32[]{:S(2)}, u32[]{:S(2)}) async-start(bf16[8,16,1536]{2,1,0:T(8,128)(2,1)} %shard_map.152), calls=%async_computation.3 | async-start | bytes 786432 | tf_op jit(solution)/shard_map/all_to_all | solution.py:346
  129.7 8.9 %all-to-all-done.3.got = bf16[8,16,1536]{2,1,0:T(8,128)(2,1)S(1)} async-done(((bf16[8,16,1536]{2,1,0:T(8,128)(2,1)}), bf16[8,16,1536]{2,1,0:T(8,128)(2,1)S(1)}, u32[]{:S(2)}, u32[]{:S(2)}) %all-to-all-start.3) | async-done | bytes 393248 | tf_op jit(solution)/shard_map/all_to_all | solution.py:346
  138.6 0.3 shard_map.153
  138.9 10.9 %all_to_all.32.rows = bf16[8,16,1536]{2,1,0:T(8,128)(2,1)} all-to-all(bf16[8,16,1536]{2,1,0:T(8,128)(2,1)S(1)} %get-tuple-element.12), channel_id=1, replica_groups=mesh['cfg'=2,'z'=8,'pair'=2,'side'=2,'x'=4,'core'=2] {'side','x'}, dimensions={0} | all-to-all | bytes 786432 | tf_op jit(solution)/shard_map/all_to_all | solution.py:352
  149.9 5.7 %shard_map.154 = bf16[8,16,1536]{2,1,0:T(8,128)(2,1)} custom-call(bf16[8,16,1536]{2,1,0:T(8,128)(2,1)} %all_to_all.32.rows, bf16[64,96,384]{2,1,0:T(8,128)(2,1)} %all-gather.5.cloned.1.call-done.weights), custom_call_target="tpu_custom_call" | custom-call | flops 10000000 | bytes 4000000 | tf_op jit(solution)/shard_map/pallas_call | solution.py:354
  155.6 0.0 copy-start.3
  155.6 0.0 copy-start.4
  155.6 4.7 %all-to-all-start.5 = ((bf16[8,16,1536]{2,1,0:T(8,128)(2,1)}), bf16[8,16,1536]{2,1,0:T(8,128)(2,1)S(1)}, u32[]{:S(2)}, u32[]{:S(2)}) async-start(bf16[8,16,1536]{2,1,0:T(8,128)(2,1)} %shard_map.154), calls=%async_computation.5 | async-start | bytes 786432 | tf_op jit(solution)/shard_map/all_to_all | solution.py:361
  160.3 0.2 copy.17.weight
  160.6 6.3 %all-to-all-done.5.got = bf16[8,16,1536]{2,1,0:T(8,128)(2,1)S(1)} async-done(((bf16[8,16,1536]{2,1,0:T(8,128)(2,1)}), bf16[8,16,1536]{2,1,0:T(8,128)(2,1)S(1)}, u32[]{:S(2)}, u32[]{:S(2)}) %all-to-all-start.5) | async-done | bytes 393248 | tf_op jit(solution)/shard_map/all_to_all | solution.py:361
  166.9 0.7 shard_map.155
  167.6 5.1 %collective-permute-start = (f32[16,64]{1,0:T(8,128)S(1)}, f32[16,64]{1,0:T(8,128)S(1)}, u32[]{:S(2)}, u32[]{:S(2)}) collective-permute-start(f32[16,64]{1,0:T(8,128)S(1)} %get-tuple-element.17.mine), channel_id=1, source_target_pairs={{0,256},{256,0},{1,257},{257,1},{2,258},{258,2},{3,259},{259,3},{4... | collective-permute-start | bytes 12296 | tf_op jit(solution)/shard_map/ppermute | solution.py:367
  173.3 3.7 %collective-permute-done.other = f32[16,64]{1,0:T(8,128)S(1)} collective-permute-done((f32[16,64]{1,0:T(8,128)S(1)}, f32[16,64]{1,0:T(8,128)S(1)}, u32[]{:S(2)}, u32[]{:S(2)}) %collective-permute-start) | collective-permute-done | bytes 4128 | tf_op jit(solution)/shard_map/ppermute | solution.py:367
  177.0 0.7 shard_map.156
  (10 shorter events, 0.0 us)
Async XLA Ops:
  17.3 13.8 %all-to-all-start = ((bf16[4,96,384]{2,1,0:T(8,128)(2,1)}), bf16[4,96,384]{2,1,0:T(8,128)(2,1)S(1)}, u32[]{:S(2)}, u32[]{:S(2)}) async-start(bf16[4,96,384]{2,1,0:T(8,128)(2,1)} %shard_map.150), calls=%async_computation | async-start | bytes 589824 | tf_op jit(solution)/shard_map/all_to_all | solution.py:320
  23.6 57.0 %all-gather.3.cloned.1.call-start = ((), (), s32[]{:S(2)}) async-start(), calls=%async_computation.6 | async-start | bytes 2654208 | tf_op jit(solution)/shard_map/all_gather | solution.py:338
  29.0 51.7 %copy-start.6 = (bf16[32,80,128]{2,1,0:T(8,128)(2,1)S(1)}, bf16[32,80,128]{2,1,0:T(8,128)(2,1)}, u32[]{:S(2)}) copy-start(bf16[32,80,128]{2,1,0:T(8,128)(2,1)} %get-tuple-element.11) | copy-start | bytes 1966084
  31.1 0.7 copy-start.5
  31.9 118.0 %all-gather.5.cloned.1.call-start = ((), (), s32[]{:S(2)}) async-start(), calls=%async_computation.7 | async-start | bytes 7077888 | tf_op jit(solution)/shard_map/all_gather | solution.py:339
  80.7 43.2 %copy-start.2 = (bf16[192,1536]{1,0:T(8,128)(2,1)S(1)}, bf16[192,1536]{1,0:T(8,128)(2,1)}, u32[]{:S(2)}) copy-start(bf16[192,1536]{1,0:T(8,128)(2,1)} %weight.2) | copy-start | bytes 1769476
  80.7 57.9 %copy-start = (bf16[1,128,1536]{2,1,0:T(8,128)(2,1)S(1)}, bf16[1,128,1536]{2,1,0:T(8,128)(2,1)}, u32[]{:S(2)}) copy-start(bf16[1,128,1536]{2,1,0:T(8,128)(2,1)} %tokens.1) | copy-start | bytes 1179652
  80.7 57.9 %copy-start.1 = (f32[2,8,1536]{2,1,0:T(8,128)S(1)}, f32[2,8,1536]{2,1,0:T(8,128)}, u32[]{:S(2)}) copy-start(f32[2,8,1536]{2,1,0:T(8,128)} %mods.3) | copy-start | bytes 294916
  125.4 13.2 %all-to-all-start.3 = ((bf16[8,16,1536]{2,1,0:T(8,128)(2,1)}), bf16[8,16,1536]{2,1,0:T(8,128)(2,1)S(1)}, u32[]{:S(2)}, u32[]{:S(2)}) async-start(bf16[8,16,1536]{2,1,0:T(8,128)(2,1)} %shard_map.152), calls=%async_computation.3 | async-start | bytes 786432 | tf_op jit(solution)/shard_map/all_to_all | solution.py:346
  149.8 10.5 %copy-start.7 = (bf16[1536,64]{0,1:T(8,128)(2,1)S(1)}, bf16[1536,64]{0,1:T(8,128)(2,1)}, u32[]{:S(2)}) copy-start(bf16[1536,64]{0,1:T(8,128)(2,1)} %param.21) | copy-start | bytes 589828
  155.6 21.4 %copy-start.3 = (f32[16,32]{1,0:T(8,128)S(1)}, f32[16,32]{1,0:T(8,128)}, u32[]{:S(2)}) copy-start(f32[16,32]{1,0:T(8,128)} %latent.1) | copy-start | bytes 6148
  155.6 21.4 %copy-start.4 = (f32[8,128]{1,0:T(8,128)S(1)}, f32[8,128]{1,0:T(8,128)}, u32[]{:S(2)}) copy-start(f32[8,128]{1,0:T(8,128)} %get-tuple-element.16.alphas) | copy-start | bytes 12292
  155.6 11.3 %all-to-all-start.5 = ((bf16[8,16,1536]{2,1,0:T(8,128)(2,1)}), bf16[8,16,1536]{2,1,0:T(8,128)(2,1)S(1)}, u32[]{:S(2)}, u32[]{:S(2)}) async-start(bf16[8,16,1536]{2,1,0:T(8,128)(2,1)} %shard_map.154), calls=%async_computation.5 | async-start | bytes 786432 | tf_op jit(solution)/shard_map/all_to_all | solution.py:361
  167.6 9.4 %collective-permute-start = (f32[16,64]{1,0:T(8,128)S(1)}, f32[16,64]{1,0:T(8,128)S(1)}, u32[]{:S(2)}, u32[]{:S(2)}) collective-permute-start(f32[16,64]{1,0:T(8,128)S(1)} %get-tuple-element.17.mine), channel_id=1, source_target_pairs={{0,256},{256,0},{1,257},{257,1},{2,258},{258,2},{3,259},{259,3},{4... | collective-permute-start | bytes 12296 | tf_op jit(solution)/shard_map/ppermute | solution.py:367
Sparse Core Ops, SparseCore 0:
  32.0 48.6 all-gather.2
  82.7 20.8 all-gather.4

commit v6 on v5

--- a/solution.py
+++ b/solution.py
@@ -209,25 +209,15 @@
         out[block] = normed
 
 
-def feed_forward_kernel(rows, weights, out, up, down, arrived):
-    def fetch(part, side):
-        far = weights.at[pl.ds(SEQ * part, SEQ), PIECE * side : PIECE * side + PIECE, :]
-        return pltpu.make_async_copy(far, (up, down)[side].at[part], arrived.at[part, side])
-
-    fetch(0, 0).start()
-    fetch(0, 1).start()
+def feed_forward_kernel(rows, own, other, out):
     block = rows[...].reshape(GROUP * OWN, D)
     result = None
-    for part in range(2):
-        fetch(part, 0).wait()
-        if part == 0:
-            fetch(1, 0).start()
-        hidden = jnp.dot(block, up[part].reshape(D, UNITS), preferred_element_type=F32)
+    for weights in (other, own):
+        up = weights[:, 0:PIECE, :].reshape(D, UNITS)
+        down = weights[:, PIECE : 2 * PIECE, :].reshape(D, UNITS)
+        hidden = jnp.dot(block, up, preferred_element_type=F32)
         activated = jax.nn.gelu(hidden, approximate=True).astype(BF16)
-        fetch(part, 1).wait()
-        if part == 0:
-            fetch(1, 1).start()
-        term = lax.dot_general(activated, down[part].reshape(D, UNITS), ROWS_BY_ROWS, preferred_element_type=F32)
+        term = lax.dot_general(activated, down, ROWS_BY_ROWS, preferred_element_type=F32)
         result = term if result is None else result + term
     out[...] = result.astype(BF16).reshape(GROUP, OWN, D)
 
@@ -250,7 +240,7 @@
     after_mlp = after[...] + pick(5) * sum_blocks(got)
     hidden_out[0] = after_mlp.astype(BF16)
     normed = (layer_norm(after_mlp, 1e-05) * (1.0 + pick(7)) + pick(6)).astype(BF16)
-    predicted[...] = jnp.dot(normed, weight[...], preferred_element_type=F32)
+    predicted[...] = lax.dot_general(normed, weight[...], ROWS_BY_ROWS, preferred_element_type=F32)
 
 
 def alpha_bar(last):
@@ -280,12 +270,12 @@
 ALONE = 60
 
 
-def call(kernel, specs, shapes, mib=24, result=VMEM, scratch=()):
+def call(kernel, specs, shapes, mib=24, scratch=()):
     return pl.pallas_call(
         kernel,
         out_shape=shapes,
         in_specs=specs,
-        out_specs=jax.tree.map(lambda _: result, shapes),
+        out_specs=jax.tree.map(lambda _: VMEM, shapes),
         scratch_shapes=scratch,
         compiler_params=pltpu.CompilerParams(vmem_limit_bytes=mib * 2**20),
         cost_estimate=pl.CostEstimate(flops=10_000_000, bytes_accessed=4_000_000, transcendentals=0),
@@ -314,7 +304,6 @@
         [HBM, HBM],
         jax.ShapeDtypeStruct((4, 2 * PIECE, UNITS), BF16),
         mib=ALONE,
-        result=HBM,
         scratch=[pltpu.SemaphoreType.DMA((4, 2))],
     )(up_weight, down_weight.T)
     pieces = lax.all_to_all(pieces, LINE, 0, 0, tiled=True)
@@ -334,9 +323,8 @@
             pltpu.SemaphoreType.DMA((6,)),
         ],
     )(place, text_count, step_index, tokens_in, modulation, qk_gain, positions, jnp.asarray(frequencies()), qkv_weight)
-    sent, pieces = lax.optimization_barrier((sent, pieces))
+    sent, pieces, branch, part = lax.optimization_barrier((sent, pieces, branch, part))
     weights = lax.all_gather(pieces, "z", axis=0, tiled=True)
-    weights = lax.all_gather(weights, "core", axis=0, tiled=True)
     got = lax.all_to_all(sent, SEQ_AXES, 0, 0, tiled=True)
     attended = call(attend_kernel, [VMEM], jax.ShapeDtypeStruct((SEQ, 32, 128), BF16))(got)
     back = lax.all_to_all(attended, SEQ_AXES, 0, 0, tiled=True)
@@ -349,21 +337,16 @@
         [SMEM, SMEM, SMEM, VMEM, VMEM, VMEM],
         (jax.ShapeDtypeStruct((OWN, D), F32), shared),
     )(place, part, text_count, partial, tokens_in, modulation)
+    rows, weights = lax.optimization_barrier((rows, weights))
     rows = lax.all_to_all(rows, SHARERS, 0, 0, tiled=True)
-    both = pltpu.VMEM((2, SEQ, PIECE, UNITS), BF16)
-    mlp = call(
-        feed_forward_kernel,
-        [VMEM, HBM],
-        shared,
-        mib=ALONE,
-        scratch=[both, both, pltpu.SemaphoreType.DMA((2, 2))],
-    )(rows, weights)
+    swapped = lax.ppermute(weights, "core", [(0, 1), (1, 0)])
+    mlp = call(feed_forward_kernel, [VMEM, VMEM, VMEM], shared)(rows, weights, swapped)
     mlp = lax.all_to_all(mlp, SHARERS, 0, 0, tiled=True)
     hidden_out, predicted = call(
         predict_kernel,
         [SMEM, SMEM, SMEM, VMEM, VMEM, VMEM, VMEM],
         (jax.ShapeDtypeStruct((1, OWN, D), BF16), jax.ShapeDtypeStruct((OWN, 64), F32)),
-    )(place, part, text_count, mlp, after, modulation, proj_weight)
+    )(place, part, text_count, mlp, after, modulation, proj_weight.T)
     partner = lax.ppermute(predicted, "cfg", [(0, 1), (1, 0)])
     latent_prev = call(
         step_kernel,

time: 187 us -> 138 us (0.74); the launches traced: 185 us -> 138 us
  waiting for transfers between devices: 69.8 us -> 7.72 us
  blocking collectives: 50.6 us -> 86.6 us
  Pallas kernels: 26.6 us -> 13.3 us
  starting transfers between devices: 20.5 us -> 11.4 us
    all_gather x1, waiting for transfers between devices: 48.7 us -> 0.02 us  [body(): weights = lax.all_gather(pieces, 'z', axis=0, tiled=True)]
    all_to_all x0 -> x2, blocking collectives: none -> 24.4 us  [the longest x1 13 us: body(): partial = lax.all_to_all(partial, BLK_AXES, 0, 0, tiled=True)]
    all_to_all x2 -> x0, waiting for transfers between devices: 15.3 us -> none  [the longest x1 8.94 us: body(): partial = lax.all_to_all(partial, BLK_AXES, 0, 0, tiled=True)]
    all_to_all x1, blocking collectives: 23.6 us -> 34.4 us  [body(): got = lax.all_to_all(sent, SEQ_AXES, 0, 0, tiled=True)]
    all_to_all x2 -> x0, starting transfers between devices: 8.96 us -> none  [the longest x1 4.74 us: body(): mlp = lax.all_to_all(mlp, SHARERS, 0, 0, tiled=True)]
    pallas_call x1, Pallas kernels: 10.1 us -> 1.67 us  [body(): call(pieces_kernel, [HBM, HBM], jax.ShapeDtypeStruct((4, 2 * PIECE, UNITS...]
    pallas_call x1, Pallas kernels: 5.72 us -> 1.36 us  [body(): call(feed_forward_kernel, [VMEM, VMEM, VMEM], shared)]
    ppermute x1, waiting for transfers between devices: 3.69 us -> 5.63 us  [body(): partner = lax.ppermute(predicted, 'cfg', [(0, 1), (1, 0)])]
  transfers between devices with their start and end apart: 6 -> 4, of which waited for: 5 -> 2; matrix products, arithmetic and copies ran while one was open for 0% -> 0% of each run, Pallas kernels for 5% -> 6%
where the time goes in v6:
time: 138 us
  blocking collectives  86.6 us (63%)
  between operations  16.1 us (12%)
  Pallas kernels  13.3 us (10%)
  starting transfers between devices  11.4 us (8%)
  waiting for transfers between devices  7.72 us (6%)
  local copies, waits for them, and re-layouts  2.42 us (2%)
    all_to_all x1, blocking collectives, body(): got = lax.all_to_all(sent, SEQ_AXES, 0, 0, tiled=True)  34.4 us
    all_to_all x1, blocking collectives, body(): back = lax.all_to_all(attended, SEQ_AXES, 0, 0, tiled=True)  16 us
    all_to_all x1, blocking collectives, body(): partial = lax.all_to_all(partial, BLK_AXES, 0, 0, tiled=True)  13 us
    all_to_all x1, blocking collectives, body(): rows = lax.all_to_all(rows, SHARERS, 0, 0, tiled=True)  11.7 us
    all_to_all x1, blocking collectives, body(): mlp = lax.all_to_all(mlp, SHARERS, 0, 0, tiled=True)  11.4 us
    all_to_all x1, starting transfers between devices, body(): pieces = lax.all_to_all(pieces, LINE, 0, 0, tiled=True)  6.35 us
    ppermute x1, waiting for transfers between devices, body(): partner = lax.ppermute(predicted, 'cfg', [(0, 1), (1, 0)])  5.63 us
    pallas_call x1, Pallas kernels, body(): call(project_kernel, [SMEM, SMEM, SMEM] + [HBM] * 6, (jax.ShapeDtypeStruc...  4.12 us
  transfers between devices with their start and end apart: 4, of which 2 were waited for; matrix products, arithmetic and copies ran while one was open for 0% of the time, Pallas kernels for 6%

profile of v6, /device:TPU:56, one launch (start us, length us, event | category | flops | bytes accessed | tf_op | source)
XLA Modules:
  0.0 137.6 jit_solution(7000926678956282093)
XLA Ops:
  7.2 1.7 %shard_map.150 = bf16[4,96,384]{2,1,0:T(8,128)(2,1)} custom-call(bf16[48,768]{1,0:T(8,128)(2,1)} %up.1, bf16[48,768]{1,0:T(8,128)(2,1)} %bitcast.6), custom_call_target="tpu_custom_call" | custom-call | flops 10000000 | bytes 4000000 | tf_op jit(solution)/shard_map/pallas_call | solution.py:302
  8.8 6.4 %all-to-all-start = ((bf16[4,96,384]{2,1,0:T(8,128)(2,1)}), bf16[4,96,384]{2,1,0:T(8,128)(2,1)S(1)}, u32[]{:S(2)}, u32[]{:S(2)}) async-start(bf16[4,96,384]{2,1,0:T(8,128)(2,1)} %shard_map.150), calls=%async_computation | async-start | bytes 589824 | tf_op jit(solution)/shard_map/all_to_all | solution.py:309
  15.2 0.0 all-gather.2.cloned.1.call-start
  16.5 0.0 copy-start.3
  16.5 4.1 %shard_map.149 = (bf16[32,80,128]{2,1,0:T(8,128)(2,1)}, f32[8,128]{1,0:T(8,128)}) custom-call(s32[1]{0:T(128)} %bitcast.place, s32[1]{0:T(128)S(6)} %copy.16.text, s32[1]{0:T(128)S(6)} %copy.17.step, bf16[1,128,1536]{2,1,0:T(8,128)(2,1)} %tokens.1, f32[2,8,1536]{2,1,0:T(8,128)} %mods.3, f32[2,64]{1,0:T(2,128)} %gain_far.1, s32[3,128]{1,0:T(4,128)} %positions_far.1, ...), custom_call_target="tpu_custom_call" | custom-call | flops 10000000 | bytes 4000000 | tf_op jit(solution)/shard_map/pallas_call | solution.py:311
  20.6 2.0 %all-to-all-done = bf16[4,96,384]{2,1,0:T(8,128)(2,1)S(1)} async-done(((bf16[4,96,384]{2,1,0:T(8,128)(2,1)}), bf16[4,96,384]{2,1,0:T(8,128)(2,1)S(1)}, u32[]{:S(2)}, u32[]{:S(2)}) %all-to-all-start) | async-done | bytes 294944 | tf_op jit(solution)/shard_map/all_to_all | solution.py:309
  22.7 0.7 copy-done.7
  23.4 0.0 all-gather.2.cloned.1.call-update
  23.4 0.0 copy-start.1
  23.4 0.0 copy-start.2
  23.5 34.4 %all_to_all.30.got = bf16[32,80,128]{2,1,0:T(8,128)(2,1)S(1)} all-to-all(bf16[32,80,128]{2,1,0:T(8,128)(2,1)} %get-tuple-element.16), channel_id=1, replica_groups=mesh['cfg'=2,'z'=8,'pair'=2,'side'=2,'x'=4,'core'=2] {'z','pair','side'}, dimensions={0} | all-to-all | bytes 1310720 | tf_op jit(solution)/shard_map/all_to_all | solution.py:328
  57.9 3.5 %shard_map.151 = bf16[32,32,128]{2,1,0:T(8,128)(2,1)S(1)} custom-call(bf16[32,80,128]{2,1,0:T(8,128)(2,1)S(1)} %all_to_all.30.got), custom_call_target="tpu_custom_call" | custom-call | flops 10000000 | bytes 4000000 | tf_op jit(solution)/shard_map/pallas_call | solution.py:329
  61.3 16.0 %all_to_all.31.got = bf16[32,32,128]{2,1,0:T(8,128)(2,1)S(1)} all-to-all(bf16[32,32,128]{2,1,0:T(8,128)(2,1)S(1)} %shard_map.151), channel_id=1, replica_groups=mesh['cfg'=2,'z'=8,'pair'=2,'side'=2,'x'=4,'core'=2] {'z','pair','side'}, dimensions={0} | all-to-all | bytes 524288 | tf_op jit(solution)/shard_map/all_to_all | solution.py:330
  77.4 0.0 copy-done.3
  77.4 0.9 shard_map.152
  78.3 13.0 %all_to_all.32.got = bf16[8,16,1536]{2,1,0:T(8,128)(2,1)S(1)} all-to-all(bf16[8,16,1536]{2,1,0:T(8,128)(2,1)S(1)} %shard_map.152), channel_id=1, replica_groups=mesh['cfg'=2,'z'=8,'pair'=2,'side'=2,'x'=4,'core'=2] {'x','core'}, dimensions={0} | all-to-all | bytes 786432 | tf_op jit(solution)/shard_map/all_to_all | solution.py:334
  91.3 0.0 copy-done.1
  91.3 0.0 copy-done.2
  91.3 0.3 shard_map.153
  91.6 0.0 all-gather.2.cloned.1.call-done.own
  91.6 1.9 %collective-permute-start = (bf16[32,96,384]{2,1,0:T(8,128)(2,1)}, bf16[32,96,384]{2,1,0:T(8,128)(2,1)S(1)}, u32[]{:S(2)}, u32[]{:S(2)}) collective-permute-start(bf16[32,96,384]{2,1,0:T(8,128)(2,1)} %all-gather.2.cloned.1.call-done.own), channel_id=1, source_target_pairs={{0,1},{1,0},{2,3},{3,2},{4,5},{5,4},{6,7},{7,6},{8,9},{9,8},{10,11... | collective-permute-start | bytes 7077896 | tf_op jit(solution)/shard_map/ppermute | solution.py:342
  93.5 11.7 %all_to_all.33.rows = bf16[8,16,1536]{2,1,0:T(8,128)(2,1)S(1)} all-to-all(bf16[8,16,1536]{2,1,0:T(8,128)(2,1)S(1)} %get-tuple-element.19), channel_id=1, replica_groups=mesh['cfg'=2,'z'=8,'pair'=2,'side'=2,'x'=4,'core'=2] {'side','x'}, dimensions={0} | all-to-all | bytes 786432 | tf_op jit(solution)/shard_map/all_to_all | solution.py:341
  105.2 0.0 collective-permute-done.other
  105.2 1.7 %copy-done = bf16[32,96,384]{2,1,0:T(8,128)(2,1)S(1)} copy-done((bf16[32,96,384]{2,1,0:T(8,128)(2,1)S(1)}, bf16[32,96,384]{2,1,0:T(8,128)(2,1)}, u32[]{:S(2)}) %copy-start) | copy-done | bytes 2359320
  106.9 1.4 shard_map.154
  108.3 11.4 %all_to_all.34.got = bf16[8,16,1536]{2,1,0:T(8,128)(2,1)S(1)} all-to-all(bf16[8,16,1536]{2,1,0:T(8,128)(2,1)S(1)} %shard_map.154), channel_id=1, replica_groups=mesh['cfg'=2,'z'=8,'pair'=2,'side'=2,'x'=4,'core'=2] {'side','x'}, dimensions={0} | all-to-all | bytes 786432 | tf_op jit(solution)/shard_map/all_to_all | solution.py:344
  119.7 0.0 copy-done.4
  119.7 0.9 shard_map.155
  120.6 3.2 %collective-permute-start.1 = (f32[16,64]{1,0:T(8,128)S(1)}, f32[16,64]{1,0:T(8,128)S(1)}, u32[]{:S(2)}, u32[]{:S(2)}) collective-permute-start(f32[16,64]{1,0:T(8,128)S(1)} %get-tuple-element.25.mine), channel_id=1, source_target_pairs={{0,256},{256,0},{1,257},{257,1},{2,258},{258,2},{3,259},{259,3},{4... | collective-permute-start | bytes 12296 | tf_op jit(solution)/shard_map/ppermute | solution.py:350
  124.4 5.6 %collective-permute-done.1.other = f32[16,64]{1,0:T(8,128)S(1)} collective-permute-done((f32[16,64]{1,0:T(8,128)S(1)}, f32[16,64]{1,0:T(8,128)S(1)}, u32[]{:S(2)}, u32[]{:S(2)}) %collective-permute-start.1) | collective-permute-done | bytes 4128 | tf_op jit(solution)/shard_map/ppermute | solution.py:350
  130.0 0.0 copy-done.5
  130.0 0.7 shard_map.156
  (6 shorter events, 0.0 us)
Async XLA Ops:
  8.8 13.8 %all-to-all-start = ((bf16[4,96,384]{2,1,0:T(8,128)(2,1)}), bf16[4,96,384]{2,1,0:T(8,128)(2,1)S(1)}, u32[]{:S(2)}, u32[]{:S(2)}) async-start(bf16[4,96,384]{2,1,0:T(8,128)(2,1)} %shard_map.150), calls=%async_computation | async-start | bytes 589824 | tf_op jit(solution)/shard_map/all_to_all | solution.py:309
  15.2 76.4 %all-gather.2.cloned.1.call-start = ((), (), s32[]{:S(2)}) async-start(), calls=%async_computation.6 | async-start | bytes 2654208 | tf_op jit(solution)/shard_map/all_gather | solution.py:327
  16.5 60.9 %copy-start.3 = (bf16[192,1536]{1,0:T(8,128)(2,1)S(1)}, bf16[192,1536]{1,0:T(8,128)(2,1)}, u32[]{:S(2)}) copy-start(bf16[192,1536]{1,0:T(8,128)(2,1)} %weight.1) | copy-start | bytes 1769476
  22.7 0.7 copy-start.7
  23.4 67.9 %copy-start.1 = (bf16[1,128,1536]{2,1,0:T(8,128)(2,1)S(1)}, bf16[1,128,1536]{2,1,0:T(8,128)(2,1)}, u32[]{:S(2)}) copy-start(bf16[1,128,1536]{2,1,0:T(8,128)(2,1)} %tokens.1) | copy-start | bytes 1179652
  23.4 67.8 %copy-start.2 = (f32[2,8,1536]{2,1,0:T(8,128)S(1)}, f32[2,8,1536]{2,1,0:T(8,128)}, u32[]{:S(2)}) copy-start(f32[2,8,1536]{2,1,0:T(8,128)} %mods.3) | copy-start | bytes 294916
  91.6 13.6 %collective-permute-start = (bf16[32,96,384]{2,1,0:T(8,128)(2,1)}, bf16[32,96,384]{2,1,0:T(8,128)(2,1)S(1)}, u32[]{:S(2)}, u32[]{:S(2)}) collective-permute-start(bf16[32,96,384]{2,1,0:T(8,128)(2,1)} %all-gather.2.cloned.1.call-done.own), channel_id=1, source_target_pairs={{0,1},{1,0},{2,3},{3,2},{4,5},{5,4},{6,7},{7,6},{8,9},{9,8},{10,11... | collective-permute-start | bytes 7077896 | tf_op jit(solution)/shard_map/ppermute | solution.py:342
  105.2 1.7 %copy-start = (bf16[32,96,384]{2,1,0:T(8,128)(2,1)S(1)}, bf16[32,96,384]{2,1,0:T(8,128)(2,1)}, u32[]{:S(2)}) copy-start(bf16[32,96,384]{2,1,0:T(8,128)(2,1)} %all-gather.2.cloned.1.call-done.own) | copy-start | bytes 7077892
  106.9 12.8 %copy-start.4 = (bf16[1536,64]{0,1:T(8,128)(2,1)S(1)}, bf16[1536,64]{0,1:T(8,128)(2,1)}, u32[]{:S(2)}) copy-start(bf16[1536,64]{0,1:T(8,128)(2,1)} %param.21) | copy-start | bytes 589828
  106.9 23.1 %copy-start.5 = (f32[16,32]{1,0:T(8,128)S(1)}, f32[16,32]{1,0:T(8,128)}, u32[]{:S(2)}) copy-start(f32[16,32]{1,0:T(8,128)} %latent.1) | copy-start | bytes 6148
  106.9 23.1 %copy-start.6 = (f32[8,128]{1,0:T(8,128)S(1)}, f32[8,128]{1,0:T(8,128)}, u32[]{:S(2)}) copy-start(f32[8,128]{1,0:T(8,128)} %get-tuple-element.24.alphas) | copy-start | bytes 12292
  120.6 9.4 %collective-permute-start.1 = (f32[16,64]{1,0:T(8,128)S(1)}, f32[16,64]{1,0:T(8,128)S(1)}, u32[]{:S(2)}, u32[]{:S(2)}) collective-permute-start(f32[16,64]{1,0:T(8,128)S(1)} %get-tuple-element.25.mine), channel_id=1, source_target_pairs={{0,256},{256,0},{1,257},{257,1},{2,258},{258,2},{3,259},{259,3},{4... | collective-permute-start | bytes 12296 | tf_op jit(solution)/shard_map/ppermute | solution.py:350
Sparse Core Ops, SparseCore 0:
  23.6 62.0 all-gather.1

commit v7 on v6

--- a/solution.py
+++ b/solution.py
@@ -222,6 +222,13 @@
     out[...] = result.astype(BF16).reshape(GROUP, OWN, D)
 
 
+def assemble_kernel(place, *refs):
+    blocks, out = refs[:9], refs[9]
+    for block, away, start in zip(blocks, (0, -1, -2, -3, -4, 1, 2, 3, 4), (0, 0, 0, 0, 0, 0, 0, 0, 2)):
+        first = (place[0] // 4 + 8 + away) % 8 * 4 + start
+        out[pl.ds(first, block.shape[0])] = block[...]
+
+
 def pieces_kernel(up, down, out, arrived):
     copies = []
     for device in range(4):
@@ -308,6 +315,9 @@
     )(up_weight, down_weight.T)
     pieces = lax.all_to_all(pieces, LINE, 0, 0, tiled=True)
 
+    def shifted(block, step):
+        return lax.ppermute(block, "z", [(z, (z + step) % 8) for z in range(8)])
+
     sent, alphas = call(
         project_kernel,
         [SMEM, SMEM, SMEM] + [HBM] * 6,
@@ -324,19 +334,35 @@
         ],
     )(place, text_count, step_index, tokens_in, modulation, qk_gain, positions, jnp.asarray(frequencies()), qkv_weight)
     sent, pieces, branch, part = lax.optimization_barrier((sent, pieces, branch, part))
-    weights = lax.all_gather(pieces, "z", axis=0, tiled=True)
     got = lax.all_to_all(sent, SEQ_AXES, 0, 0, tiled=True)
+    below, above = [shifted(pieces, 1)], [shifted(pieces, -1)]
+    got, below, above = lax.optimization_barrier((got, below, above))
     attended = call(attend_kernel, [VMEM], jax.ShapeDtypeStruct((SEQ, 32, 128), BF16))(got)
+    attended, below, above = lax.optimization_barrier((attended, below, above))
     back = lax.all_to_all(attended, SEQ_AXES, 0, 0, tiled=True)
+    below.append(shifted(below[0], 1))
+    above.append(shifted(above[0], -1))
+    back, below, above = lax.optimization_barrier((back, below, above))
     blocks = jax.ShapeDtypeStruct((BLK, OWN, D), BF16)
     shared = jax.ShapeDtypeStruct((GROUP, OWN, D), BF16)
     partial = call(out_project_kernel, [VMEM, VMEM], blocks)(back, out_weight)
+    partial, below, above = lax.optimization_barrier((partial, below, above))
     partial = lax.all_to_all(partial, BLK_AXES, 0, 0, tiled=True)
+    below.append(shifted(below[1], 1))
+    above.append(shifted(above[1], -1))
+    below.append(shifted(below[2][0:2], 1))
+    above.append(shifted(above[2][2:4], -1))
+    partial, below, above = lax.optimization_barrier((partial, below, above))
     after, rows = call(
         after_attention_kernel,
         [SMEM, SMEM, SMEM, VMEM, VMEM, VMEM],
         (jax.ShapeDtypeStruct((OWN, D), F32), shared),
     )(place, part, text_count, partial, tokens_in, modulation)
+    weights = call(
+        assemble_kernel,
+        [SMEM] + [VMEM] * 9,
+        jax.ShapeDtypeStruct((SEQ, 2 * PIECE, UNITS), BF16),
+    )(place, pieces, *below, *above)
     rows, weights = lax.optimization_barrier((rows, weights))
     rows = lax.all_to_all(rows, SHARERS, 0, 0, tiled=True)
     swapped = lax.ppermute(weights, "core", [(0, 1), (1, 0)])

time: 138 us -> 144 us (1.043)
  blocking collectives: 86.6 us -> 25.1 us
  starting transfers between devices: 11.4 us -> 65.7 us
  waiting for transfers between devices: 7.72 us -> 34.5 us
  between operations: 16.1 us -> 2.78 us
  local copies, waits for them, and re-layouts: 2.42 us -> 0.06 us
  Pallas kernels: 13.3 us -> 15.1 us
    all_to_all x3 -> x0, blocking collectives: 63.5 us -> none  [the longest x1 34.4 us: body(): got = lax.all_to_all(sent, SEQ_AXES, 0, 0, tiled=True)]
    ppermute x0 -> x8, starting transfers between devices: none -> 28.3 us  [shifted(): return lax.ppermute(block, 'z', [(z, (z + step) % 8) for z in range(8)])]
    all_to_all x0 -> x3, starting transfers between devices: none -> 25.9 us  [the longest x1 13.7 us: body(): got = lax.all_to_all(sent, SEQ_AXES, 0, 0, tiled=True)]
    ppermute x0 -> x8, waiting for transfers between devices: none -> 25.5 us  [shifted(): return lax.ppermute(block, 'z', [(z, (z + step) % 8) for z in range(8)])]
    unnamed x16 -> x12, local copies, waits for them, and re-layouts: 2.42 us -> 0.03 us
    all_to_all x1, blocking collectives: 11.7 us -> 13.7 us  [body(): rows = lax.all_to_all(rows, SHARERS, 0, 0, tiled=True)]
  transfers between devices with their start and end apart: 4 -> 14, of which waited for: 2 -> 8; matrix products, arithmetic and copies ran while one was open for 0% -> 0% of each run, Pallas kernels for 6% -> 3%
where the time goes in v7:
time: 144 us; the launch traced here: 143 us
  starting transfers between devices  65.7 us (46%)
  waiting for transfers between devices  34.5 us (24%)
  blocking collectives  25.1 us (17%)
  Pallas kernels  15.1 us (10%)
  between operations  2.78 us (2%)
    ppermute x8, starting transfers between devices, shifted(): return lax.ppermute(block, 'z', [(z, (z + step) % 8) for z in range(8)])  28.3 us
    ppermute x8, waiting for transfers between devices, shifted(): return lax.ppermute(block, 'z', [(z, (z + step) % 8) for z in range(8)])  25.5 us
    all_to_all x1, starting transfers between devices, body(): got = lax.all_to_all(sent, SEQ_AXES, 0, 0, tiled=True)  13.7 us
    all_to_all x1, blocking collectives, body(): rows = lax.all_to_all(rows, SHARERS, 0, 0, tiled=True)  13.7 us
    all_to_all x1, blocking collectives, body(): mlp = lax.all_to_all(mlp, SHARERS, 0, 0, tiled=True)  11.4 us
    all_to_all x1, starting transfers between devices, body(): back = lax.all_to_all(attended, SEQ_AXES, 0, 0, tiled=True)  7.88 us
    all_to_all x1, starting transfers between devices, body(): pieces = lax.all_to_all(pieces, LINE, 0, 0, tiled=True)  6.35 us
    ppermute x1, waiting for transfers between devices, body(): partner = lax.ppermute(predicted, 'cfg', [(0, 1), (1, 0)])  5.64 us
  transfers between devices with their start and end apart: 14, of which 8 were waited for; matrix products, arithmetic and copies ran while one was open for 0% of the time, Pallas kernels for 3%

profile of v7, /device:TPU:56, one launch (start us, length us, event | category | flops | bytes accessed | tf_op | source)
XLA Modules:
  0.0 143.2 jit_solution(15339118362526034859)
XLA Ops:
  0.6 1.7 %shard_map.150 = bf16[4,96,384]{2,1,0:T(8,128)(2,1)} custom-call(bf16[48,768]{1,0:T(8,128)(2,1)} %up.1, bf16[48,768]{1,0:T(8,128)(2,1)} %bitcast.6), custom_call_target="tpu_custom_call" | custom-call | flops 10000000 | bytes 4000000 | tf_op jit(solution)/shard_map/pallas_call | solution.py:309
  2.3 6.4 %all-to-all-start = ((bf16[4,96,384]{2,1,0:T(8,128)(2,1)}), bf16[4,96,384]{2,1,0:T(8,128)(2,1)S(1)}, u32[]{:S(2)}, u32[]{:S(2)}) async-start(bf16[4,96,384]{2,1,0:T(8,128)(2,1)} %shard_map.150), calls=%async_computation | async-start | bytes 589824 | tf_op jit(solution)/shard_map/all_to_all | solution.py:316
  10.0 4.1 %shard_map.149 = (bf16[32,80,128]{2,1,0:T(8,128)(2,1)}, f32[8,128]{1,0:T(8,128)}) custom-call(s32[1]{0:T(128)} %bitcast.place, s32[1]{0:T(128)S(6)} %copy.16.text, s32[1]{0:T(128)S(6)} %copy.17.step, bf16[1,128,1536]{2,1,0:T(8,128)(2,1)} %tokens.1, f32[2,8,1536]{2,1,0:T(8,128)} %mods.3, f32[2,64]{1,0:T(2,128)} %gain_far.1, s32[3,128]{1,0:T(4,128)} %positions_far.1, ...), custom_call_target="tpu_custom_call" | custom-call | flops 10000000 | bytes 4000000 | tf_op jit(solution)/shard_map/pallas_call | solution.py:321
  14.1 2.0 %all-to-all-done.refs_0_ = bf16[4,96,384]{2,1,0:T(8,128)(2,1)S(1)} async-done(((bf16[4,96,384]{2,1,0:T(8,128)(2,1)}), bf16[4,96,384]{2,1,0:T(8,128)(2,1)S(1)}, u32[]{:S(2)}, u32[]{:S(2)}) %all-to-all-start) | async-done | bytes 294944 | tf_op jit(solution)/shard_map/all_to_all | solution.py:316
  16.2 13.7 %all-to-all-start.1 = ((bf16[32,80,128]{2,1,0:T(8,128)(2,1)}), bf16[32,80,128]{2,1,0:T(8,128)(2,1)S(1)}, u32[]{:S(2)}, u32[]{:S(2)}) async-start(bf16[32,80,128]{2,1,0:T(8,128)(2,1)} %get-tuple-element.41), calls=%async_computation.1 | async-start | bytes 1310720 | tf_op jit(solution)/shard_map/all_to_all | solution.py:337
  29.9 3.5 %collective-permute-start = (bf16[4,96,384]{2,1,0:T(8,128)(2,1)S(1)}, bf16[4,96,384]{2,1,0:T(8,128)(2,1)S(1)}, u32[]{:S(2)}, u32[]{:S(2)}) collective-permute-start(bf16[4,96,384]{2,1,0:T(8,128)(2,1)S(1)} %all-to-all-done.refs_0_), channel_id=1, source_target_pairs={{0,32},{32,64},{64,96},{96,128},{128,160},{160,192},{192,224},{224... | collective-permute-start | bytes 884744 | tf_op jit(solution)/shard_map/ppermute | solution.py:319
  33.4 3.7 %collective-permute-start.1 = (bf16[4,96,384]{2,1,0:T(8,128)(2,1)S(1)}, bf16[4,96,384]{2,1,0:T(8,128)(2,1)S(1)}, u32[]{:S(2)}, u32[]{:S(2)}) collective-permute-start(bf16[4,96,384]{2,1,0:T(8,128)(2,1)S(1)} %all-to-all-done.refs_0_), channel_id=1, source_target_pairs={{0,224},{32,0},{64,32},{96,64},{128,96},{160,128},{192,160},{224,1... | collective-permute-start | bytes 884744 | tf_op jit(solution)/shard_map/ppermute | solution.py:319
  37.1 15.3 %collective-permute-done.refs_1_ = bf16[4,96,384]{2,1,0:T(8,128)(2,1)S(1)} collective-permute-done((bf16[4,96,384]{2,1,0:T(8,128)(2,1)S(1)}, bf16[4,96,384]{2,1,0:T(8,128)(2,1)S(1)}, u32[]{:S(2)}, u32[]{:S(2)}) %collective-permute-start) | collective-permute-done | bytes 294944 | tf_op jit(solution)/shard_map/ppermute | solution.py:319
  52.4 4.2 %shard_map.151 = bf16[32,32,128]{2,1,0:T(8,128)(2,1)} custom-call(bf16[32,80,128]{2,1,0:T(8,128)(2,1)S(1)} %all-to-all-done.1.got), custom_call_target="tpu_custom_call" | custom-call | flops 10000000 | bytes 4000000 | tf_op jit(solution)/shard_map/pallas_call | solution.py:340
  56.6 7.9 %all-to-all-start.2 = ((bf16[32,32,128]{2,1,0:T(8,128)(2,1)}), bf16[32,32,128]{2,1,0:T(8,128)(2,1)S(1)}, u32[]{:S(2)}, u32[]{:S(2)}) async-start(bf16[32,32,128]{2,1,0:T(8,128)(2,1)} %shard_map.151), calls=%async_computation.2 | async-start | bytes 524288 | tf_op jit(solution)/shard_map/all_to_all | solution.py:342
  64.5 3.4 %collective-permute-start.2 = (bf16[4,96,384]{2,1,0:T(8,128)(2,1)S(1)}, bf16[4,96,384]{2,1,0:T(8,128)(2,1)S(1)}, u32[]{:S(2)}, u32[]{:S(2)}) collective-permute-start(bf16[4,96,384]{2,1,0:T(8,128)(2,1)S(1)} %collective-permute-done.refs_1_), channel_id=1, source_target_pairs={{0,32},{32,64},{64,96},{96,128},{128,160},{160,192},{192,224},{224... | collective-permute-start | bytes 884744 | tf_op jit(solution)/shard_map/ppermute | solution.py:319
  67.9 3.7 %collective-permute-start.3 = (bf16[4,96,384]{2,1,0:T(8,128)(2,1)S(1)}, bf16[4,96,384]{2,1,0:T(8,128)(2,1)S(1)}, u32[]{:S(2)}, u32[]{:S(2)}) collective-permute-start(bf16[4,96,384]{2,1,0:T(8,128)(2,1)S(1)} %collective-permute-done.1.refs_5_), channel_id=1, source_target_pairs={{0,224},{32,0},{64,32},{96,64},{128,96},{160,128},{192,160},{224,1... | collective-permute-start | bytes 884744 | tf_op jit(solution)/shard_map/ppermute | solution.py:319
  71.6 8.1 %collective-permute-done.2.refs_2_ = bf16[4,96,384]{2,1,0:T(8,128)(2,1)S(1)} collective-permute-done((bf16[4,96,384]{2,1,0:T(8,128)(2,1)S(1)}, bf16[4,96,384]{2,1,0:T(8,128)(2,1)S(1)}, u32[]{:S(2)}, u32[]{:S(2)}) %collective-permute-start.2) | collective-permute-done | bytes 294944 | tf_op jit(solution)/shard_map/ppermute | solution.py:319
  79.7 1.6 %shard_map.152 = bf16[8,16,1536]{2,1,0:T(8,128)(2,1)} custom-call(bf16[32,32,128]{2,1,0:T(8,128)(2,1)S(1)} %all-to-all-done.2.got, bf16[192,1536]{1,0:T(8,128)(2,1)S(1)} %copy-done.2), custom_call_target="tpu_custom_call" | custom-call | flops 10000000 | bytes 4000000 | tf_op jit(solution)/shard_map/pallas_call | solution.py:348
  81.3 2.7 %collective-permute-start.4 = (bf16[4,96,384]{2,1,0:T(8,128)(2,1)S(1)}, bf16[4,96,384]{2,1,0:T(8,128)(2,1)S(1)}, u32[]{:S(2)}, u32[]{:S(2)}) collective-permute-start(bf16[4,96,384]{2,1,0:T(8,128)(2,1)S(1)} %collective-permute-done.2.refs_2_), channel_id=1, source_target_pairs={{0,32},{32,64},{64,96},{96,128},{128,160},{160,192},{192,224},{224... | collective-permute-start | bytes 884744 | tf_op jit(solution)/shard_map/ppermute | solution.py:319
  84.0 4.3 %collective-permute-start.6 = (bf16[4,96,384]{2,1,0:T(8,128)(2,1)S(1)}, bf16[4,96,384]{2,1,0:T(8,128)(2,1)S(1)}, u32[]{:S(2)}, u32[]{:S(2)}) collective-permute-start(bf16[4,96,384]{2,1,0:T(8,128)(2,1)S(1)} %collective-permute-done.3.refs_6_), channel_id=1, source_target_pairs={{0,224},{32,0},{64,32},{96,64},{128,96},{160,128},{192,160},{224,1... | collective-permute-start | bytes 884744 | tf_op jit(solution)/shard_map/ppermute | solution.py:319
  88.3 4.3 %all-to-all-start.3 = ((bf16[8,16,1536]{2,1,0:T(8,128)(2,1)}), bf16[8,16,1536]{2,1,0:T(8,128)(2,1)S(1)}, u32[]{:S(2)}, u32[]{:S(2)}) async-start(bf16[8,16,1536]{2,1,0:T(8,128)(2,1)} %shard_map.152), calls=%async_computation.3 | async-start | bytes 786432 | tf_op jit(solution)/shard_map/all_to_all | solution.py:350
  92.7 0.5 collective-permute-done.4.refs_3_
  93.2 1.9 %collective-permute-start.5 = (bf16[2,96,384]{2,1,0:T(8,128)(2,1)S(1)}, bf16[2,96,384]{2,1,0:T(8,128)(2,1)S(1)}, u32[]{:S(2)}, u32[]{:S(2)}) collective-permute-start(bf16[2,96,384]{2,1,0:T(8,128)(2,1)S(1)} %slice.8), channel_id=1, source_target_pairs={{0,32},{32,64},{64,96},{96,128},{128,160},{160,192},{192,224},{224... | collective-permute-start | bytes 442376 | tf_op jit(solution)/shard_map/ppermute | solution.py:319
  95.1 5.1 %collective-permute-start.7 = (bf16[2,96,384]{2,1,0:T(8,128)(2,1)S(1)}, bf16[2,96,384]{2,1,0:T(8,128)(2,1)S(1)}, u32[]{:S(2)}, u32[]{:S(2)}) collective-permute-start(bf16[2,96,384]{2,1,0:T(8,128)(2,1)S(1)} %slice.9), channel_id=1, source_target_pairs={{0,224},{32,0},{64,32},{96,64},{128,96},{160,128},{192,160},{224,1... | collective-permute-start | bytes 442376 | tf_op jit(solution)/shard_map/ppermute | solution.py:319
  100.3 1.3 all-to-all-done.3.got
  101.6 0.4 collective-permute-done.5.refs_4_
  102.0 1.2 collective-permute-done.7.refs_8_
  103.3 0.3 shard_map.153
  103.8 1.9 %collective-permute-start.8 = (bf16[32,96,384]{2,1,0:T(8,128)(2,1)S(1)}, bf16[32,96,384]{2,1,0:T(8,128)(2,1)S(1)}, u32[]{:S(2)}, u32[]{:S(2)}) collective-permute-start(bf16[32,96,384]{2,1,0:T(8,128)(2,1)S(1)} %shard_map.154.own), channel_id=1, source_target_pairs={{0,1},{1,0},{2,3},{3,2},{4,5},{5,4},{6,7},{7,6},{8,9},{9,8},{10,11... | collective-permute-start | bytes 7077896 | tf_op jit(solution)/shard_map/ppermute | solution.py:368
  105.7 13.7 %all_to_all.30.rows = bf16[8,16,1536]{2,1,0:T(8,128)(2,1)S(1)} all-to-all(bf16[8,16,1536]{2,1,0:T(8,128)(2,1)S(1)} %get-tuple-element.69), channel_id=1, replica_groups=mesh['cfg'=2,'z'=8,'pair'=2,'side'=2,'x'=4,'core'=2] {'side','x'}, dimensions={0} | all-to-all | bytes 786432 | tf_op jit(solution)/shard_map/all_to_all | solution.py:367
  119.4 1.4 shard_map.155
  120.8 11.4 %all_to_all.31.got = bf16[8,16,1536]{2,1,0:T(8,128)(2,1)S(1)} all-to-all(bf16[8,16,1536]{2,1,0:T(8,128)(2,1)S(1)} %shard_map.155), channel_id=1, replica_groups=mesh['cfg'=2,'z'=8,'pair'=2,'side'=2,'x'=4,'core'=2] {'side','x'}, dimensions={0} | all-to-all | bytes 786432 | tf_op jit(solution)/shard_map/all_to_all | solution.py:370
  132.2 0.9 shard_map.156
  133.1 3.1 %collective-permute-start.9 = (f32[16,64]{1,0:T(8,128)S(1)}, f32[16,64]{1,0:T(8,128)S(1)}, u32[]{:S(2)}, u32[]{:S(2)}) collective-permute-start(f32[16,64]{1,0:T(8,128)S(1)} %get-tuple-element.75.mine), channel_id=1, source_target_pairs={{0,256},{256,0},{1,257},{257,1},{2,258},{258,2},{3,259},{259,3},{4... | collective-permute-start | bytes 12296 | tf_op jit(solution)/shard_map/ppermute | solution.py:376
  136.9 5.6 %collective-permute-done.9.other = f32[16,64]{1,0:T(8,128)S(1)} collective-permute-done((f32[16,64]{1,0:T(8,128)S(1)}, f32[16,64]{1,0:T(8,128)S(1)}, u32[]{:S(2)}, u32[]{:S(2)}) %collective-permute-start.9) | collective-permute-done | bytes 4128 | tf_op jit(solution)/shard_map/ppermute | solution.py:376
  142.5 0.7 shard_map.157
  (21 shorter events, 0.3 us)
Async XLA Ops:
  2.3 13.8 %all-to-all-start = ((bf16[4,96,384]{2,1,0:T(8,128)(2,1)}), bf16[4,96,384]{2,1,0:T(8,128)(2,1)S(1)}, u32[]{:S(2)}, u32[]{:S(2)}) async-start(bf16[4,96,384]{2,1,0:T(8,128)(2,1)} %shard_map.150), calls=%async_computation | async-start | bytes 589824 | tf_op jit(solution)/shard_map/all_to_all | solution.py:316
  10.0 69.7 %copy-start.2 = (bf16[192,1536]{1,0:T(8,128)(2,1)S(1)}, bf16[192,1536]{1,0:T(8,128)(2,1)}, u32[]{:S(2)}) copy-start(bf16[192,1536]{1,0:T(8,128)(2,1)} %weight.1) | copy-start | bytes 1769476
  16.2 36.3 %all-to-all-start.1 = ((bf16[32,80,128]{2,1,0:T(8,128)(2,1)}), bf16[32,80,128]{2,1,0:T(8,128)(2,1)S(1)}, u32[]{:S(2)}, u32[]{:S(2)}) async-start(bf16[32,80,128]{2,1,0:T(8,128)(2,1)} %get-tuple-element.41), calls=%async_computation.1 | async-start | bytes 1310720 | tf_op jit(solution)/shard_map/all_to_all | solution.py:337
  29.9 73.4 %copy-start = (bf16[1,128,1536]{2,1,0:T(8,128)(2,1)S(1)}, bf16[1,128,1536]{2,1,0:T(8,128)(2,1)}, u32[]{:S(2)}) copy-start(bf16[1,128,1536]{2,1,0:T(8,128)(2,1)} %tokens.1) | copy-start | bytes 1179652
  29.9 73.3 %copy-start.1 = (f32[2,8,1536]{2,1,0:T(8,128)S(1)}, f32[2,8,1536]{2,1,0:T(8,128)}, u32[]{:S(2)}) copy-start(f32[2,8,1536]{2,1,0:T(8,128)} %mods.3) | copy-start | bytes 294916
  29.9 22.5 %collective-permute-start = (bf16[4,96,384]{2,1,0:T(8,128)(2,1)S(1)}, bf16[4,96,384]{2,1,0:T(8,128)(2,1)S(1)}, u32[]{:S(2)}, u32[]{:S(2)}) collective-permute-start(bf16[4,96,384]{2,1,0:T(8,128)(2,1)S(1)} %all-to-all-done.refs_0_), channel_id=1, source_target_pairs={{0,32},{32,64},{64,96},{96,128},{128,160},{160,192},{192,224},{224... | collective-permute-start | bytes 884744 | tf_op jit(solution)/shard_map/ppermute | solution.py:319
  33.4 19.0 %collective-permute-start.1 = (bf16[4,96,384]{2,1,0:T(8,128)(2,1)S(1)}, bf16[4,96,384]{2,1,0:T(8,128)(2,1)S(1)}, u32[]{:S(2)}, u32[]{:S(2)}) collective-permute-start(bf16[4,96,384]{2,1,0:T(8,128)(2,1)S(1)} %all-to-all-done.refs_0_), channel_id=1, source_target_pairs={{0,224},{32,0},{64,32},{96,64},{128,96},{160,128},{192,160},{224,1... | collective-permute-start | bytes 884744 | tf_op jit(solution)/shard_map/ppermute | solution.py:319
  56.6 23.1 %all-to-all-start.2 = ((bf16[32,32,128]{2,1,0:T(8,128)(2,1)}), bf16[32,32,128]{2,1,0:T(8,128)(2,1)S(1)}, u32[]{:S(2)}, u32[]{:S(2)}) async-start(bf16[32,32,128]{2,1,0:T(8,128)(2,1)} %shard_map.151), calls=%async_computation.2 | async-start | bytes 524288 | tf_op jit(solution)/shard_map/all_to_all | solution.py:342
  64.5 15.2 %collective-permute-start.2 = (bf16[4,96,384]{2,1,0:T(8,128)(2,1)S(1)}, bf16[4,96,384]{2,1,0:T(8,128)(2,1)S(1)}, u32[]{:S(2)}, u32[]{:S(2)}) collective-permute-start(bf16[4,96,384]{2,1,0:T(8,128)(2,1)S(1)} %collective-permute-done.refs_1_), channel_id=1, source_target_pairs={{0,32},{32,64},{64,96},{96,128},{128,160},{160,192},{192,224},{224... | collective-permute-start | bytes 884744 | tf_op jit(solution)/shard_map/ppermute | solution.py:319
  67.9 11.8 %collective-permute-start.3 = (bf16[4,96,384]{2,1,0:T(8,128)(2,1)S(1)}, bf16[4,96,384]{2,1,0:T(8,128)(2,1)S(1)}, u32[]{:S(2)}, u32[]{:S(2)}) collective-permute-start(bf16[4,96,384]{2,1,0:T(8,128)(2,1)S(1)} %collective-permute-done.1.refs_5_), channel_id=1, source_target_pairs={{0,224},{32,0},{64,32},{96,64},{128,96},{160,128},{192,160},{224,1... | collective-permute-start | bytes 884744 | tf_op jit(solution)/shard_map/ppermute | solution.py:319
  81.3 11.9 %collective-permute-start.4 = (bf16[4,96,384]{2,1,0:T(8,128)(2,1)S(1)}, bf16[4,96,384]{2,1,0:T(8,128)(2,1)S(1)}, u32[]{:S(2)}, u32[]{:S(2)}) collective-permute-start(bf16[4,96,384]{2,1,0:T(8,128)(2,1)S(1)} %collective-permute-done.2.refs_2_), channel_id=1, source_target_pairs={{0,32},{32,64},{64,96},{96,128},{128,160},{160,192},{192,224},{224... | collective-permute-start | bytes 884744 | tf_op jit(solution)/shard_map/ppermute | solution.py:319
  84.0 11.1 %collective-permute-start.6 = (bf16[4,96,384]{2,1,0:T(8,128)(2,1)S(1)}, bf16[4,96,384]{2,1,0:T(8,128)(2,1)S(1)}, u32[]{:S(2)}, u32[]{:S(2)}) collective-permute-start(bf16[4,96,384]{2,1,0:T(8,128)(2,1)S(1)} %collective-permute-done.3.refs_6_), channel_id=1, source_target_pairs={{0,224},{32,0},{64,32},{96,64},{128,96},{160,128},{192,160},{224,1... | collective-permute-start | bytes 884744 | tf_op jit(solution)/shard_map/ppermute | solution.py:319
  88.3 13.3 %all-to-all-start.3 = ((bf16[8,16,1536]{2,1,0:T(8,128)(2,1)}), bf16[8,16,1536]{2,1,0:T(8,128)(2,1)S(1)}, u32[]{:S(2)}, u32[]{:S(2)}) async-start(bf16[8,16,1536]{2,1,0:T(8,128)(2,1)} %shard_map.152), calls=%async_computation.3 | async-start | bytes 786432 | tf_op jit(solution)/shard_map/all_to_all | solution.py:350
  93.2 8.9 %collective-permute-start.5 = (bf16[2,96,384]{2,1,0:T(8,128)(2,1)S(1)}, bf16[2,96,384]{2,1,0:T(8,128)(2,1)S(1)}, u32[]{:S(2)}, u32[]{:S(2)}) collective-permute-start(bf16[2,96,384]{2,1,0:T(8,128)(2,1)S(1)} %slice.8), channel_id=1, source_target_pairs={{0,32},{32,64},{64,96},{96,128},{128,160},{160,192},{192,224},{224... | collective-permute-start | bytes 442376 | tf_op jit(solution)/shard_map/ppermute | solution.py:319
  95.1 8.1 %collective-permute-start.7 = (bf16[2,96,384]{2,1,0:T(8,128)(2,1)S(1)}, bf16[2,96,384]{2,1,0:T(8,128)(2,1)S(1)}, u32[]{:S(2)}, u32[]{:S(2)}) collective-permute-start(bf16[2,96,384]{2,1,0:T(8,128)(2,1)S(1)} %slice.9), channel_id=1, source_target_pairs={{0,224},{32,0},{64,32},{96,64},{128,96},{160,128},{192,160},{224,1... | collective-permute-start | bytes 442376 | tf_op jit(solution)/shard_map/ppermute | solution.py:319
  103.8 15.6 %collective-permute-start.8 = (bf16[32,96,384]{2,1,0:T(8,128)(2,1)S(1)}, bf16[32,96,384]{2,1,0:T(8,128)(2,1)S(1)}, u32[]{:S(2)}, u32[]{:S(2)}) collective-permute-start(bf16[32,96,384]{2,1,0:T(8,128)(2,1)S(1)} %shard_map.154.own), channel_id=1, source_target_pairs={{0,1},{1,0},{2,3},{3,2},{4,5},{5,4},{6,7},{7,6},{8,9},{9,8},{10,11... | collective-permute-start | bytes 7077896 | tf_op jit(solution)/shard_map/ppermute | solution.py:368
  119.4 12.8 %copy-start.3 = (bf16[1536,64]{0,1:T(8,128)(2,1)S(1)}, bf16[1536,64]{0,1:T(8,128)(2,1)}, u32[]{:S(2)}) copy-start(bf16[1536,64]{0,1:T(8,128)(2,1)} %param.21) | copy-start | bytes 589828
  119.4 23.1 %copy-start.4 = (f32[16,32]{1,0:T(8,128)S(1)}, f32[16,32]{1,0:T(8,128)}, u32[]{:S(2)}) copy-start(f32[16,32]{1,0:T(8,128)} %latent.1) | copy-start | bytes 6148
  119.4 23.1 %copy-start.5 = (f32[8,128]{1,0:T(8,128)S(1)}, f32[8,128]{1,0:T(8,128)}, u32[]{:S(2)}) copy-start(f32[8,128]{1,0:T(8,128)} %get-tuple-element.74.alphas) | copy-start | bytes 12292
  133.1 9.4 %collective-permute-start.9 = (f32[16,64]{1,0:T(8,128)S(1)}, f32[16,64]{1,0:T(8,128)S(1)}, u32[]{:S(2)}, u32[]{:S(2)}) collective-permute-start(f32[16,64]{1,0:T(8,128)S(1)} %get-tuple-element.75.mine), channel_id=1, source_target_pairs={{0,256},{256,0},{1,257},{257,1},{2,258},{258,2},{3,259},{259,3},{4... | collective-permute-start | bytes 12296 | tf_op jit(solution)/shard_map/ppermute | solution.py:376

commit v8 on v6

--- a/solution.py
+++ b/solution.py
@@ -49,6 +49,13 @@
     return table
 
 
+def index_of(axes):
+    index = 0
+    for axis in axes:
+        index = index * lax.axis_size(axis) + lax.axis_index(axis)
+    return index
+
+
 def layer_norm(values, epsilon):
     centered = values - jnp.mean(values, -1, keepdims=True)
     spread = jnp.mean(centered * centered, -1, keepdims=True)
@@ -59,7 +66,7 @@
     return lambda row: jnp.where(video, mods[1, row : row + 1, :], mods[0, row : row + 1, :])
 
 
-def project_kernel(place, text, step, tokens_far, mods_far, gain_far, positions_far, table_far, qkv_far, out, alphas, *scratch):
+def project_kernel(text, step, tokens_far, mods_far, gain_far, positions_far, table_far, qkv_far, out, alphas, *scratch):
     tokens, mods, gain, positions, table, qkv, arrived = scratch
     far = (tokens_far, mods_far, gain_far, positions_far, table_far, qkv_far)
     copies = [pltpu.make_async_copy(a, b, arrived.at[i]) for i, (a, b) in enumerate(zip(far, scratch))]
@@ -69,7 +76,7 @@
     alphas[...] = jnp.where(row == 0, alpha_bar(step[0]), alpha_bar(step[0] - STRIDE))
     for copy in copies[:5]:
         copy.wait()
-    ids = place[0] * TOK + lax.broadcasted_iota(jnp.int32, (TOK, 1), 0)
+    ids = index_of(SEQ_AXES) * TOK + lax.broadcasted_iota(jnp.int32, (TOK, 1), 0)
     video = ids >= text[0]
     pick = picker(mods, video)
     residual = tokens[0].astype(F32)
@@ -187,8 +194,8 @@
     out[...] = total.astype(BF16).reshape(BLK, OWN, D)
 
 
-def own_video(place, part, text):
-    ids = place[0] * TOK + part[0] * OWN + lax.broadcasted_iota(jnp.int32, (OWN, 1), 0)
+def own_video(text):
+    ids = index_of(SEQ_AXES) * TOK + index_of(BLK_AXES) * OWN + lax.broadcasted_iota(jnp.int32, (OWN, 1), 0)
     return ids >= text[0]
 
 
@@ -199,9 +206,9 @@
     return total
 
 
-def after_attention_kernel(place, part, text, got, tokens, mods, after, out):
-    pick = picker(mods, own_video(place, part, text))
-    residual = tokens[0, pl.ds(pl.multiple_of(part[0] * OWN, OWN), OWN), :].astype(F32)
+def after_attention_kernel(text, got, tokens, mods, after, out):
+    pick = picker(mods, own_video(text))
+    residual = tokens[0, pl.ds(pl.multiple_of(index_of(BLK_AXES) * OWN, OWN), OWN), :].astype(F32)
     summed = residual + pick(2) * sum_blocks(got)
     after[...] = summed
     normed = (layer_norm(summed, 1e-05) * (1.0 + pick(4)) + pick(3)).astype(BF16)
@@ -235,8 +242,8 @@
         copy.wait()
 
 
-def predict_kernel(place, part, text, got, after, mods, weight, hidden_out, predicted):
-    pick = picker(mods, own_video(place, part, text))
+def predict_kernel(text, got, after, mods, weight, hidden_out, predicted):
+    pick = picker(mods, own_video(text))
     after_mlp = after[...] + pick(5) * sum_blocks(got)
     hidden_out[0] = after_mlp.astype(BF16)
     normed = (layer_norm(after_mlp, 1e-05) * (1.0 + pick(7)) + pick(6)).astype(BF16)
@@ -252,9 +259,9 @@
     return jnp.exp(jnp.sum(jnp.sum(kept, 1, keepdims=True), 0, keepdims=True))
 
 
-def step_kernel(branch, guidance, alphas, mine, other, latent, out):
+def step_kernel(guidance, alphas, mine, other, latent, out):
     alpha_now, alpha_prev = alphas[0:1, 0:1], alphas[1:2, 0:1]
-    is_cond = branch[0] == 0
+    is_cond = lax.axis_index("cfg") == 0
     own, partner = mine[...], other[...]
     cond = jnp.where(is_cond, own, partner)
     uncond = jnp.where(is_cond, partner, own)
@@ -267,7 +274,7 @@
     out[...] = jnp.sqrt(alpha_prev) * clean + jnp.sqrt(1.0 - alpha_prev) * noise
 
 
-ALONE = 60
+ALONE = 63
 
 
 def call(kernel, specs, shapes, mib=24, scratch=()):
@@ -297,8 +304,6 @@
     step_index,
     guidance,
 ):
-    branch, place, part = (lax.axis_index(axes).reshape(1) for axes in ("cfg", SEQ_AXES, BLK_AXES))
-
     pieces = call(
         pieces_kernel,
         [HBM, HBM],
@@ -310,7 +315,7 @@
 
     sent, alphas = call(
         project_kernel,
-        [SMEM, SMEM, SMEM] + [HBM] * 6,
+        [SMEM, SMEM] + [HBM] * 6,
         (jax.ShapeDtypeStruct((SEQ, 80, 128), BF16), jax.ShapeDtypeStruct((8, 128), F32)),
         mib=ALONE,
         scratch=[
@@ -322,8 +327,8 @@
             pltpu.VMEM((3, 192, D), BF16),
             pltpu.SemaphoreType.DMA((6,)),
         ],
-    )(place, text_count, step_index, tokens_in, modulation, qk_gain, positions, jnp.asarray(frequencies()), qkv_weight)
-    sent, pieces, branch, part = lax.optimization_barrier((sent, pieces, branch, part))
+    )(text_count, step_index, tokens_in, modulation, qk_gain, positions, jnp.asarray(frequencies()), qkv_weight)
+    sent, pieces = lax.optimization_barrier((sent, pieces))
     weights = lax.all_gather(pieces, "z", axis=0, tiled=True)
     got = lax.all_to_all(sent, SEQ_AXES, 0, 0, tiled=True)
     attended = call(attend_kernel, [VMEM], jax.ShapeDtypeStruct((SEQ, 32, 128), BF16))(got)
@@ -334,9 +339,9 @@
     partial = lax.all_to_all(partial, BLK_AXES, 0, 0, tiled=True)
     after, rows = call(
         after_attention_kernel,
-        [SMEM, SMEM, SMEM, VMEM, VMEM, VMEM],
+        [SMEM, VMEM, VMEM, VMEM],
         (jax.ShapeDtypeStruct((OWN, D), F32), shared),
-    )(place, part, text_count, partial, tokens_in, modulation)
+    )(text_count, partial, tokens_in, modulation)
     rows, weights = lax.optimization_barrier((rows, weights))
     rows = lax.all_to_all(rows, SHARERS, 0, 0, tiled=True)
     swapped = lax.ppermute(weights, "core", [(0, 1), (1, 0)])
@@ -344,15 +349,15 @@
     mlp = lax.all_to_all(mlp, SHARERS, 0, 0, tiled=True)
     hidden_out, predicted = call(
         predict_kernel,
-        [SMEM, SMEM, SMEM, VMEM, VMEM, VMEM, VMEM],
+        [SMEM, VMEM, VMEM, VMEM, VMEM],
         (jax.ShapeDtypeStruct((1, OWN, D), BF16), jax.ShapeDtypeStruct((OWN, 64), F32)),
-    )(place, part, text_count, mlp, after, modulation, proj_weight.T)
+    )(text_count, mlp, after, modulation, proj_weight.T)
     partner = lax.ppermute(predicted, "cfg", [(0, 1), (1, 0)])
     latent_prev = call(
         step_kernel,
-        [SMEM, SMEM, VMEM, VMEM, VMEM, VMEM],
+        [SMEM, VMEM, VMEM, VMEM, VMEM],
         jax.ShapeDtypeStruct((OWN, 32), F32),
-    )(branch, guidance, alphas, predicted, partner, latent)
+    )(guidance, alphas, predicted, partner, latent)
     return (hidden_out, latent_prev)
 
 

time: 138 us -> 138 us (level)
  no operation moved by 1% of the time
where the time goes in v8:
time: 138 us
  blocking collectives  86.6 us (63%)
  between operations  16.1 us (12%)
  Pallas kernels  13.4 us (10%)
  starting transfers between devices  11.4 us (8%)
  waiting for transfers between devices  7.72 us (6%)
  local copies, waits for them, and re-layouts  2.42 us (2%)
    all_to_all x1, blocking collectives, body(): got = lax.all_to_all(sent, SEQ_AXES, 0, 0, tiled=True)  34.4 us
    all_to_all x1, blocking collectives, body(): back = lax.all_to_all(attended, SEQ_AXES, 0, 0, tiled=True)  16 us
    all_to_all x1, blocking collectives, body(): partial = lax.all_to_all(partial, BLK_AXES, 0, 0, tiled=True)  13 us
    all_to_all x1, blocking collectives, body(): rows = lax.all_to_all(rows, SHARERS, 0, 0, tiled=True)  11.7 us
    all_to_all x1, blocking collectives, body(): mlp = lax.all_to_all(mlp, SHARERS, 0, 0, tiled=True)  11.4 us
    all_to_all x1, starting transfers between devices, body(): pieces = lax.all_to_all(pieces, LINE, 0, 0, tiled=True)  6.35 us
    ppermute x1, waiting for transfers between devices, body(): partner = lax.ppermute(predicted, 'cfg', [(0, 1), (1, 0)])  5.63 us
    pallas_call x1, Pallas kernels, body(): call(project_kernel, [SMEM, SMEM] + [HBM] * 6, (jax.ShapeDtypeStruct((SEQ...  4.12 us
  transfers between devices with their start and end apart: 4, of which 2 were waited for; matrix products, arithmetic and copies ran while one was open for 0% of the time, Pallas kernels for 6%

profile of v8, /device:TPU:56, one launch (start us, length us, event | category | flops | bytes accessed | tf_op | source)
XLA Modules:
  0.0 137.6 jit_solution(10860922672290808487)
XLA Ops:
  7.2 1.7 %shard_map.150 = bf16[4,96,384]{2,1,0:T(8,128)(2,1)} custom-call(bf16[48,768]{1,0:T(8,128)(2,1)} %up.1, bf16[48,768]{1,0:T(8,128)(2,1)} %bitcast.3), custom_call_target="tpu_custom_call" | custom-call | flops 10000000 | bytes 4000000 | tf_op jit(solution)/shard_map/pallas_call | solution.py:307
  8.8 6.4 %all-to-all-start = ((bf16[4,96,384]{2,1,0:T(8,128)(2,1)}), bf16[4,96,384]{2,1,0:T(8,128)(2,1)S(1)}, u32[]{:S(2)}, u32[]{:S(2)}) async-start(bf16[4,96,384]{2,1,0:T(8,128)(2,1)} %shard_map.150), calls=%async_computation | async-start | bytes 589824 | tf_op jit(solution)/shard_map/all_to_all | solution.py:314
  15.2 0.0 all-gather.2.cloned.1.call-start
  16.5 0.0 copy-start.3
  16.5 4.1 %shard_map.149 = (bf16[32,80,128]{2,1,0:T(8,128)(2,1)}, f32[8,128]{1,0:T(8,128)}) custom-call(s32[1]{0:T(128)S(6)} %copy.16.text, s32[1]{0:T(128)S(6)} %copy.17.step, bf16[1,128,1536]{2,1,0:T(8,128)(2,1)} %tokens.1, f32[2,8,1536]{2,1,0:T(8,128)} %mods.3, f32[2,64]{1,0:T(2,128)} %gain_far.1, s32[3,128]{1,0:T(4,128)} %positions_far.1, ...), custom_call_target="tpu_custom_call" | custom-call | flops 10000000 | bytes 4000000 | tf_op jit(solution)/shard_map/pallas_call | solution.py:316
  20.6 2.0 %all-to-all-done = bf16[4,96,384]{2,1,0:T(8,128)(2,1)S(1)} async-done(((bf16[4,96,384]{2,1,0:T(8,128)(2,1)}), bf16[4,96,384]{2,1,0:T(8,128)(2,1)S(1)}, u32[]{:S(2)}, u32[]{:S(2)}) %all-to-all-start) | async-done | bytes 294944 | tf_op jit(solution)/shard_map/all_to_all | solution.py:314
  22.7 0.7 copy-done.7
  23.4 0.0 all-gather.2.cloned.1.call-update
  23.4 0.0 copy-start.1
  23.4 0.0 copy-start.2
  23.5 34.4 %all_to_all.30.got = bf16[32,80,128]{2,1,0:T(8,128)(2,1)S(1)} all-to-all(bf16[32,80,128]{2,1,0:T(8,128)(2,1)} %get-tuple-element.13), channel_id=1, replica_groups=mesh['cfg'=2,'z'=8,'pair'=2,'side'=2,'x'=4,'core'=2] {'z','pair','side'}, dimensions={0} | all-to-all | bytes 1310720 | tf_op jit(solution)/shard_map/all_to_all | solution.py:333
  57.9 3.5 %shard_map.151 = bf16[32,32,128]{2,1,0:T(8,128)(2,1)S(1)} custom-call(bf16[32,80,128]{2,1,0:T(8,128)(2,1)S(1)} %all_to_all.30.got), custom_call_target="tpu_custom_call" | custom-call | flops 10000000 | bytes 4000000 | tf_op jit(solution)/shard_map/pallas_call | solution.py:334
  61.3 16.0 %all_to_all.31.got = bf16[32,32,128]{2,1,0:T(8,128)(2,1)S(1)} all-to-all(bf16[32,32,128]{2,1,0:T(8,128)(2,1)S(1)} %shard_map.151), channel_id=1, replica_groups=mesh['cfg'=2,'z'=8,'pair'=2,'side'=2,'x'=4,'core'=2] {'z','pair','side'}, dimensions={0} | all-to-all | bytes 524288 | tf_op jit(solution)/shard_map/all_to_all | solution.py:335
  77.4 0.0 copy-done.3
  77.4 0.9 shard_map.152
  78.3 13.0 %all_to_all.32.got = bf16[8,16,1536]{2,1,0:T(8,128)(2,1)S(1)} all-to-all(bf16[8,16,1536]{2,1,0:T(8,128)(2,1)S(1)} %shard_map.152), channel_id=1, replica_groups=mesh['cfg'=2,'z'=8,'pair'=2,'side'=2,'x'=4,'core'=2] {'x','core'}, dimensions={0} | all-to-all | bytes 786432 | tf_op jit(solution)/shard_map/all_to_all | solution.py:339
  91.3 0.0 copy-done.1
  91.3 0.0 copy-done.2
  91.3 0.3 shard_map.153
  91.6 0.0 all-gather.2.cloned.1.call-done.own
  91.6 1.9 %collective-permute-start = (bf16[32,96,384]{2,1,0:T(8,128)(2,1)}, bf16[32,96,384]{2,1,0:T(8,128)(2,1)S(1)}, u32[]{:S(2)}, u32[]{:S(2)}) collective-permute-start(bf16[32,96,384]{2,1,0:T(8,128)(2,1)} %all-gather.2.cloned.1.call-done.own), channel_id=1, source_target_pairs={{0,1},{1,0},{2,3},{3,2},{4,5},{5,4},{6,7},{7,6},{8,9},{9,8},{10,11... | collective-permute-start | bytes 7077896 | tf_op jit(solution)/shard_map/ppermute | solution.py:347
  93.5 11.7 %all_to_all.33.rows = bf16[8,16,1536]{2,1,0:T(8,128)(2,1)S(1)} all-to-all(bf16[8,16,1536]{2,1,0:T(8,128)(2,1)S(1)} %get-tuple-element.16), channel_id=1, replica_groups=mesh['cfg'=2,'z'=8,'pair'=2,'side'=2,'x'=4,'core'=2] {'side','x'}, dimensions={0} | all-to-all | bytes 786432 | tf_op jit(solution)/shard_map/all_to_all | solution.py:346
  105.2 0.0 collective-permute-done.other
  105.2 1.7 %copy-done = bf16[32,96,384]{2,1,0:T(8,128)(2,1)S(1)} copy-done((bf16[32,96,384]{2,1,0:T(8,128)(2,1)S(1)}, bf16[32,96,384]{2,1,0:T(8,128)(2,1)}, u32[]{:S(2)}) %copy-start) | copy-done | bytes 2359320
  106.9 1.4 %shard_map.154 = bf16[8,16,1536]{2,1,0:T(8,128)(2,1)S(1)} custom-call(bf16[8,16,1536]{2,1,0:T(8,128)(2,1)S(1)} %all_to_all.33.rows, bf16[32,96,384]{2,1,0:T(8,128)(2,1)S(1)} %copy-done, bf16[32,96,384]{2,1,0:T(8,128)(2,1)S(1)} %collective-permute-done.other), custom_call_target="tpu_custom_call" | custom-call | flops 10000000 | bytes 4000000 | tf_op jit(solution)/shard_map/pallas_call | solution.py:348
  108.3 11.4 %all_to_all.34.got = bf16[8,16,1536]{2,1,0:T(8,128)(2,1)S(1)} all-to-all(bf16[8,16,1536]{2,1,0:T(8,128)(2,1)S(1)} %shard_map.154), channel_id=1, replica_groups=mesh['cfg'=2,'z'=8,'pair'=2,'side'=2,'x'=4,'core'=2] {'side','x'}, dimensions={0} | all-to-all | bytes 786432 | tf_op jit(solution)/shard_map/all_to_all | solution.py:349
  119.7 0.0 copy-done.4
  119.7 0.9 shard_map.155
  120.6 3.2 %collective-permute-start.1 = (f32[16,64]{1,0:T(8,128)S(1)}, f32[16,64]{1,0:T(8,128)S(1)}, u32[]{:S(2)}, u32[]{:S(2)}) collective-permute-start(f32[16,64]{1,0:T(8,128)S(1)} %get-tuple-element.21.mine), channel_id=1, source_target_pairs={{0,256},{256,0},{1,257},{257,1},{2,258},{258,2},{3,259},{259,3},{4... | collective-permute-start | bytes 12296 | tf_op jit(solution)/shard_map/ppermute | solution.py:355
  124.4 5.6 %collective-permute-done.1.other = f32[16,64]{1,0:T(8,128)S(1)} collective-permute-done((f32[16,64]{1,0:T(8,128)S(1)}, f32[16,64]{1,0:T(8,128)S(1)}, u32[]{:S(2)}, u32[]{:S(2)}) %collective-permute-start.1) | collective-permute-done | bytes 4128 | tf_op jit(solution)/shard_map/ppermute | solution.py:355
  130.0 0.0 copy-done.5
  130.1 0.7 shard_map.156
  (6 shorter events, 0.0 us)
Async XLA Ops:
  8.8 13.8 %all-to-all-start = ((bf16[4,96,384]{2,1,0:T(8,128)(2,1)}), bf16[4,96,384]{2,1,0:T(8,128)(2,1)S(1)}, u32[]{:S(2)}, u32[]{:S(2)}) async-start(bf16[4,96,384]{2,1,0:T(8,128)(2,1)} %shard_map.150), calls=%async_computation | async-start | bytes 589824 | tf_op jit(solution)/shard_map/all_to_all | solution.py:314
  15.2 76.4 %all-gather.2.cloned.1.call-start = ((), (), s32[]{:S(2)}) async-start(), calls=%async_computation.6 | async-start | bytes 2654208 | tf_op jit(solution)/shard_map/all_gather | solution.py:332
  16.5 60.9 %copy-start.3 = (bf16[192,1536]{1,0:T(8,128)(2,1)S(1)}, bf16[192,1536]{1,0:T(8,128)(2,1)}, u32[]{:S(2)}) copy-start(bf16[192,1536]{1,0:T(8,128)(2,1)} %weight.1) | copy-start | bytes 1769476
  22.7 0.7 copy-start.7
  23.4 67.9 %copy-start.1 = (bf16[1,128,1536]{2,1,0:T(8,128)(2,1)S(1)}, bf16[1,128,1536]{2,1,0:T(8,128)(2,1)}, u32[]{:S(2)}) copy-start(bf16[1,128,1536]{2,1,0:T(8,128)(2,1)} %tokens.1) | copy-start | bytes 1179652
  23.4 67.8 %copy-start.2 = (f32[2,8,1536]{2,1,0:T(8,128)S(1)}, f32[2,8,1536]{2,1,0:T(8,128)}, u32[]{:S(2)}) copy-start(f32[2,8,1536]{2,1,0:T(8,128)} %mods.3) | copy-start | bytes 294916
  91.6 13.6 %collective-permute-start = (bf16[32,96,384]{2,1,0:T(8,128)(2,1)}, bf16[32,96,384]{2,1,0:T(8,128)(2,1)S(1)}, u32[]{:S(2)}, u32[]{:S(2)}) collective-permute-start(bf16[32,96,384]{2,1,0:T(8,128)(2,1)} %all-gather.2.cloned.1.call-done.own), channel_id=1, source_target_pairs={{0,1},{1,0},{2,3},{3,2},{4,5},{5,4},{6,7},{7,6},{8,9},{9,8},{10,11... | collective-permute-start | bytes 7077896 | tf_op jit(solution)/shard_map/ppermute | solution.py:347
  105.2 1.7 %copy-start = (bf16[32,96,384]{2,1,0:T(8,128)(2,1)S(1)}, bf16[32,96,384]{2,1,0:T(8,128)(2,1)}, u32[]{:S(2)}) copy-start(bf16[32,96,384]{2,1,0:T(8,128)(2,1)} %all-gather.2.cloned.1.call-done.own) | copy-start | bytes 7077892
  106.9 12.8 %copy-start.4 = (bf16[1536,64]{0,1:T(8,128)(2,1)S(1)}, bf16[1536,64]{0,1:T(8,128)(2,1)}, u32[]{:S(2)}) copy-start(bf16[1536,64]{0,1:T(8,128)(2,1)} %param.21) | copy-start | bytes 589828
  106.9 23.1 %copy-start.5 = (f32[16,32]{1,0:T(8,128)S(1)}, f32[16,32]{1,0:T(8,128)}, u32[]{:S(2)}) copy-start(f32[16,32]{1,0:T(8,128)} %latent.1) | copy-start | bytes 6148
  106.9 23.1 %copy-start.6 = (f32[8,128]{1,0:T(8,128)S(1)}, f32[8,128]{1,0:T(8,128)}, u32[]{:S(2)}) copy-start(f32[8,128]{1,0:T(8,128)} %get-tuple-element.20.alphas) | copy-start | bytes 12292
  120.6 9.4 %collective-permute-start.1 = (f32[16,64]{1,0:T(8,128)S(1)}, f32[16,64]{1,0:T(8,128)S(1)}, u32[]{:S(2)}, u32[]{:S(2)}) collective-permute-start(f32[16,64]{1,0:T(8,128)S(1)} %get-tuple-element.21.mine), channel_id=1, source_target_pairs={{0,256},{256,0},{1,257},{257,1},{2,258},{258,2},{3,259},{259,3},{4... | collective-permute-start | bytes 12296 | tf_op jit(solution)/shard_map/ppermute | solution.py:355
Sparse Core Ops, SparseCore 0:
  23.6 62.0 all-gather.1

commit v9 on v8

--- a/solution.py
+++ b/solution.py
@@ -206,7 +206,9 @@
     return total
 
 
-def after_attention_kernel(text, got, tokens, mods, after, out):
+def after_attention_kernel(text, got, tokens, mods, weights, after, out, own, arrived):
+    fetch = pltpu.make_async_copy(weights, own, arrived)
+    fetch.start()
     pick = picker(mods, own_video(text))
     residual = tokens[0, pl.ds(pl.multiple_of(index_of(BLK_AXES) * OWN, OWN), OWN), :].astype(F32)
     summed = residual + pick(2) * sum_blocks(got)
@@ -214,6 +216,7 @@
     normed = (layer_norm(summed, 1e-05) * (1.0 + pick(4)) + pick(3)).astype(BF16)
     for block in range(GROUP):
         out[block] = normed
+    fetch.wait()
 
 
 def feed_forward_kernel(rows, own, other, out):
@@ -337,15 +340,17 @@
     shared = jax.ShapeDtypeStruct((GROUP, OWN, D), BF16)
     partial = call(out_project_kernel, [VMEM, VMEM], blocks)(back, out_weight)
     partial = lax.all_to_all(partial, BLK_AXES, 0, 0, tiled=True)
-    after, rows = call(
+    partial, weights = lax.optimization_barrier((partial, weights))
+    after, rows, own = call(
         after_attention_kernel,
-        [SMEM, VMEM, VMEM, VMEM],
-        (jax.ShapeDtypeStruct((OWN, D), F32), shared),
-    )(text_count, partial, tokens_in, modulation)
-    rows, weights = lax.optimization_barrier((rows, weights))
+        [SMEM, VMEM, VMEM, VMEM, HBM],
+        (jax.ShapeDtypeStruct((OWN, D), F32), shared, jax.ShapeDtypeStruct((SEQ, 2 * PIECE, UNITS), BF16)),
+        mib=50,
+        scratch=[pltpu.SemaphoreType.DMA],
+    )(text_count, partial, tokens_in, modulation, weights)
     rows = lax.all_to_all(rows, SHARERS, 0, 0, tiled=True)
     swapped = lax.ppermute(weights, "core", [(0, 1), (1, 0)])
-    mlp = call(feed_forward_kernel, [VMEM, VMEM, VMEM], shared)(rows, weights, swapped)
+    mlp = call(feed_forward_kernel, [VMEM, VMEM, VMEM], shared)(rows, own, swapped)
     mlp = lax.all_to_all(mlp, SHARERS, 0, 0, tiled=True)
     hidden_out, predicted = call(
         predict_kernel,

time: 138 us -> 138 us (level)
  local copies, waits for them, and re-layouts: 2.42 us -> 0.74 us
  Pallas kernels: 13.4 us -> 14.8 us
    unnamed x16 -> x14, local copies, waits for them, and re-layouts: 2.42 us -> 0.74 us
    pallas_call x2, Pallas kernels: 1.67 us -> 3.06 us  [the longest x1 1.7 us: body(): call(after_attention_kernel, [SMEM, VMEM, VMEM, VMEM, HBM], (jax.ShapeDty...]
  transfers between devices with their start and end apart: 4 -> 4, of which waited for: 2 -> 2; matrix products, arithmetic and copies ran while one was open for 0% -> 0% of each run, Pallas kernels for 6% -> 7%
where the time goes in v9:
time: 138 us; the launch traced here: 137 us
  blocking collectives  86.6 us (63%)
  between operations  16.1 us (12%)
  Pallas kernels  14.8 us (11%)
  starting transfers between devices  11.4 us (8%)
  waiting for transfers between devices  7.72 us (6%)
    all_to_all x1, blocking collectives, body(): got = lax.all_to_all(sent, SEQ_AXES, 0, 0, tiled=True)  34.4 us
    all_to_all x1, blocking collectives, body(): back = lax.all_to_all(attended, SEQ_AXES, 0, 0, tiled=True)  16 us
    all_to_all x1, blocking collectives, body(): partial = lax.all_to_all(partial, BLK_AXES, 0, 0, tiled=True)  13 us
    all_to_all x1, blocking collectives, body(): rows = lax.all_to_all(rows, SHARERS, 0, 0, tiled=True)  11.7 us
    all_to_all x1, blocking collectives, body(): mlp = lax.all_to_all(mlp, SHARERS, 0, 0, tiled=True)  11.4 us
    all_to_all x1, starting transfers between devices, body(): pieces = lax.all_to_all(pieces, LINE, 0, 0, tiled=True)  6.35 us
    ppermute x1, waiting for transfers between devices, body(): partner = lax.ppermute(predicted, 'cfg', [(0, 1), (1, 0)])  5.65 us
    pallas_call x1, Pallas kernels, body(): call(project_kernel, [SMEM, SMEM] + [HBM] * 6, (jax.ShapeDtypeStruct((SEQ...  4.12 us
  transfers between devices with their start and end apart: 4, of which 2 were waited for; matrix products, arithmetic and copies ran while one was open for 0% of the time, Pallas kernels for 7%

profile of v9, /device:TPU:56, one launch (start us, length us, event | category | flops | bytes accessed | tf_op | source)
XLA Modules:
  0.0 137.3 jit_solution(16273341621682925305)
XLA Ops:
  7.2 1.7 %shard_map.150 = bf16[4,96,384]{2,1,0:T(8,128)(2,1)} custom-call(bf16[48,768]{1,0:T(8,128)(2,1)} %up.1, bf16[48,768]{1,0:T(8,128)(2,1)} %bitcast.3), custom_call_target="tpu_custom_call" | custom-call | flops 10000000 | bytes 4000000 | tf_op jit(solution)/shard_map/pallas_call | solution.py:310
  8.8 6.4 %all-to-all-start = ((bf16[4,96,384]{2,1,0:T(8,128)(2,1)}), bf16[4,96,384]{2,1,0:T(8,128)(2,1)S(1)}, u32[]{:S(2)}, u32[]{:S(2)}) async-start(bf16[4,96,384]{2,1,0:T(8,128)(2,1)} %shard_map.150), calls=%async_computation | async-start | bytes 589824 | tf_op jit(solution)/shard_map/all_to_all | solution.py:317
  15.2 0.0 all-gather.2.cloned.1.call-start
  16.5 0.0 copy-start.2
  16.5 4.1 %shard_map.149 = (bf16[32,80,128]{2,1,0:T(8,128)(2,1)}, f32[8,128]{1,0:T(8,128)}) custom-call(s32[1]{0:T(128)S(6)} %copy.16.text, s32[1]{0:T(128)S(6)} %copy.17.step, bf16[1,128,1536]{2,1,0:T(8,128)(2,1)} %tokens.1, f32[2,8,1536]{2,1,0:T(8,128)} %mods.3, f32[2,64]{1,0:T(2,128)} %gain_far.1, s32[3,128]{1,0:T(4,128)} %positions_far.1, ...), custom_call_target="tpu_custom_call" | custom-call | flops 10000000 | bytes 4000000 | tf_op jit(solution)/shard_map/pallas_call | solution.py:319
  20.6 2.0 %all-to-all-done = bf16[4,96,384]{2,1,0:T(8,128)(2,1)S(1)} async-done(((bf16[4,96,384]{2,1,0:T(8,128)(2,1)}), bf16[4,96,384]{2,1,0:T(8,128)(2,1)S(1)}, u32[]{:S(2)}, u32[]{:S(2)}) %all-to-all-start) | async-done | bytes 294944 | tf_op jit(solution)/shard_map/all_to_all | solution.py:317
  22.7 0.7 copy-done.6
  23.4 0.0 all-gather.2.cloned.1.call-update
  23.4 0.0 copy-start
  23.4 0.0 copy-start.1
  23.4 34.4 %all_to_all.30.got = bf16[32,80,128]{2,1,0:T(8,128)(2,1)S(1)} all-to-all(bf16[32,80,128]{2,1,0:T(8,128)(2,1)} %get-tuple-element.14), channel_id=1, replica_groups=mesh['cfg'=2,'z'=8,'pair'=2,'side'=2,'x'=4,'core'=2] {'z','pair','side'}, dimensions={0} | all-to-all | bytes 1310720 | tf_op jit(solution)/shard_map/all_to_all | solution.py:336
  57.9 3.5 %shard_map.151 = bf16[32,32,128]{2,1,0:T(8,128)(2,1)S(1)} custom-call(bf16[32,80,128]{2,1,0:T(8,128)(2,1)S(1)} %all_to_all.30.got), custom_call_target="tpu_custom_call" | custom-call | flops 10000000 | bytes 4000000 | tf_op jit(solution)/shard_map/pallas_call | solution.py:337
  61.3 16.0 %all_to_all.31.got = bf16[32,32,128]{2,1,0:T(8,128)(2,1)S(1)} all-to-all(bf16[32,32,128]{2,1,0:T(8,128)(2,1)S(1)} %shard_map.151), channel_id=1, replica_groups=mesh['cfg'=2,'z'=8,'pair'=2,'side'=2,'x'=4,'core'=2] {'z','pair','side'}, dimensions={0} | all-to-all | bytes 524288 | tf_op jit(solution)/shard_map/all_to_all | solution.py:338
  77.4 0.0 copy-done.2
  77.4 0.9 shard_map.152
  78.3 13.0 %all_to_all.32.got = bf16[8,16,1536]{2,1,0:T(8,128)(2,1)S(1)} all-to-all(bf16[8,16,1536]{2,1,0:T(8,128)(2,1)S(1)} %shard_map.152), channel_id=1, replica_groups=mesh['cfg'=2,'z'=8,'pair'=2,'side'=2,'x'=4,'core'=2] {'x','core'}, dimensions={0} | all-to-all | bytes 786432 | tf_op jit(solution)/shard_map/all_to_all | solution.py:342
  91.3 0.0 all-gather.2.cloned.1.call-done.weights
  91.3 1.9 %collective-permute-start = (bf16[32,96,384]{2,1,0:T(8,128)(2,1)}, bf16[32,96,384]{2,1,0:T(8,128)(2,1)S(1)}, u32[]{:S(2)}, u32[]{:S(2)}) collective-permute-start(bf16[32,96,384]{2,1,0:T(8,128)(2,1)} %all-gather.2.cloned.1.call-done.weights), channel_id=1, source_target_pairs={{0,1},{1,0},{2,3},{3,2},{4,5},{5,4},{6,7},{7,6},{8,9},{9,8},{10,11... | collective-permute-start | bytes 7077896 | tf_op jit(solution)/shard_map/ppermute | solution.py:352
  93.2 0.0 copy-done
  93.2 0.0 copy-done.1
  93.2 1.7 %shard_map.153 = (f32[16,1536]{1,0:T(8,128)S(1)}, bf16[8,16,1536]{2,1,0:T(8,128)(2,1)S(1)}, bf16[32,96,384]{2,1,0:T(8,128)(2,1)S(1)}) custom-call(s32[1]{0:T(128)S(6)} %copy.16.text, bf16[8,16,1536]{2,1,0:T(8,128)(2,1)S(1)} %all_to_all.32.got, bf16[1,128,1536]{2,1,0:T(8,128)(2,1)S(1)} %copy-done, f32[2,8,1536]{2,1,0:T(8,128)S(1)} %copy-done.1, ...), custom_call_target="tpu_custom_call" | custom-call | flops 10000000 | bytes 4000000 | tf_op jit(solution)/shard_map/pallas_call | solution.py:344
  94.9 11.7 %all_to_all.33.rows = bf16[8,16,1536]{2,1,0:T(8,128)(2,1)S(1)} all-to-all(bf16[8,16,1536]{2,1,0:T(8,128)(2,1)S(1)} %get-tuple-element.18), channel_id=1, replica_groups=mesh['cfg'=2,'z'=8,'pair'=2,'side'=2,'x'=4,'core'=2] {'side','x'}, dimensions={0} | all-to-all | bytes 786432 | tf_op jit(solution)/shard_map/all_to_all | solution.py:351
  106.6 0.0 collective-permute-done.other
  106.6 1.4 shard_map.154
  108.0 11.4 %all_to_all.34.got = bf16[8,16,1536]{2,1,0:T(8,128)(2,1)S(1)} all-to-all(bf16[8,16,1536]{2,1,0:T(8,128)(2,1)S(1)} %shard_map.154), channel_id=1, replica_groups=mesh['cfg'=2,'z'=8,'pair'=2,'side'=2,'x'=4,'core'=2] {'side','x'}, dimensions={0} | all-to-all | bytes 786432 | tf_op jit(solution)/shard_map/all_to_all | solution.py:354
  119.4 0.0 copy-done.3
  119.4 0.9 shard_map.155
  120.3 3.1 %collective-permute-start.1 = (f32[16,64]{1,0:T(8,128)S(1)}, f32[16,64]{1,0:T(8,128)S(1)}, u32[]{:S(2)}, u32[]{:S(2)}) collective-permute-start(f32[16,64]{1,0:T(8,128)S(1)} %get-tuple-element.23.mine), channel_id=1, source_target_pairs={{0,256},{256,0},{1,257},{257,1},{2,258},{258,2},{3,259},{259,3},{4... | collective-permute-start | bytes 12296 | tf_op jit(solution)/shard_map/ppermute | solution.py:360
  124.1 5.6 %collective-permute-done.1.other = f32[16,64]{1,0:T(8,128)S(1)} collective-permute-done((f32[16,64]{1,0:T(8,128)S(1)}, f32[16,64]{1,0:T(8,128)S(1)}, u32[]{:S(2)}, u32[]{:S(2)}) %collective-permute-start.1) | collective-permute-done | bytes 4128 | tf_op jit(solution)/shard_map/ppermute | solution.py:360
  129.8 0.0 copy-done.4
  129.8 0.0 copy-done.5
  129.8 0.7 shard_map.156
  (4 shorter events, 0.0 us)
Async XLA Ops:
  8.8 13.8 %all-to-all-start = ((bf16[4,96,384]{2,1,0:T(8,128)(2,1)}), bf16[4,96,384]{2,1,0:T(8,128)(2,1)S(1)}, u32[]{:S(2)}, u32[]{:S(2)}) async-start(bf16[4,96,384]{2,1,0:T(8,128)(2,1)} %shard_map.150), calls=%async_computation | async-start | bytes 589824 | tf_op jit(solution)/shard_map/all_to_all | solution.py:317
  15.2 76.1 %all-gather.2.cloned.1.call-start = ((), (), s32[]{:S(2)}) async-start(), calls=%async_computation.6 | async-start | bytes 2654208 | tf_op jit(solution)/shard_map/all_gather | solution.py:335
  16.5 60.9 %copy-start.2 = (bf16[192,1536]{1,0:T(8,128)(2,1)S(1)}, bf16[192,1536]{1,0:T(8,128)(2,1)}, u32[]{:S(2)}) copy-start(bf16[192,1536]{1,0:T(8,128)(2,1)} %weight.1) | copy-start | bytes 1769476
  22.7 0.7 copy-start.6
  23.4 69.8 %copy-start = (bf16[1,128,1536]{2,1,0:T(8,128)(2,1)S(1)}, bf16[1,128,1536]{2,1,0:T(8,128)(2,1)}, u32[]{:S(2)}) copy-start(bf16[1,128,1536]{2,1,0:T(8,128)(2,1)} %tokens.1) | copy-start | bytes 1179652
  23.4 69.8 %copy-start.1 = (f32[2,8,1536]{2,1,0:T(8,128)S(1)}, f32[2,8,1536]{2,1,0:T(8,128)}, u32[]{:S(2)}) copy-start(f32[2,8,1536]{2,1,0:T(8,128)} %mods.3) | copy-start | bytes 294916
  91.3 15.3 %collective-permute-start = (bf16[32,96,384]{2,1,0:T(8,128)(2,1)}, bf16[32,96,384]{2,1,0:T(8,128)(2,1)S(1)}, u32[]{:S(2)}, u32[]{:S(2)}) collective-permute-start(bf16[32,96,384]{2,1,0:T(8,128)(2,1)} %all-gather.2.cloned.1.call-done.weights), channel_id=1, source_target_pairs={{0,1},{1,0},{2,3},{3,2},{4,5},{5,4},{6,7},{7,6},{8,9},{9,8},{10,11... | collective-permute-start | bytes 7077896 | tf_op jit(solution)/shard_map/ppermute | solution.py:352
  106.6 12.8 %copy-start.3 = (bf16[1536,64]{0,1:T(8,128)(2,1)S(1)}, bf16[1536,64]{0,1:T(8,128)(2,1)}, u32[]{:S(2)}) copy-start(bf16[1536,64]{0,1:T(8,128)(2,1)} %param.21) | copy-start | bytes 589828
  106.6 23.1 %copy-start.4 = (f32[16,32]{1,0:T(8,128)S(1)}, f32[16,32]{1,0:T(8,128)}, u32[]{:S(2)}) copy-start(f32[16,32]{1,0:T(8,128)} %latent.1) | copy-start | bytes 6148
  106.6 23.1 %copy-start.5 = (f32[8,128]{1,0:T(8,128)S(1)}, f32[8,128]{1,0:T(8,128)}, u32[]{:S(2)}) copy-start(f32[8,128]{1,0:T(8,128)} %get-tuple-element.22.alphas) | copy-start | bytes 12292
  120.3 9.4 %collective-permute-start.1 = (f32[16,64]{1,0:T(8,128)S(1)}, f32[16,64]{1,0:T(8,128)S(1)}, u32[]{:S(2)}, u32[]{:S(2)}) collective-permute-start(f32[16,64]{1,0:T(8,128)S(1)} %get-tuple-element.23.mine), channel_id=1, source_target_pairs={{0,256},{256,0},{1,257},{257,1},{2,258},{258,2},{3,259},{259,3},{4... | collective-permute-start | bytes 12296 | tf_op jit(solution)/shard_map/ppermute | solution.py:360
Sparse Core Ops, SparseCore 0:
  23.5 61.9 all-gather.1

commit v10 on v8

--- a/solution.py
+++ b/solution.py
@@ -216,17 +216,21 @@
         out[block] = normed
 
 
-def feed_forward_kernel(rows, own, other, out):
+def feed_forward_kernel(rows, other, own_far, out, own, arrived):
+    fetch = pltpu.make_async_copy(own_far, own, arrived)
+    fetch.start()
     block = rows[...].reshape(GROUP * OWN, D)
-    result = None
-    for weights in (other, own):
+
+    def term(weights):
         up = weights[:, 0:PIECE, :].reshape(D, UNITS)
         down = weights[:, PIECE : 2 * PIECE, :].reshape(D, UNITS)
         hidden = jnp.dot(block, up, preferred_element_type=F32)
         activated = jax.nn.gelu(hidden, approximate=True).astype(BF16)
-        term = lax.dot_general(activated, down, ROWS_BY_ROWS, preferred_element_type=F32)
-        result = term if result is None else result + term
-    out[...] = result.astype(BF16).reshape(GROUP, OWN, D)
+        return lax.dot_general(activated, down, ROWS_BY_ROWS, preferred_element_type=F32)
+
+    result = term(other)
+    fetch.wait()
+    out[...] = (result + term(own)).astype(BF16).reshape(GROUP, OWN, D)
 
 
 def pieces_kernel(up, down, out, arrived):
@@ -345,7 +349,13 @@
     rows, weights = lax.optimization_barrier((rows, weights))
     rows = lax.all_to_all(rows, SHARERS, 0, 0, tiled=True)
     swapped = lax.ppermute(weights, "core", [(0, 1), (1, 0)])
-    mlp = call(feed_forward_kernel, [VMEM, VMEM, VMEM], shared)(rows, weights, swapped)
+    mlp = call(
+        feed_forward_kernel,
+        [VMEM, VMEM, HBM],
+        shared,
+        mib=50,
+        scratch=[pltpu.VMEM((SEQ, 2 * PIECE, UNITS), BF16), pltpu.SemaphoreType.DMA],
+    )(rows, swapped, weights)
     mlp = lax.all_to_all(mlp, SHARERS, 0, 0, tiled=True)
     hidden_out, predicted = call(
         predict_kernel,

time: 138 us -> 138 us (level)
  Pallas kernels: 13.4 us -> 15.2 us
  local copies, waits for them, and re-layouts: 2.42 us -> 0.74 us
    pallas_call x1, Pallas kernels: 1.4 us -> 3.18 us  [body(): call(feed_forward_kernel, [VMEM, VMEM, HBM], shared, mib=50, scratch=[plt...]
    unnamed x16 -> x14, local copies, waits for them, and re-layouts: 2.42 us -> 0.74 us
where the time goes in v10:
time: 138 us
  blocking collectives  86.6 us (63%)
  between operations  16.1 us (12%)
  Pallas kernels  15.2 us (11%)
  starting transfers between devices  11.4 us (8%)
  waiting for transfers between devices  7.73 us (6%)
    all_to_all x1, blocking collectives, body(): got = lax.all_to_all(sent, SEQ_AXES, 0, 0, tiled=True)  34.4 us
    all_to_all x1, blocking collectives, body(): back = lax.all_to_all(attended, SEQ_AXES, 0, 0, tiled=True)  16 us
    all_to_all x1, blocking collectives, body(): partial = lax.all_to_all(partial, BLK_AXES, 0, 0, tiled=True)  13 us
    all_to_all x1, blocking collectives, body(): rows = lax.all_to_all(rows, SHARERS, 0, 0, tiled=True)  11.7 us
    all_to_all x1, blocking collectives, body(): mlp = lax.all_to_all(mlp, SHARERS, 0, 0, tiled=True)  11.4 us
    all_to_all x1, starting transfers between devices, body(): pieces = lax.all_to_all(pieces, LINE, 0, 0, tiled=True)  6.35 us
    ppermute x1, waiting for transfers between devices, body(): partner = lax.ppermute(predicted, 'cfg', [(0, 1), (1, 0)])  5.64 us
    pallas_call x1, Pallas kernels, body(): call(project_kernel, [SMEM, SMEM] + [HBM] * 6, (jax.ShapeDtypeStruct((SEQ...  4.12 us
  transfers between devices with their start and end apart: 4, of which 2 were waited for; matrix products, arithmetic and copies ran while one was open for 0% of the time, Pallas kernels for 6%

profile of v10, /device:TPU:56, one launch (start us, length us, event | category | flops | bytes accessed | tf_op | source)
XLA Modules:
  0.0 137.7 jit_solution(830093675322053429)
XLA Ops:
  7.2 1.7 %shard_map.150 = bf16[4,96,384]{2,1,0:T(8,128)(2,1)} custom-call(bf16[48,768]{1,0:T(8,128)(2,1)} %up.1, bf16[48,768]{1,0:T(8,128)(2,1)} %bitcast.3), custom_call_target="tpu_custom_call" | custom-call | flops 10000000 | bytes 4000000 | tf_op jit(solution)/shard_map/pallas_call | solution.py:311
  8.8 6.4 %all-to-all-start = ((bf16[4,96,384]{2,1,0:T(8,128)(2,1)}), bf16[4,96,384]{2,1,0:T(8,128)(2,1)S(1)}, u32[]{:S(2)}, u32[]{:S(2)}) async-start(bf16[4,96,384]{2,1,0:T(8,128)(2,1)} %shard_map.150), calls=%async_computation | async-start | bytes 589824 | tf_op jit(solution)/shard_map/all_to_all | solution.py:318
  15.2 0.0 all-gather.2.cloned.1.call-start
  16.5 0.0 copy-start.2
  16.5 4.1 %shard_map.149 = (bf16[32,80,128]{2,1,0:T(8,128)(2,1)}, f32[8,128]{1,0:T(8,128)}) custom-call(s32[1]{0:T(128)S(6)} %copy.16.text, s32[1]{0:T(128)S(6)} %copy.17.step, bf16[1,128,1536]{2,1,0:T(8,128)(2,1)} %tokens.1, f32[2,8,1536]{2,1,0:T(8,128)} %mods.3, f32[2,64]{1,0:T(2,128)} %gain_far.1, s32[3,128]{1,0:T(4,128)} %positions_far.1, ...), custom_call_target="tpu_custom_call" | custom-call | flops 10000000 | bytes 4000000 | tf_op jit(solution)/shard_map/pallas_call | solution.py:320
  20.6 2.0 %all-to-all-done = bf16[4,96,384]{2,1,0:T(8,128)(2,1)S(1)} async-done(((bf16[4,96,384]{2,1,0:T(8,128)(2,1)}), bf16[4,96,384]{2,1,0:T(8,128)(2,1)S(1)}, u32[]{:S(2)}, u32[]{:S(2)}) %all-to-all-start) | async-done | bytes 294944 | tf_op jit(solution)/shard_map/all_to_all | solution.py:318
  22.7 0.7 copy-done.6
  23.4 0.0 all-gather.2.cloned.1.call-update
  23.4 0.0 copy-start
  23.4 0.0 copy-start.1
  23.4 34.4 %all_to_all.30.got = bf16[32,80,128]{2,1,0:T(8,128)(2,1)S(1)} all-to-all(bf16[32,80,128]{2,1,0:T(8,128)(2,1)} %get-tuple-element.13), channel_id=1, replica_groups=mesh['cfg'=2,'z'=8,'pair'=2,'side'=2,'x'=4,'core'=2] {'z','pair','side'}, dimensions={0} | all-to-all | bytes 1310720 | tf_op jit(solution)/shard_map/all_to_all | solution.py:337
  57.9 3.5 %shard_map.151 = bf16[32,32,128]{2,1,0:T(8,128)(2,1)S(1)} custom-call(bf16[32,80,128]{2,1,0:T(8,128)(2,1)S(1)} %all_to_all.30.got), custom_call_target="tpu_custom_call" | custom-call | flops 10000000 | bytes 4000000 | tf_op jit(solution)/shard_map/pallas_call | solution.py:338
  61.3 16.0 %all_to_all.31.got = bf16[32,32,128]{2,1,0:T(8,128)(2,1)S(1)} all-to-all(bf16[32,32,128]{2,1,0:T(8,128)(2,1)S(1)} %shard_map.151), channel_id=1, replica_groups=mesh['cfg'=2,'z'=8,'pair'=2,'side'=2,'x'=4,'core'=2] {'z','pair','side'}, dimensions={0} | all-to-all | bytes 524288 | tf_op jit(solution)/shard_map/all_to_all | solution.py:339
  77.4 0.0 copy-done.2
  77.4 0.9 shard_map.152
  78.3 13.0 %all_to_all.32.got = bf16[8,16,1536]{2,1,0:T(8,128)(2,1)S(1)} all-to-all(bf16[8,16,1536]{2,1,0:T(8,128)(2,1)S(1)} %shard_map.152), channel_id=1, replica_groups=mesh['cfg'=2,'z'=8,'pair'=2,'side'=2,'x'=4,'core'=2] {'x','core'}, dimensions={0} | all-to-all | bytes 786432 | tf_op jit(solution)/shard_map/all_to_all | solution.py:343
  91.3 0.0 copy-done
  91.3 0.0 copy-done.1
  91.3 0.3 shard_map.153
  91.6 0.0 all-gather.2.cloned.1.call-done.own_far
  91.6 1.9 %collective-permute-start = (bf16[32,96,384]{2,1,0:T(8,128)(2,1)}, bf16[32,96,384]{2,1,0:T(8,128)(2,1)S(1)}, u32[]{:S(2)}, u32[]{:S(2)}) collective-permute-start(bf16[32,96,384]{2,1,0:T(8,128)(2,1)} %all-gather.2.cloned.1.call-done.own_far), channel_id=1, source_target_pairs={{0,1},{1,0},{2,3},{3,2},{4,5},{5,4},{6,7},{7,6},{8,9},{9,8},{10,11... | collective-permute-start | bytes 7077896 | tf_op jit(solution)/shard_map/ppermute | solution.py:351
  93.5 11.7 %all_to_all.33.rows = bf16[8,16,1536]{2,1,0:T(8,128)(2,1)S(1)} all-to-all(bf16[8,16,1536]{2,1,0:T(8,128)(2,1)S(1)} %get-tuple-element.16), channel_id=1, replica_groups=mesh['cfg'=2,'z'=8,'pair'=2,'side'=2,'x'=4,'core'=2] {'side','x'}, dimensions={0} | all-to-all | bytes 786432 | tf_op jit(solution)/shard_map/all_to_all | solution.py:350
  105.2 0.0 collective-permute-done.other
  105.2 3.2 %shard_map.154 = bf16[8,16,1536]{2,1,0:T(8,128)(2,1)S(1)} custom-call(bf16[8,16,1536]{2,1,0:T(8,128)(2,1)S(1)} %all_to_all.33.rows, bf16[32,96,384]{2,1,0:T(8,128)(2,1)S(1)} %collective-permute-done.other, bf16[32,96,384]{2,1,0:T(8,128)(2,1)} %all-gather.2.cloned.1.call-done.own_far), custom_call_target="tpu_custom_call" | custom-call | flops 10000000 | bytes 4000000 | tf_op jit(solution)/shard_map/pallas_call | solution.py:352
  108.4 11.4 %all_to_all.34.got = bf16[8,16,1536]{2,1,0:T(8,128)(2,1)S(1)} all-to-all(bf16[8,16,1536]{2,1,0:T(8,128)(2,1)S(1)} %shard_map.154), channel_id=1, replica_groups=mesh['cfg'=2,'z'=8,'pair'=2,'side'=2,'x'=4,'core'=2] {'side','x'}, dimensions={0} | all-to-all | bytes 786432 | tf_op jit(solution)/shard_map/all_to_all | solution.py:359
  119.9 0.0 copy-done.3
  119.9 0.9 shard_map.155
  120.8 3.1 %collective-permute-start.1 = (f32[16,64]{1,0:T(8,128)S(1)}, f32[16,64]{1,0:T(8,128)S(1)}, u32[]{:S(2)}, u32[]{:S(2)}) collective-permute-start(f32[16,64]{1,0:T(8,128)S(1)} %get-tuple-element.21.mine), channel_id=1, source_target_pairs={{0,256},{256,0},{1,257},{257,1},{2,258},{258,2},{3,259},{259,3},{4... | collective-permute-start | bytes 12296 | tf_op jit(solution)/shard_map/ppermute | solution.py:365
  124.6 5.6 %collective-permute-done.1.other = f32[16,64]{1,0:T(8,128)S(1)} collective-permute-done((f32[16,64]{1,0:T(8,128)S(1)}, f32[16,64]{1,0:T(8,128)S(1)}, u32[]{:S(2)}, u32[]{:S(2)}) %collective-permute-start.1) | collective-permute-done | bytes 4128 | tf_op jit(solution)/shard_map/ppermute | solution.py:365
  130.2 0.0 copy-done.4
  130.2 0.0 copy-done.5
  130.2 0.7 shard_map.156
  (4 shorter events, 0.0 us)
Async XLA Ops:
  8.8 13.8 %all-to-all-start = ((bf16[4,96,384]{2,1,0:T(8,128)(2,1)}), bf16[4,96,384]{2,1,0:T(8,128)(2,1)S(1)}, u32[]{:S(2)}, u32[]{:S(2)}) async-start(bf16[4,96,384]{2,1,0:T(8,128)(2,1)} %shard_map.150), calls=%async_computation | async-start | bytes 589824 | tf_op jit(solution)/shard_map/all_to_all | solution.py:318
  15.2 76.4 %all-gather.2.cloned.1.call-start = ((), (), s32[]{:S(2)}) async-start(), calls=%async_computation.6 | async-start | bytes 2654208 | tf_op jit(solution)/shard_map/all_gather | solution.py:336
  16.5 60.9 %copy-start.2 = (bf16[192,1536]{1,0:T(8,128)(2,1)S(1)}, bf16[192,1536]{1,0:T(8,128)(2,1)}, u32[]{:S(2)}) copy-start(bf16[192,1536]{1,0:T(8,128)(2,1)} %weight.1) | copy-start | bytes 1769476
  22.7 0.7 copy-start.6
  23.4 67.9 %copy-start = (bf16[1,128,1536]{2,1,0:T(8,128)(2,1)S(1)}, bf16[1,128,1536]{2,1,0:T(8,128)(2,1)}, u32[]{:S(2)}) copy-start(bf16[1,128,1536]{2,1,0:T(8,128)(2,1)} %tokens.1) | copy-start | bytes 1179652
  23.4 67.9 %copy-start.1 = (f32[2,8,1536]{2,1,0:T(8,128)S(1)}, f32[2,8,1536]{2,1,0:T(8,128)}, u32[]{:S(2)}) copy-start(f32[2,8,1536]{2,1,0:T(8,128)} %mods.3) | copy-start | bytes 294916
  91.6 13.6 %collective-permute-start = (bf16[32,96,384]{2,1,0:T(8,128)(2,1)}, bf16[32,96,384]{2,1,0:T(8,128)(2,1)S(1)}, u32[]{:S(2)}, u32[]{:S(2)}) collective-permute-start(bf16[32,96,384]{2,1,0:T(8,128)(2,1)} %all-gather.2.cloned.1.call-done.own_far), channel_id=1, source_target_pairs={{0,1},{1,0},{2,3},{3,2},{4,5},{5,4},{6,7},{7,6},{8,9},{9,8},{10,11... | collective-permute-start | bytes 7077896 | tf_op jit(solution)/shard_map/ppermute | solution.py:351
  105.2 14.6 %copy-start.3 = (bf16[1536,64]{0,1:T(8,128)(2,1)S(1)}, bf16[1536,64]{0,1:T(8,128)(2,1)}, u32[]{:S(2)}) copy-start(bf16[1536,64]{0,1:T(8,128)(2,1)} %param.21) | copy-start | bytes 589828
  105.2 25.0 %copy-start.4 = (f32[16,32]{1,0:T(8,128)S(1)}, f32[16,32]{1,0:T(8,128)}, u32[]{:S(2)}) copy-start(f32[16,32]{1,0:T(8,128)} %latent.1) | copy-start | bytes 6148
  105.2 25.0 %copy-start.5 = (f32[8,128]{1,0:T(8,128)S(1)}, f32[8,128]{1,0:T(8,128)}, u32[]{:S(2)}) copy-start(f32[8,128]{1,0:T(8,128)} %get-tuple-element.20.alphas) | copy-start | bytes 12292
  120.8 9.4 %collective-permute-start.1 = (f32[16,64]{1,0:T(8,128)S(1)}, f32[16,64]{1,0:T(8,128)S(1)}, u32[]{:S(2)}, u32[]{:S(2)}) collective-permute-start(f32[16,64]{1,0:T(8,128)S(1)} %get-tuple-element.21.mine), channel_id=1, source_target_pairs={{0,256},{256,0},{1,257},{257,1},{2,258},{258,2},{3,259},{259,3},{4... | collective-permute-start | bytes 12296 | tf_op jit(solution)/shard_map/ppermute | solution.py:365
Sparse Core Ops, SparseCore 0:
  23.5 61.9 all-gather.1
